TPU v7x, 32 devices: a whole 2x2x4 slice. The times are simulated.
32 devices in a mesh: group: 4 (over y, core), member: 8 (over z, x).
Axes of the slice: x: 2, y: 2, z: 4, core: 2. Of those that a mesh axis runs over, the one named last changes fastest.
Arguments:
- store: float32 [32768, 1024], P(('group', 'member')), may hold values from -6 to 6
- cache: float32 [4096, 1024], P('member'), may hold values from -6 to 6
- hot_local: int32 [32, 1], P(('group', 'member')), may hold values from 0 to 7
- hit_member: int32 [32768, 1], P(('group', 'member')), may hold values from 0 to 7; in each aligned block of 1024 rows (0 to 1023, 1024 to 2047, ...) at most 256 rows name the same one
- hit_row: int32 [32768], P(('group', 'member')), may hold values from 0 to 511
- miss_owner: int32 [16384, 1], P(('group', 'member')), may hold values from 0 to 31; in each aligned block of 512 rows (0 to 511, 512 to 1023, ...) at most 32 rows name the same one
- miss_row: int32 [16384], P(('group', 'member')), may hold values from 0 to 1023
- tgt_self: int32 [32768], P(('group', 'member')), may hold values from 0 to 1535
- tgt_nbr: int32 [32768, 10], P(('group', 'member')), may hold values from 0 to 1535
- tgt_mask: int32 [32768, 10], P(('group', 'member')), may hold values 0 or 1
- seed_self: int32 [4096], P(('group', 'member')), may hold values from 0 to 1023
- seed_nbr: int32 [4096, 5], P(('group', 'member')), may hold values from 0 to 1023
- seed_mask: int32 [4096, 5], P(('group', 'member')), may hold values 0 or 1
- w1_self: bfloat16 [1024, 512], replicated, may hold values from -0.1875 to 0.1875
- w1_nbr: bfloat16 [1024, 512], replicated, may hold values from -0.1875 to 0.1875
- w2_self: bfloat16 [512, 512], replicated, may hold values from -0.25 to 0.25
- w2_nbr: bfloat16 [512, 512], replicated, may hold values from -0.25 to 0.25
- d_emb: bfloat16 [4096, 512], P(('group', 'member')), may hold values from -6 to 6
Outputs:
- emb: bfloat16 [4096, 512], P(('group', 'member'))
- grad_w1_self: float32 [1024, 512], replicated
- grad_w1_nbr: float32 [1024, 512], replicated
- grad_w2_self: float32 [512, 512], replicated
- grad_w2_nbr: float32 [512, 512], replicated
- new_cache: float32 [4096, 1024], P('member')
Inputs may be any that keep to these rules, and one draw needn't show every extreme that they name: `hit_member`: among the rows of one device at most 256 name the same member, a bound that some block reaches of them. `miss_owner`: among the rows of one device at most 32 name the same owner, a bound that some block reaches of them.
All inputs are finite; a program needn't handle non-finite values. No bound on the sum of `tgt_mask` or of `seed_mask` on one device may be relied on, other than what follows from the above.
Results may differ from a plain program's by a relative error of at most 0.0067.
Values may be sent and summed in bfloat16 or wider, within the bound.
No kernel may reach another device: no remote copies, remote signals or barrier semaphores. Data moves between devices by JAX's collectives and lax.ppermute only.
A program may use at most 128 MiB of HBM per device.

v0:
```python
import math

import jax
import jax.numpy as jnp
from jax import lax
from jax.sharding import PartitionSpec as P

BLOCK = 128


def slot_of(peer, count, capacity):
    peer_lanes = lax.iota(jnp.int32, count)
    peer_flags = (peer[:, None] == peer_lanes[None, :]).astype(jnp.int32)
    before = jnp.cumsum(peer_flags, axis=0) - peer_flags
    return peer * capacity + jnp.sum(before * peer_flags, axis=1)


def one_hot_sum(index, present, columns):
    positions = lax.iota(jnp.int32, columns)
    table = jnp.zeros((index.shape[0], columns), jnp.float32)
    for column in range(index.shape[1]):
        hit_flag = (index[:, column : column + 1] == positions[None, :]) & (
            present[:, column : column + 1] > 0
        )
        table = table + jnp.where(hit_flag, 1.0, 0.0)
    return table


def silu_slope(pre):
    gate_sig = jax.nn.sigmoid(pre)
    return gate_sig * (1.0 + pre * (1.0 - gate_sig))


def on_device(
    store,
    cache,
    hot_local,
    hit_member,
    hit_row,
    miss_owner,
    miss_row,
    tgt_self,
    tgt_nbr,
    tgt_mask,
    seed_self,
    seed_nbr,
    seed_mask,
    w1_self,
    w1_nbr,
    w2_self,
    w2_nbr,
    d_emb,
):
    feat_width = store.shape[1]
    hot_rows = store.reshape(-1, BLOCK, feat_width)[hot_local[0]].reshape(-1, feat_width)
    new_cache = lax.all_gather(hot_rows, "group", axis=0, tiled=True)
    members = lax.axis_size("member")
    groups = lax.axis_size("group")
    owners = groups * members
    hit_count = hit_row.shape[0]
    hit_cap = 2 * hit_count // members
    hit_pos = slot_of(hit_member[:, 0], members, hit_cap)
    hit_ids = (
        jnp.zeros((members * hit_cap,), jnp.int32)
        .at[hit_pos]
        .set(hit_row)
        .reshape(members, hit_cap)
    )
    found_rows = cache[
        lax.all_to_all(hit_ids, "member", split_axis=0, concat_axis=0, tiled=True)
    ].astype(jnp.bfloat16)
    hit_back = lax.all_to_all(found_rows, "member", split_axis=0, concat_axis=0, tiled=True)
    x_hits = hit_back.reshape(-1, feat_width)[hit_pos]
    miss_count = miss_row.shape[0]
    miss_cap = 2 * miss_count // owners
    miss_pos = slot_of(miss_owner[:, 0], owners, miss_cap)
    request_ids = jnp.zeros((owners * miss_cap,), jnp.int32).at[miss_pos].set(miss_row)
    owned_rows = store[
        lax.all_to_all(
            request_ids.reshape(owners, miss_cap),
            ("group", "member"),
            split_axis=0,
            concat_axis=0,
            tiled=True,
        )
    ].astype(jnp.bfloat16)
    miss_back = lax.all_to_all(
        owned_rows, ("group", "member"), split_axis=0, concat_axis=0, tiled=True
    )
    x_misses = miss_back.reshape(-1, feat_width)[miss_pos]
    fetched = jnp.concatenate([x_hits, x_misses], 0)
    adjacency = one_hot_sum(tgt_nbr, tgt_mask, hit_count + miss_count).astype(jnp.bfloat16)
    count_one = jnp.maximum(jnp.sum(tgt_mask.astype(jnp.float32), 1), 1.0)
    nbr_total = jnp.dot(adjacency, fetched, preferred_element_type=jnp.float32)
    mean_one = (nbr_total / count_one[:, None]).astype(jnp.bfloat16)
    self_one = fetched[tgt_self]
    pre_one = jnp.dot(self_one, w1_self, preferred_element_type=jnp.float32) + jnp.dot(
        mean_one, w1_nbr, preferred_element_type=jnp.float32
    )
    hidden = jax.nn.silu(pre_one).astype(jnp.bfloat16)
    target_rows = hidden.shape[0]
    adjacency_two = one_hot_sum(seed_nbr, seed_mask, target_rows).astype(jnp.bfloat16)
    picker = one_hot_sum(seed_self[:, None], jnp.ones_like(seed_self[:, None]), target_rows).astype(
        jnp.bfloat16
    )
    count_two = jnp.maximum(jnp.sum(seed_mask.astype(jnp.float32), 1), 1.0)
    mean_two = (
        jnp.dot(adjacency_two, hidden, preferred_element_type=jnp.float32) / count_two[:, None]
    ).astype(jnp.bfloat16)
    self_two = hidden[seed_self]
    emb = (
        jnp.dot(self_two, w2_self, preferred_element_type=jnp.float32)
        + jnp.dot(mean_two, w2_nbr, preferred_element_type=jnp.float32)
    ).astype(jnp.bfloat16)
    term_w2_self = jnp.dot(self_two.T, d_emb, preferred_element_type=jnp.float32)
    term_w2_nbr = jnp.dot(mean_two.T, d_emb, preferred_element_type=jnp.float32)
    back_self = jnp.dot(d_emb, w2_self.T, preferred_element_type=jnp.float32).astype(jnp.bfloat16)
    back_mean = (
        jnp.dot(d_emb, w2_nbr.T, preferred_element_type=jnp.float32) / count_two[:, None]
    ).astype(jnp.bfloat16)
    back_hidden = jnp.dot(picker.T, back_self, preferred_element_type=jnp.float32) + jnp.dot(
        adjacency_two.T, back_mean, preferred_element_type=jnp.float32
    )
    back_pre = (back_hidden * silu_slope(pre_one)).astype(jnp.bfloat16)
    term_w1_self = jnp.dot(self_one.T, back_pre, preferred_element_type=jnp.float32)
    term_w1_nbr = jnp.dot(mean_one.T, back_pre, preferred_element_type=jnp.float32)
    summed = lax.psum((term_w1_self, term_w1_nbr, term_w2_self, term_w2_nbr), ("group", "member"))
    grad_scale = 1.0 / math.sqrt(d_emb.shape[0] * owners)
    return (
        emb,
        summed[0] * grad_scale,
        summed[1] * grad_scale,
        summed[2] * grad_scale,
        summed[3] * grad_scale,
        new_cache,
    )


def solution(mesh):
    in_specs = (
        P(("group", "member"), None),
        P("member", None),
        P(("group", "member"), None),
        P(("group", "member"), None),
        P(("group", "member")),
        P(("group", "member"), None),
        P(("group", "member")),
        P(("group", "member")),
        P(("group", "member"), None),
        P(("group", "member"), None),
        P(("group", "member")),
        P(("group", "member"), None),
        P(("group", "member"), None),
        P(),
        P(),
        P(),
        P(),
        P(("group", "member"), None),
    )
    out_specs = (P(("group", "member"), None), P(), P(), P(), P(), P("member", None))
    return jax.shard_map(
        on_device, mesh=mesh, in_specs=in_specs, out_specs=out_specs, check_vma=False
    )
```

profile of v0, /device:TPU:0, one launch (start us, length us, event | category | flops | bytes accessed | tf_op | source)
XLA Modules:
  0.0 436.6 jit_solution(2398134194012880089)
XLA Ops:
  11.8 2.6 scatter_custom_fusion.1
  15.1 7.3 %all-to-all-start.2 = ((s32[32,1,32]{2,1,0:T(1,128)}), s32[32,1,32]{2,1,0:T(1,128)S(1)}, u32[]{:S(2)}, u32[]{:S(2)}) async-start(s32[32,1,32]{2,1,0:T(1,128)} %all_to_all.26), calls=%async_computation.2 | async-start | bytes 32768 | tf_op jit(solution)/shard_map/all_to_all | solution.py:79
  23.1 2.3 reduce-window.14
  27.2 5.0 %scatter_custom_fusion = s32[2048]{0:T(1024)} fusion(s32[1024]{0:T(1024)S(1)} %bitcast.127, s32[1024]{0:T(1024)} %param.22, s32[]{:T(128)} %constant.12.clone.1), kind=kCustom, calls=%fused_computation.127 | custom fusion | bytes 8704 | tf_op jit(solution)/shard_map/scatter | solution.py:66
  32.3 5.8 %all-to-all-start = ((s32[8,1,256]{2,1,0:T(1,128)}), s32[8,1,256]{2,1,0:T(1,128)S(1)}, u32[]{:S(2)}, u32[]{:S(2)}) async-start(s32[8,1,256]{2,1,0:T(1,128)} %bitcast.5), calls=%async_computation | async-start | bytes 16384 | tf_op jit(solution)/shard_map/all_to_all | solution.py:70
  38.2 8.2 %gather_fusion.2 = bf16[1024,1024]{1,0:T(8,128)(2,1)} fusion(f32[1024,1024]{1,0:T(8,128)} %param.18, s32[1024]{0:T(1024)S(1)} %broadcast_clamp_fusion.1), kind=kCustom, calls=%fused_computation.2 | custom fusion | bytes 4198400 | tf_op jit(solution)/shard_map/gather | solution.py:78
  46.4 6.1 %all-to-all-start.3 = ((bf16[32,32,1024]{2,1,0:T(8,128)(2,1)}), bf16[32,32,1024]{2,1,0:T(8,128)(2,1)}, u32[]{:S(2)}, u32[]{:S(2)}) async-start(bf16[32,32,1024]{2,1,0:T(8,128)(2,1)} %bitcast.118), calls=%async_computation.3 | async-start | bytes 4194304 | tf_op jit(solution)/shard_map/all_to_all | solution.py:87
  52.6 9.2 %gather_fusion = bf16[2048,1024]{1,0:T(8,128)(2,1)} fusion(f32[512,1024]{1,0:T(8,128)S(1)} %copy-done, s32[2048]{0:T(1024)S(1)} %broadcast_clamp_fusion), kind=kCustom, calls=%fused_computation | custom fusion | bytes 8396800 | tf_op jit(solution)/shard_map/gather | solution.py:69
  61.8 40.8 %all-to-all-done.3 = bf16[32,32,1024]{2,1,0:T(8,128)(2,1)} async-done(((bf16[32,32,1024]{2,1,0:T(8,128)(2,1)}), bf16[32,32,1024]{2,1,0:T(8,128)(2,1)}, u32[]{:S(2)}, u32[]{:S(2)}) %all-to-all-start.3) | async-done | bytes 2097184 | tf_op jit(solution)/shard_map/all_to_all | solution.py:87
  102.6 4.7 %all-to-all-start.1 = ((bf16[8,256,1024]{2,1,0:T(8,128)(2,1)}), bf16[8,256,1024]{2,1,0:T(8,128)(2,1)}, u32[]{:S(2)}, u32[]{:S(2)}) async-start(bf16[8,256,1024]{2,1,0:T(8,128)(2,1)} %bitcast.117), calls=%async_computation.1 | async-start | bytes 8388608 | tf_op jit(solution)/shard_map/all_to_all | solution.py:72
  112.5 4.6 %gather_fusion.3 = bf16[512,1024]{1,0:T(8,128)(2,1)S(1)} fusion(bf16[1024,1024]{1,0:T(8,128)(2,1)} %bitcast.17, s32[1024]{0:T(1024)S(1)} %pad_clamp_fusion.1), kind=kCustom, calls=%fused_computation.3 | custom fusion | bytes 2099200 | tf_op jit(solution)/shard_map/gather | solution.py:90
  117.1 83.5 %all-to-all-done.1 = bf16[8,256,1024]{2,1,0:T(8,128)(2,1)} async-done(((bf16[8,256,1024]{2,1,0:T(8,128)(2,1)}), bf16[8,256,1024]{2,1,0:T(8,128)(2,1)}, u32[]{:S(2)}, u32[]{:S(2)}) %all-to-all-start.1) | async-done | bytes 4194336 | tf_op jit(solution)/shard_map/all_to_all | solution.py:72
  200.6 8.7 %gather_fusion.1 = bf16[1024,1024]{1,0:T(8,128)(2,1)} fusion(bf16[2048,1024]{1,0:T(8,128)(2,1)} %bitcast.9, s32[1024]{0:T(1024)S(1)} %broadcast_clamp_fusion.2), kind=kCustom, calls=%fused_computation.1 | custom fusion | bytes 4198400 | tf_op jit(solution)/shard_map/gather | solution.py:73
  209.3 3.1 constant_dynamic-update-slice_fusion.1
  213.5 8.3 %gather_fusion.4 = bf16[1024,1024]{1,0:T(8,128)(2,1)} fusion(bf16[1536,1024]{1,0:T(8,128)(2,1)} %constant_dynamic-update-slice_fusion, s32[1024]{0:T(1024)S(1)} %get-tuple-element.53), kind=kCustom, calls=%fused_computation.4 | custom fusion | bytes 4198400 | tf_op jit(solution)/shard_map/gather | solution.py:96
  221.8 19.4 %divide_convert_fusion = bf16[1024,1024]{1,0:T(8,128)(2,1)S(1)} fusion(f32[1024]{0:T(1024)S(1)} %broadcast_maximum_fusion, bf16[1536,1024]{1,0:T(8,128)(2,1)} %constant_dynamic-update-slice_fusion, s32[1024]{0:T(1024)S(1)} %bitcast.141, s32[1024]{0:T(1024)S(1)} %bitcast.142, s32[1024]{0:T(1024)S(1)} %bitcast.134, s32[1024]{0:T(1024)S(1)} %bitcast.135, ...), kind=kOutput, calls=%fused_computation.29 | convolution fusion | flops 3286237184 | bytes 5298176 | tf_op jit(solution)/shard_map/dot_general | solution.py:94
  243.2 3.2 multiply_convert_fusion.1
  246.4 2.2 gather_fusion.5
  249.9 2.0 fusion.35
  253.3 4.7 %multiply_convert_fusion = bf16[1024,512]{1,0:T(8,128)(2,1)} fusion(f32[1024,512]{1,0:T(8,128)} %get-tuple-element.52, f32[1024,512]{1,0:T(8,128)} %fusion.36, bf16[128,512]{1,0:T(8,128)(2,1)S(1)} %copy-done.6, bf16[512,512]{1,0:T(8,128)(2,1)S(1)} %copy-done.9, f32[128]{0:T(128)S(1)} %broadcast_maximum_fusion.1, s32[128]{0:T(128)S(1)} %get-tuple-element.49, ...), kind=kOutput, calls=%fused_computation.53 | convolution fusion | flops 209321984 | bytes 5901952 | tf_op jit(solution)/shard_map/dot_general | solution.py:121
  258.0 4.6 %fusion.70 = f32[1024,512]{1,0:T(8,128)} fusion(bf16[1024,1024]{1,0:T(8,128)(2,1)} %gather_fusion.4, bf16[1024,512]{1,0:T(8,128)(2,1)} %multiply_convert_fusion), kind=kOutput, calls=%fused_computation.158 | convolution fusion | flops 1073741824 | bytes 5242880 | tf_op jit(solution)/shard_map/dot_general | solution.py:125
  262.6 2.6 fusion.71
  267.4 152.9 %all-reduce.3.cloned.1.call-done = (f32[1024,512]{1,0:T(8,128)}, f32[1024,512]{1,0:T(8,128)}, f32[512,512]{1,0:T(8,128)}, f32[512,512]{1,0:T(8,128)}) async-done(((f32[1024,512]{1,0:T(8,128)}, f32[1024,512]{1,0:T(8,128)}, f32[512,512]{1,0:T(8,128)}, f32[512,512]{1,0:T(8,128)}), (f32[1024,512]{1,0:T(8,128)}, f32[1024,512]{1,0:T(8,128)}, f32[512,512]{1,0:T(8,128)}, ...) | async-done | bytes 6291472 | tf_op jit(solution)/shard_map/psum | solution.py:127
  420.3 3.3 broadcast_multiply_fusion.1
  (94 shorter events, 24.8 us)
Async XLA Ops:
  8.0 44.6 %copy-start = (f32[512,1024]{1,0:T(8,128)S(1)}, f32[512,1024]{1,0:T(8,128)}, u32[]{:S(2)}) copy-start(f32[512,1024]{1,0:T(8,128)} %param.19) | copy-start | bytes 6291460
  15.1 17.2 %all-to-all-start.2 = ((s32[32,1,32]{2,1,0:T(1,128)}), s32[32,1,32]{2,1,0:T(1,128)S(1)}, u32[]{:S(2)}, u32[]{:S(2)}) async-start(s32[32,1,32]{2,1,0:T(1,128)} %all_to_all.26), calls=%async_computation.2 | async-start | bytes 32768 | tf_op jit(solution)/shard_map/all_to_all | solution.py:79
  32.3 14.1 %all-to-all-start = ((s32[8,1,256]{2,1,0:T(1,128)}), s32[8,1,256]{2,1,0:T(1,128)S(1)}, u32[]{:S(2)}, u32[]{:S(2)}) async-start(s32[8,1,256]{2,1,0:T(1,128)} %bitcast.5), calls=%async_computation | async-start | bytes 16384 | tf_op jit(solution)/shard_map/all_to_all | solution.py:70
  46.4 56.2 %all-to-all-start.3 = ((bf16[32,32,1024]{2,1,0:T(8,128)(2,1)}), bf16[32,32,1024]{2,1,0:T(8,128)(2,1)}, u32[]{:S(2)}, u32[]{:S(2)}) async-start(bf16[32,32,1024]{2,1,0:T(8,128)(2,1)} %bitcast.118), calls=%async_computation.3 | async-start | bytes 4194304 | tf_op jit(solution)/shard_map/all_to_all | solution.py:87
  102.6 7.5 %copy-start.13 = (s32[128,5]{0,1:T(8,128)S(1)}, s32[128,5]{0,1:T(8,128)}, u32[]{:S(2)}) copy-start(s32[128,5]{0,1:T(8,128)} %param.30) | copy-start | bytes 7684
  102.6 7.5 %copy-start.11 = (s32[1024,10]{0,1:T(8,128)S(1)}, s32[1024,10]{0,1:T(8,128)}, u32[]{:S(2)}) copy-start(s32[1024,10]{0,1:T(8,128)} %param.27) | copy-start | bytes 122884
  102.6 7.7 %copy-start.16 = (s32[128]{0:T(128)S(1)}, s32[128]{0:T(128)}, u32[]{:S(2)}) copy-start(s32[128]{0:T(128)} %param.28) | copy-start | bytes 1540
  102.6 7.8 %copy-start.15 = (s32[128,5]{0,1:T(8,128)S(1)}, s32[128,5]{0,1:T(8,128)}, u32[]{:S(2)}) copy-start(s32[128,5]{0,1:T(8,128)} %param.29) | copy-start | bytes 7684
  102.6 7.8 %copy-start.14 = (s32[1024]{0:T(1024)S(1)}, s32[1024]{0:T(1024)}, u32[]{:S(2)}) copy-start(s32[1024]{0:T(1024)} %param.25) | copy-start | bytes 12292
  102.6 7.8 %copy-start.12 = (s32[1024,10]{0,1:T(8,128)S(1)}, s32[1024,10]{0,1:T(8,128)}, u32[]{:S(2)}) copy-start(s32[1024,10]{0,1:T(8,128)} %param.26) | copy-start | bytes 122884
  102.6 7.9 %copy-start.6 = (bf16[128,512]{1,0:T(8,128)(2,1)S(1)}, bf16[128,512]{1,0:T(8,128)(2,1)}, u32[]{:S(2)}) copy-start(bf16[128,512]{1,0:T(8,128)(2,1)} %param.35) | copy-start | bytes 393220
  102.6 98.0 %all-to-all-start.1 = ((bf16[8,256,1024]{2,1,0:T(8,128)(2,1)}), bf16[8,256,1024]{2,1,0:T(8,128)(2,1)}, u32[]{:S(2)}, u32[]{:S(2)}) async-start(bf16[8,256,1024]{2,1,0:T(8,128)(2,1)} %bitcast.117), calls=%async_computation.1 | async-start | bytes 8388608 | tf_op jit(solution)/shard_map/all_to_all | solution.py:72
  107.3 3.2 copy-start.4
  107.3 157.9 %all-gather.3.cloned.1.call-start = ((), (), s32[]{:S(2)}) async-start(), calls=%async_computation.4 | async-start | bytes 2621440 | tf_op jit(solution)/shard_map/all_gather | solution.py:56
  110.0 310.2 %all-reduce.3.cloned.1.call-start = ((), (), s32[]{:S(2)}) async-start(), calls=%async_computation.5 | async-start | bytes 12582912 | tf_op jit(solution)/shard_map/psum | solution.py:127
  221.8 19.4 %copy-start.1 = (bf16[1024,1024]{1,0:T(8,128)(2,1)S(1)}, bf16[1024,1024]{1,0:T(8,128)(2,1)}, u32[]{:S(2)}) copy-start(bf16[1024,1024]{1,0:T(8,128)(2,1)} %gather_fusion.4) | copy-start | bytes 6291460
  221.8 19.4 %copy-start.17 = (bf16[1024,512]{1,0:T(8,128)(2,1)S(1)}, bf16[1024,512]{1,0:T(8,128)(2,1)}, u32[]{:S(2)}) copy-start(bf16[1024,512]{1,0:T(8,128)(2,1)} %param.31) | copy-start | bytes 3145732
  241.3 2.0 copy-start.18
  249.9 3.4 copy-start.9
  258.0 4.6 %copy-start.20 = (bf16[1024,1024]{1,0:T(8,128)(2,1)S(1)}, bf16[1024,1024]{1,0:T(8,128)(2,1)}, u32[]{:S(2)}) copy-start(bf16[1024,1024]{1,0:T(8,128)(2,1)} %copy-done.19) | copy-start | bytes 6291460
  258.0 4.6 %copy-start.21 = (bf16[1024,512]{1,0:T(8,128)(2,1)S(1)}, bf16[1024,512]{1,0:T(8,128)(2,1)}, u32[]{:S(2)}) copy-start(bf16[1024,512]{1,0:T(8,128)(2,1)} %multiply_convert_fusion) | copy-start | bytes 3145732
  420.3 3.3 copy-start.3
  425.1 1.6 copy-start.7
  425.1 2.7 copy-start.2
  (4 other events, 5.2 us)
Sparse Core Ops, SparseCore 0:
  110.2 22.9 all-gather.2
Sparse Core Ops, SparseCore 1:
  265.3 154.9 all-reduce.2
where the time goes:
time: 437 us
  waiting for transfers between devices  277 us (63%)
  local copies, waits for them, and re-layouts  59.9 us (14%)
  matrix products  43.6 us (10%)
  starting transfers between devices  24 us (5%)
  between operations  16.5 us (4%)
  other arithmetic  15.3 us (4%)
    psum x1, waiting for transfers between devices, on_device(): lax.psum((term_w1_self, term_w1_nbr, term_w2_self, term_w2_nbr), ('group'...  153 us
    all_to_all x1, waiting for transfers between devices, on_device(): lax.all_to_all(found_rows, 'member', split_axis=0, concat_axis=0, tiled=T...  83.5 us
    all_to_all x1, waiting for transfers between devices, on_device(): lax.all_to_all(owned_rows, ('group', 'member'), split_axis=0, concat_axis...  40.8 us
    dot_general x1, matrix products, on_device(): nbr_total = jnp.dot(adjacency, fetched, preferred_element_type=jnp.float32)  19.4 us
    gather x1, local copies, waits for them, and re-layouts, on_device(): cache[lax.all_to_all(hit_ids, 'member', split_axis=0, concat_axis=0, tile...  9.18 us
  transfers between devices with their start and end apart: 6, of which 3 were waited for; matrix products, arithmetic and copies ran while one was open for 23% of the time, Pallas kernels for 0%

commit v1 on v0

v1 whole, which is shorter than its diff:
```python
import functools
import math

import jax
import jax.numpy as jnp
from jax import lax
from jax.experimental import pallas as pl
from jax.experimental.pallas import tpu as pltpu
from jax.sharding import PartitionSpec as P

BLOCK = 128
BOTH = ("group", "member")
F32, BF16, I32 = jnp.float32, jnp.bfloat16, jnp.int32
GRANT = 29 * 1024 * 1024


def dot(a, b, ca=1, cb=0):
    return lax.dot_general(a, b, (((ca,), (cb,)), ((), ())), preferred_element_type=F32)


def iota(shape, dim):
    return lax.broadcasted_iota(I32, shape, dim)


def kernel_call(body, out_shape, scratch=(), smem=0, flops=0):
    def call(*operands):
        specs = [pl.BlockSpec(memory_space=pltpu.SMEM)] * smem
        specs += [pl.BlockSpec(memory_space=pltpu.VMEM)] * (len(operands) - smem)
        return pl.pallas_call(
            body,
            out_shape=out_shape,
            in_specs=specs,
            out_specs=jax.tree.map(lambda _: pl.BlockSpec(memory_space=pltpu.VMEM), out_shape),
            scratch_shapes=list(scratch),
            compiler_params=pltpu.CompilerParams(vmem_limit_bytes=GRANT),
            cost_estimate=pl.CostEstimate(flops=0, bytes_accessed=0, transcendentals=0),
        )(*operands)

    return call


def request_body(owner_ref, row_ref, ids_ref, slot_ref):
    count = owner_ref.shape[1]
    owners, cap = ids_ref.shape
    flags = owner_ref[...] == iota((owners, count), 0)
    flag = flags.astype(F32).astype(BF16)
    earlier = (iota((count, count), 0) < iota((count, count), 1)).astype(F32).astype(BF16)
    rank = jnp.sum(jnp.where(flags, dot(flag, earlier), 0.0), axis=0, keepdims=True).astype(I32)
    slot_ref[...] = owner_ref[...] * cap + rank
    ranked = (rank == iota((cap, count), 0)).astype(F32).astype(BF16)
    row = row_ref[...]
    high = jnp.where(flags, (row // 128).astype(F32), 0.0).astype(BF16)
    low = jnp.where(flags, (row % 128).astype(F32), 0.0).astype(BF16)
    ids_ref[...] = (dot(high, ranked, 1, 1) * 128.0 + dot(low, ranked, 1, 1)).astype(I32)


def serve_body(ids_ref, store_ref, rows_ref):
    peers, cap = ids_ref.shape
    total, held = peers * cap, store_ref.shape[0]
    ids = ids_ref[...]
    spread = (iota((total, peers), 0) // cap == iota((total, peers), 1)).astype(F32).astype(BF16)
    high = dot(spread, (ids // 128).astype(F32).astype(BF16))
    low = dot(spread, (ids % 128).astype(F32).astype(BF16))
    here = iota((total, cap), 0) % cap == iota((total, cap), 1)
    flat = jnp.sum(jnp.where(here, high * 128.0 + low, 0.0), axis=1, keepdims=True).astype(I32)
    step = 256
    for at in range(0, total, step):
        pick = (flat[at : at + step] == iota((step, held), 1)).astype(F32).astype(BF16)
        rows_ref[at : at + step, :] = dot(pick, store_ref[...]).astype(BF16)


def tables_body(
    targets_ref, names_ref, slot_ref, mask_ref, code_ref, emb_ref, w2s_ref, w2n_ref,
    sel_hit_ref, sel_miss_ref, count_ref, back_ref, flag_ref, column_ref, *, hits,
):
    seeds, total = targets_ref.shape[1], names_ref.shape[1]
    misses = slot_ref.shape[1]
    slots = sel_miss_ref.shape[2]
    fan, fan_two = names_ref.shape[0] - 1, mask_ref.shape[0]

    def columns(rows):
        rows = rows.astype(F32)
        pad = jnp.zeros((-rows.shape[0] % 8, rows.shape[1]), F32)
        return jnp.concatenate([rows, pad], 0).T if pad.shape[0] else rows.T

    column_ref[...] = columns(code_ref[...])[:, 0:1].astype(I32)
    names = names_ref[...]
    high = (names // 128).astype(F32).astype(BF16)
    low = (names % 128).astype(F32).astype(BF16)
    place = (slot_ref[...] == iota((slots, misses), 0)).astype(F32).astype(BF16)
    targets = columns(targets_ref[...]).astype(I32)
    for turn in range(fan_two + 1):
        cut = slice(turn * seeds, (turn + 1) * seeds)
        pick = (targets[:, turn : turn + 1] == iota((seeds, total), 1)).astype(F32).astype(BF16)
        named = (dot(pick, high, 1, 1) * 128.0 + dot(pick, low, 1, 1)).astype(I32) - 1
        here = named[:, 1:] >= 0
        count_ref[cut, :] = jnp.maximum(jnp.sum(here.astype(F32), axis=1, keepdims=True), 1.0)
        for first, width in ((0, hits), (hits, misses)):
            lane = iota((seeds, width), 1) + first
            own = jnp.where(named[:, 0:1] == lane, 1.0, 0.0).astype(BF16)
            near = jnp.zeros((seeds, width), F32)
            for k in range(1, fan + 1):
                near = near + jnp.where(named[:, k : k + 1] == lane, 1.0, 0.0)
            near = near.astype(BF16)
            if first == 0:
                sel_hit_ref[0, cut, :] = own
                sel_hit_ref[1, cut, :] = near
            else:
                sel_miss_ref[0, cut, :] = dot(own, place, 1, 1).astype(BF16)
                sel_miss_ref[1, cut, :] = dot(near, place, 1, 1).astype(BF16)
    mask = columns(mask_ref[...])[:, :fan_two]
    flag_ref[...] = mask
    count_two = jnp.maximum(jnp.sum(mask, axis=1, keepdims=True), 1.0)
    back_ref[0:seeds, :] = dot(emb_ref[...], w2s_ref[...], 1, 1).astype(BF16)
    back_mean = (dot(emb_ref[...], w2n_ref[...], 1, 1) / count_two).astype(BF16).astype(F32)
    for k in range(fan_two):
        at = (k + 1) * seeds
        back_ref[at : at + seeds, :] = (mask[:, k : k + 1] * back_mean).astype(BF16)


def cached_body(code_ref, *refs, bases):
    pieces, held_ref = refs[:-1], refs[-1]
    step = 256

    @pl.loop(0, code_ref.shape[0] // step)
    def _(turn):
        cut = pl.ds(pl.multiple_of(turn * step, step), step)
        total = None
        for piece, base in zip(pieces, bases):
            lane = iota((step, piece.shape[0]), 1) + base
            pick = (code_ref[cut, :] == lane).astype(F32).astype(BF16)
            part = dot(pick, piece[...])
            total = part if total is None else total + part
        held_ref[cut, :] = total.astype(BF16)


def share_body(sel_ref, *refs):
    parts, (own_ref, near_ref) = refs[:-2], refs[-2:]
    held = parts[0][...]
    for part in parts[1:]:
        held = held + part[...]
    step = 256
    for at in range(0, own_ref.shape[0], step):
        own_ref[at : at + step, :] = dot(sel_ref[0, at : at + step, :], held).astype(BF16)
        near_ref[at : at + step, :] = dot(sel_ref[1, at : at + step, :], held)


def join_body(me_ref, *refs, count, parts):
    pieces, outs = refs[:count], refs[count:]
    for k in range(count):
        depth = pieces[k].shape[0] // parts
        place = pl.multiple_of((me_ref[0] ^ k) * depth, 16)
        for j in range(parts):
            value = pieces[k][j * depth : (j + 1) * depth, :]
            outs[j][pl.ds(place, depth), :] = value.astype(outs[j].dtype)


def join(pieces, me, dtype, parts=1):
    count = len(pieces)
    depth, width = pieces[0].shape[0] // parts, pieces[0].shape[1]
    if depth % 16 == 0:
        return kernel_call(
            functools.partial(join_body, count=count, parts=parts),
            [jax.ShapeDtypeStruct((count * depth, width), dtype)] * parts,
            smem=1,
        )(me.reshape(1), *pieces)
    outs = [jnp.zeros((count * depth, width), dtype)] * parts
    for k in range(count):
        for j in range(parts):
            value = pieces[k][j * depth : (j + 1) * depth].astype(dtype)
            outs[j] = lax.dynamic_update_slice_in_dim(outs[j], value, (me ^ k) * depth, 0)
    return outs


def step_body(core_ref, *refs, scale, step):
    sources, (count_ref, mask_ref, out_ref, send_ref, keep_ref, *refs) = refs[:10], refs[10:]
    held, (self_ref, mean_ref, hid_ref, bp_ref, sems) = refs[:10], refs[10:]
    miss_ref, w1s_ref, w1n_ref, back_ref, w2s_ref, w2n_ref, emb_ref, *turned = held
    sel_ref, own_ref, near_ref = turned
    rows, wide = own_ref.shape
    seeds = mask_ref.shape[0]
    hid = w1s_ref.shape[1]
    turns = rows // step

    def copy(i, turn=None):
        source, target, number = sources[i], held[i], i
        if turn is not None:
            cut = slice(turn * step, (turn + 1) * step)
            source, target = (
                (ref.at[:, cut, :] if len(ref.shape) == 3 else ref.at[cut, :])
                for ref in (source, target)
            )
            number = 7 + (i - 7) * turns + turn
        return pltpu.make_async_copy(source, target, sems.at[number])

    order = [(0,), (7, 0), (8, 0), (9, 0), (1,), (2,), (3,)]
    order += [(i, turn) for turn in range(1, turns) for i in (7, 8, 9)] + [(4,), (5,), (6,)]
    for item in order:
        copy(*item).start()
    copy(0).wait()
    for turn in range(turns):
        cut = slice(turn * step, (turn + 1) * step)
        copy(7, turn).wait()
        own = dot(sel_ref[0, cut, :], miss_ref[...])
        near = dot(sel_ref[1, cut, :], miss_ref[...])
        copy(8, turn).wait()
        copy(9, turn).wait()
        own = (own_ref[cut, :].astype(F32) + own).astype(BF16)
        mean = ((near_ref[cut, :] + near) / count_ref[cut, :]).astype(BF16)
        self_ref[cut, :] = own
        mean_ref[cut, :] = mean
        if turn == 0:
            copy(1).wait()
            copy(2).wait()
        pre = dot(own, w1s_ref[...]) + dot(mean, w1n_ref[...])
        gate = jax.nn.sigmoid(pre)
        hid_ref[cut, :] = (pre * gate).astype(BF16)
        slope = gate * (1.0 + pre * (1.0 - gate))
        if turn == 0:
            copy(3).wait()
        bp_ref[cut, :] = (back_ref[cut, :].astype(F32) * slope).astype(BF16)

    core = core_ref[0]
    half = (2 * wide + 2 * hid) // 2

    def put(at, value):
        value = value * scale
        place = slice(at % half, at % half + value.shape[0])

        @pl.when(core == at // half)
        def _():
            keep_ref[place, :] = value

        @pl.when(core != at // half)
        def _():
            send_ref[place, :] = value.astype(BF16)

    mask = mask_ref[...]
    count_two = jnp.maximum(jnp.sum(mask, axis=1, keepdims=True), 1.0)
    total = jnp.zeros((seeds, hid), F32)
    for k in range(mask.shape[1]):
        at = (k + 1) * seeds
        total = total + mask[:, k : k + 1] * hid_ref[at : at + seeds, :].astype(F32)
    mean_two = (total / count_two).astype(BF16)
    self_two = hid_ref[0:seeds, :]
    for i in (4, 5, 6):
        copy(i).wait()
    out_ref[...] = (dot(self_two, w2s_ref[...]) + dot(mean_two, w2n_ref[...])).astype(BF16)
    put(2 * wide, dot(self_two, emb_ref[...], 0, 0))
    put(2 * wide + hid, dot(mean_two, emb_ref[...], 0, 0))
    for base, ref in ((0, self_ref), (wide, mean_ref)):
        for at in range(0, wide, step):
            put(base + at, dot(ref[:, at : at + step], bp_ref[...], 0, 0))


def finish_body(core_ref, *refs, cuts):
    (p, p_far, q, q_far), outs, held, sems = refs[:4], refs[4:8], refs[8:12], refs[12]
    quarter = p.shape[0]
    for near_core in range(2):

        @pl.when(core_ref[0] == near_core)
        def _():
            order = [(p, p_far), (q, q_far)]
            order = [pair[core != near_core] for core in range(2) for pair in order]
            for i, (first, last) in enumerate(cuts):
                at = first
                while at < last:
                    number, place = at // quarter, at % quarter
                    upto = min(last, (number + 1) * quarter)
                    held[i][at - first : upto - first, :] = order[number][
                        place : place + upto - at, :
                    ].astype(F32)
                    at = upto
                pltpu.make_async_copy(held[i], outs[i], sems.at[i]).start()

    for i in range(len(cuts)):
        pltpu.make_async_copy(held[i], outs[i], sems.at[i]).wait()


class Slice:
    def __init__(self):
        self.groups, self.members = lax.axis_size("group"), lax.axis_size("member")
        self.size = {"c": 2, "y": self.groups // 2, "z": 4, "x": self.members // 4}
        group, member = lax.axis_index("group"), lax.axis_index("member")
        self.at = {
            "c": group % 2,
            "y": group // 2,
            "z": member // self.size["x"],
            "x": member % self.size["x"],
        }

    def swap(self, array, axis, k):
        stride = {"c": 1, "y": 2, "z": self.size["x"], "x": 1}[axis]
        name, count = ("group", self.groups) if axis in "cy" else ("member", self.members)
        return lax.ppermute(array, name, [(i, i ^ (k * stride)) for i in range(count)])

    def part(self, terms, axis, k):
        depth = terms[0].shape[0] // self.size[axis]
        place = (self.at[axis] ^ k) * depth
        return [lax.dynamic_slice_in_dim(term, place, depth, 0) for term in terms]

    def scatter(self, terms, axis):
        others = range(1, self.size[axis])
        got = [self.swap(total(self.part(terms, axis, k)).astype(BF16), axis, k) for k in others]
        return self.part(terms, axis, 0) + got

    def gather(self, part, axis, dtype=BF16, parts=1):
        pieces = [part] + [self.swap(part, axis, k) for k in range(1, self.size[axis])]
        return join(pieces, self.at[axis], dtype, parts)


def total(terms):
    out = terms[0].astype(F32)
    for term in terms[1:]:
        out = out + term.astype(F32)
    return out


def on_device(
    store,
    cache,
    hot_local,
    hit_member,
    hit_row,
    miss_owner,
    miss_row,
    tgt_self,
    tgt_nbr,
    tgt_mask,
    seed_self,
    seed_nbr,
    seed_mask,
    w1_self,
    w1_nbr,
    w2_self,
    w2_nbr,
    d_emb,
):
    box = Slice()
    nx, ny, nz = box.size["x"], box.size["y"], box.size["z"]
    wide, hid = w1_self.shape
    owners = box.groups * box.members
    hits, misses = hit_row.shape[0], miss_row.shape[0]
    cap = 2 * misses // owners
    seeds, fan_two = seed_nbr.shape
    rows = seeds * (fan_two + 1)

    share = cache.shape[0] // box.groups
    group = lax.axis_index("group")
    mine = lax.dynamic_slice_in_dim(cache, group * share, share, 0).astype(BF16)

    ids, slot = kernel_call(
        request_body,
        (
            jax.ShapeDtypeStruct((owners, cap), I32),
            jax.ShapeDtypeStruct((1, misses), I32),
        ),
        flops=2 * misses * misses * 128,
    )(miss_owner.reshape(1, -1), miss_row.reshape(1, -1))
    store_low = store.astype(BF16)
    asked = lax.all_to_all(
        ids.reshape(owners, 1, cap), BOTH, split_axis=0, concat_axis=0, tiled=True
    ).reshape(owners, cap)
    near = [mine] + [box.swap(mine, "z", k) for k in range(1, nz // 2)]

    targets = jnp.concatenate([seed_self[None, :], seed_nbr.T], 0)
    names = jnp.concatenate([tgt_self[None, :] + 1, jnp.where(tgt_mask > 0, tgt_nbr + 1, 0).T], 0)
    member, line = hit_member.reshape(1, -1), hit_row.reshape(1, -1)
    holder = line // share
    code = ((holder % 2) ^ box.at["c"]) * ny + ((holder // 2) ^ box.at["y"])
    code = code * nx + ((member % nx) ^ box.at["x"])
    code = code * nz + ((member // nx) ^ box.at["z"])
    code = code * share + line % share
    hot = lax.dynamic_slice_in_dim(store, hot_local[0, 0] * BLOCK, BLOCK, 0).astype(BF16)

    def side(part):
        found = {(k, 0): box.swap(part, "x", k) for k in range(1, nx)}
        return found | {(0, k): box.swap(part, "y", k) for k in range(1, ny)}

    def corner(sides):
        found = {}
        for i in range(1, nx):
            for j in range(1, ny):
                upper, lower = jnp.split(sides[i, 0], 2)[0], jnp.split(sides[0, j], 2)[1]
                found[i, j] = [box.swap(upper, "y", j), box.swap(lower, "x", i)]
        return found

    def cached(*batches):
        pieces, bases = [], []
        for first, batch in batches:
            for (i, j), held in batch.items():
                start = first
                for piece in held:
                    for k in range(2):
                        pieces.append(piece if k == 0 else box.swap(piece, "c", 1))
                        bases.append(((k * ny + j) * nx + i) * nz * share + start)
                    start += piece.shape[0]
        return kernel_call(
            functools.partial(cached_body, bases=bases),
            jax.ShapeDtypeStruct((hits, wide), BF16),
            flops=2 * hits * wide * sum(piece.shape[0] for piece in pieces),
        )(code, *pieces)

    near = lax.optimization_barrier(near)
    near_own = jnp.concatenate(near, 0)
    half = near_own.shape[0]
    near_side = side(near_own)
    far = [box.swap(near[0], "z", k) for k in range(nz // 2, nz)]
    asked, store_low, near_side = lax.optimization_barrier((asked, store_low, near_side))
    served = kernel_call(
        serve_body,
        jax.ShapeDtypeStruct((owners * cap, wide), BF16),
        flops=2 * owners * cap * store.shape[0] * wide,
    )(asked, store_low)
    served, far, hot, names = lax.optimization_barrier((served, far, hot, names))
    miss_rows = lax.all_to_all(
        served.reshape(owners, cap, wide), BOTH, split_axis=0, concat_axis=0, tiled=True
    ).reshape(owners * cap, wide)

    sel_hit, sel_miss, count, back, flags, code = kernel_call(
        functools.partial(tables_body, hits=hits),
        (
            jax.ShapeDtypeStruct((2, rows, hits), BF16),
            jax.ShapeDtypeStruct((2, rows, owners * cap), BF16),
            jax.ShapeDtypeStruct((rows, 1), F32),
            jax.ShapeDtypeStruct((rows, hid), BF16),
            jax.ShapeDtypeStruct((seeds, fan_two), F32),
            jax.ShapeDtypeStruct((hits, 1), I32),
        ),
        flops=8 * rows * misses * owners * cap,
    )(targets, names, slot, seed_mask.T, code, d_emb, w2_self, w2_nbr)

    far_own = jnp.concatenate(far, 0)
    far_side = side(far_own)
    near_corner = corner(near_side)
    first = cached((0, {(0, 0): [near_own]}), (half, {(0, 0): [far_own]}))
    second = cached((0, {at: [piece] for at, piece in near_side.items()}))
    far_side, near_corner, first, second = lax.optimization_barrier(
        (far_side, near_corner, first, second)
    )
    far_corner = corner(far_side)
    third = cached((half, {at: [piece] for at, piece in far_side.items()}), (0, near_corner))
    far_corner, third = lax.optimization_barrier((far_corner, third))
    fourth = cached((half, far_corner))
    own_part, near_part = kernel_call(
        share_body,
        (
            jax.ShapeDtypeStruct((rows, wide), BF16),
            jax.ShapeDtypeStruct((rows, wide), F32),
        ),
        flops=4 * hits * wide * rows,
    )(sel_hit, first, second, third, fourth)

    hot, own_part, near_part = lax.optimization_barrier((hot, own_part, near_part))
    far_hot = [hot] + [box.swap(hot, "y", k) for k in range(1, ny)]
    grad_scale = 1.0 / math.sqrt(seeds * owners)
    total_rows = 2 * wide + 2 * hid
    vmem, hbm = pl.BlockSpec(memory_space=pltpu.VMEM), pl.BlockSpec(memory_space=pltpu.HBM)
    streamed = (
        miss_rows, w1_self, w1_nbr, back, w2_self, w2_nbr, d_emb, sel_miss, own_part, near_part
    )
    turn = 256
    emb, send, keep = pl.pallas_call(
        functools.partial(step_body, scale=grad_scale, step=turn),
        out_shape=(
            jax.ShapeDtypeStruct((seeds, hid), BF16),
            jax.ShapeDtypeStruct((total_rows // 2, hid), BF16),
            jax.ShapeDtypeStruct((total_rows // 2, hid), F32),
        ),
        in_specs=[pl.BlockSpec(memory_space=pltpu.SMEM)] + [hbm] * 10 + [vmem] * 2,
        out_specs=(vmem,) * 3,
        scratch_shapes=[pltpu.VMEM(array.shape, array.dtype) for array in streamed]
        + [
            pltpu.VMEM((rows, wide), BF16),
            pltpu.VMEM((rows, wide), BF16),
            pltpu.VMEM((rows, hid), BF16),
            pltpu.VMEM((rows, hid), BF16),
            pltpu.SemaphoreType.DMA((7 + 3 * (rows // turn),)),
        ],
        compiler_params=pltpu.CompilerParams(vmem_limit_bytes=2 * GRANT),
        cost_estimate=pl.CostEstimate(
            flops=0, bytes_accessed=0, transcendentals=0
        ),
    )(box.at["c"].reshape(1), *streamed, count, flags)
    send, far_hot = lax.optimization_barrier((send, far_hot))

    sums = [keep, box.swap(send, "c", 1)]
    p = [term[: total_rows // 4] for term in sums]
    q = [term[total_rows // 4 :] for term in sums]
    p, q = box.scatter(p, "x"), box.scatter(q, "y")
    near_hot = [box.swap(block, "c", 1) for block in far_hot]
    p, q, near_hot = lax.optimization_barrier((p, q, near_hot))
    pairs = [join(pair, box.at["c"], BF16)[0] for pair in zip(far_hot, near_hot)]
    (new_cache,) = join(pairs, box.at["y"], F32)
    p, q = box.scatter(p, "y"), box.scatter(q, "x")
    others = range(1, nz)
    outgoing = [
        jnp.concatenate([total(box.part(p, "z", k)), total(box.part(q, "z", k))], 0).astype(BF16)
        for k in others
    ]
    summed = jnp.concatenate([total(box.part(p, "z", 0)), total(box.part(q, "z", 0))], 0)
    incoming = [box.swap(outgoing[k - 1], "z", k) for k in others]
    summed = total([summed] + incoming).astype(BF16)
    p, q = box.gather(summed, "z", parts=2)
    (p,), (q,) = lax.optimization_barrier((box.gather(p, "y"), box.gather(q, "x")))
    (p,), (q,) = lax.optimization_barrier((box.gather(p, "x"), box.gather(q, "y")))
    p, q = (p, box.swap(p, "c", 1)), (q, box.swap(q, "c", 1))
    cuts = [(0, wide), (wide, 2 * wide), (2 * wide, 2 * wide + hid), (2 * wide + hid, total_rows)]
    shapes = [jax.ShapeDtypeStruct((last - at, hid), F32) for at, last in cuts]
    grads = pl.pallas_call(
        functools.partial(finish_body, cuts=cuts),
        out_shape=shapes,
        in_specs=[pl.BlockSpec(memory_space=pltpu.SMEM)] + [vmem] * 4,
        out_specs=[hbm] * 4,
        scratch_shapes=[pltpu.VMEM(x.shape, x.dtype) for x in shapes]
        + [pltpu.SemaphoreType.DMA((4,))],
        compiler_params=pltpu.CompilerParams(vmem_limit_bytes=GRANT),
    )(box.at["c"].reshape(1), *p, *q)
    return (emb, *grads, new_cache)


def solution(mesh):
    split = P(BOTH)
    in_specs = (split, P("member")) + (split,) * 11 + (P(),) * 4 + (split,)
    out_specs = (split, P(), P(), P(), P(), P("member"))
    return jax.shard_map(
        on_device, mesh=mesh, in_specs=in_specs, out_specs=out_specs, check_vma=False
    )
```

time: 437 us -> 207 us (0.47)
  waiting for transfers between devices: 277 us -> 58.8 us
  Pallas kernels: 0 us -> 57 us
  matrix products: 43.6 us -> 0 us
  local copies, waits for them, and re-layouts: 59.9 us -> 27.4 us
  starting transfers between devices: 24 us -> 48.8 us
  between operations: 16.5 us -> 2.18 us
    psum x1 -> x0, waiting for transfers between devices: 153 us -> none  [on_device(): lax.psum((term_w1_self, term_w1_nbr, term_w2_self, term_w2_nbr), ('group'...]
    all_to_all x4 -> x2, waiting for transfers between devices: 124 us -> 0.01 us  [the longest x1 0.01 us: on_device(): lax.all_to_all(ids.reshape(owners, 1, cap), BOTH, split_axis=0, concat_ax...]
    ppermute x0 -> x41, waiting for transfers between devices: none -> 58.8 us  [swap(): lax.ppermute(array, name, [(i, i ^ k * stride) for i in range(count)])]
    pallas_call x0 -> x18, Pallas kernels: none -> 57 us  [the longest x16 37.5 us: call(): pl.pallas_call(body, out_shape=out_shape, in_specs=specs, out_specs=jax.t...]
    dot_general x12 -> x0, matrix products: 43.6 us -> none  [the longest x1 19.4 us: on_device(): nbr_total = jnp.dot(adjacency, fetched, preferred_element_type=jnp.float32)]
    gather x7 -> x0, local copies, waits for them, and re-layouts: 43.1 us -> none  [the longest x1 9.18 us: on_device(): cache[lax.all_to_all(hit_ids, 'member', split_axis=0, concat_axis=0, tile...]
    ppermute x0 -> x41, starting transfers between devices: none -> 36.3 us  [swap(): lax.ppermute(array, name, [(i, i ^ k * stride) for i in range(count)])]
    all_to_all x4 -> x2, starting transfers between devices: 23.9 us -> 12.5 us  [the longest x1 7.64 us: on_device(): lax.all_to_all(served.reshape(owners, cap, wide), BOTH, split_axis=0, con...]
  transfers between devices with their start and end apart: 6 -> 43, of which waited for: 3 -> 25; matrix products, arithmetic and copies ran while one was open for 23% -> 11% of each run, Pallas kernels for 0% -> 26%
where the time goes in v1:
time: 207 us; the launch traced here: 206 us
  waiting for transfers between devices  58.8 us (28%)
  Pallas kernels  57 us (28%)
  starting transfers between devices  48.8 us (24%)
  local copies, waits for them, and re-layouts  27.4 us (13%)
  other arithmetic  11.4 us (6%)
  between operations  2.18 us (1%)
    ppermute x41, waiting for transfers between devices, swap(): lax.ppermute(array, name, [(i, i ^ k * stride) for i in range(count)])  58.8 us
    pallas_call x16, Pallas kernels, call(): pl.pallas_call(body, out_shape=out_shape, in_specs=specs, out_specs=jax.t...  37.5 us
    ppermute x41, starting transfers between devices, swap(): lax.ppermute(array, name, [(i, i ^ k * stride) for i in range(count)])  36.3 us
    pallas_call x1, Pallas kernels, on_device(): pl.pallas_call(functools.partial(step_body, scale=grad_scale, step=turn),...  16.8 us
    unnamed x66, local copies, waits for them, and re-layouts  15 us
    all_to_all x1, starting transfers between devices, on_device(): lax.all_to_all(served.reshape(owners, cap, wide), BOTH, split_axis=0, con...  7.64 us
    all_to_all x1, starting transfers between devices, on_device(): lax.all_to_all(ids.reshape(owners, 1, cap), BOTH, split_axis=0, concat_ax...  4.84 us
    convert_element_type x4, other arithmetic, scatter(): total(self.part(terms, axis, k)).astype(BF16)  4.23 us
  transfers between devices with their start and end apart: 43, of which 25 were waited for; matrix products, arithmetic and copies ran while one was open for 11% of the time, Pallas kernels for 26%

profile of v1, /device:TPU:0, one launch (start us, length us, event | category | flops | bytes accessed | tf_op | source)
XLA Modules:
  0.0 205.7 jit_solution(9973760969425504701)
XLA Ops:
  3.0 3.0 %collective-permute-start = (bf16[128,1024]{1,0:T(8,128)(2,1)}, bf16[128,1024]{1,0:T(8,128)(2,1)S(1)}, u32[]{:S(2)}, u32[]{:S(2)}) collective-permute-start(bf16[128,1024]{1,0:T(8,128)(2,1)} %dynamic-slice_convert_fusion.1), channel_id=1, source_target_pairs={{0,2},{1,3},{2,0},{3,1},{4,6},{5,7},{6,4},{7,5},{8,10},{9,11},{10,... | collective-permute-start | bytes 786440 | tf_op jit(solution)/shard_map/ppermute | solution.py:295
  8.3 4.8 %all-to-all-start = ((s32[32,1,32]{2,1,0:T(1,128)}), s32[32,1,32]{2,1,0:T(1,128)S(1)}, u32[]{:S(2)}, u32[]{:S(2)}) async-start(s32[32,1,32]{2,1,0:T(1,128)} %bitcast.4), calls=%async_computation | async-start | bytes 32768 | tf_op jit(solution)/shard_map/all_to_all | solution.py:361
  19.7 2.5 %collective-permute-start.3 = (bf16[128,1024]{1,0:T(8,128)(2,1)}, bf16[128,1024]{1,0:T(8,128)(2,1)}, u32[]{:S(2)}, u32[]{:S(2)}) collective-permute-start(bf16[128,1024]{1,0:T(8,128)(2,1)} %dynamic-slice_convert_fusion.1), channel_id=1, source_target_pairs={{0,4},{1,5},{2,6},{3,7},{4,0},{5,1},{6,2},{7,3},{8,12},{9,13},{10,... | collective-permute-start | bytes 786440 | tf_op jit(solution)/shard_map/ppermute | solution.py:295
  26.7 2.5 %convert_element_type.126.store_ref = bf16[1024,1024]{1,0:T(8,128)(2,1)S(1)} convert(f32[1024,1024]{1,0:T(8,128)} %param.18) | non-fusion elementwise | flops 1048576 | bytes 6291456 | tf_op jit(solution)/shard_map/convert_element_type | solution.py:360
  31.3 2.6 %shard_map.218 = bf16[1024,1024]{1,0:T(8,128)(2,1)S(1)} custom-call(s32[32,32]{1,0:T(8,128)S(1)} %bitcast.22, bf16[1024,1024]{1,0:T(8,128)(2,1)S(1)} %convert_element_type.126.store_ref), custom_call_target="tpu_custom_call" | custom-call | tf_op jit(solution)/shard_map/pallas_call | solution.py:29
  35.2 5.8 %collective-permute-done.3 = bf16[128,1024]{1,0:T(8,128)(2,1)} collective-permute-done((bf16[128,1024]{1,0:T(8,128)(2,1)}, bf16[128,1024]{1,0:T(8,128)(2,1)}, u32[]{:S(2)}, u32[]{:S(2)}) %collective-permute-start.3) | collective-permute-done | bytes 262176 | tf_op jit(solution)/shard_map/ppermute | solution.py:295
  41.1 7.6 %all-to-all-start.1 = ((bf16[32,32,1024]{2,1,0:T(8,128)(2,1)}), bf16[32,32,1024]{2,1,0:T(8,128)(2,1)}, u32[]{:S(2)}, u32[]{:S(2)}) async-start(bf16[32,32,1024]{2,1,0:T(8,128)(2,1)} %bitcast.21), calls=%async_computation.1 | async-start | bytes 4194304 | tf_op jit(solution)/shard_map/all_to_all | solution.py:416
  60.5 10.4 %shard_map.219 = (bf16[2,768,1024]{2,1,0:T(8,128)(2,1)S(1)}, bf16[2,768,1024]{2,1,0:T(8,128)(2,1)S(1)}, f32[768,1]{1,0:T(8,128)S(1)}, bf16[768,512]{1,0:T(8,128)...) custom-call(s32[6,128]{1,0:T(8,128)S(1)} %pad_add_fusion.1.targets_ref, s32[11,1024]{1,0:T(8,128)S(1)} %copy-done.21, ...), custom_call_target="tpu_custom_call" | custom-call | tf_op jit(solution)/shard_map/pallas_call | solution.py:29
  73.7 4.4 %shard_map.220.refs_0_ = bf16[1024,1024]{1,0:T(8,128)(2,1)S(1)} custom-call(s32[1024,1]{1,0:T(8,128)S(1)} %get-tuple-element.79.code_ref, bf16[256,1024]{1,0:T(8,128)(2,1)} %constant_dynamic-update-slice_fusion.refs_0_, bf16[256,1024]{1,0:T(8,128)(2,1)S(1)} %copy-done.15, bf16[256,1024]{1,0:T(8,128)(2,1)} %constant_dynamic-update-slice_fusion.2.refs_2_, ...), custom_call_target="tpu_custom_call" | custom-call | tf_op jit(solution)/shard_map/pallas_call | solution.py:29
  78.1 4.1 %shard_map.221.refs_1_ = bf16[1024,1024]{1,0:T(8,128)(2,1)S(1)} custom-call(s32[1024,1]{1,0:T(8,128)S(1)} %get-tuple-element.79.code_ref, bf16[256,1024]{1,0:T(8,128)(2,1)S(1)} %copy-done.9, bf16[256,1024]{1,0:T(8,128)(2,1)S(1)} %copy-done.17, bf16[256,1024]{1,0:T(8,128)(2,1)S(1)} %copy-done.11, bf16[256,1024]{1,0:T(8,128)(2,1)} %collective-permute-done.12.refs_3_), custom_call_target="tpu_custom_call" | custom-call | tf_op jit(solution)/shard_map/pallas_call | solution.py:29
  82.2 7.9 %collective-permute-done.7.refs_4_ = bf16[128,1024]{1,0:T(8,128)(2,1)} collective-permute-done((bf16[128,1024]{1,0:T(8,128)(2,1)}, bf16[128,1024]{1,0:T(8,128)(2,1)}, u32[]{:S(2)}, u32[]{:S(2)}) %collective-permute-start.7) | collective-permute-done | bytes 262176 | tf_op jit(solution)/shard_map/ppermute | solution.py:295
  94.0 6.5 %shard_map.222.refs_2_ = bf16[1024,1024]{1,0:T(8,128)(2,1)S(1)} custom-call(s32[1024,1]{1,0:T(8,128)S(1)} %get-tuple-element.79.code_ref, bf16[256,1024]{1,0:T(8,128)(2,1)} %collective-permute-done.5.refs_0_, bf16[256,1024]{1,0:T(8,128)(2,1)S(1)} %collective-permute-done.15.refs_1_, bf16[256,1024]{1,0:T(8,128)(2,1)} %collective-permute-done.6.refs_2_, ...), custom_call_target="tpu_custom_call" | custom-call | tf_op jit(solution)/shard_map/pallas_call | solution.py:29
  105.2 3.1 %shard_map.223.refs_3_ = bf16[1024,1024]{1,0:T(8,128)(2,1)S(1)} custom-call(s32[1024,1]{1,0:T(8,128)S(1)} %get-tuple-element.79.code_ref, bf16[128,1024]{1,0:T(8,128)(2,1)S(1)} %collective-permute-done.13.refs_0_, bf16[128,1024]{1,0:T(8,128)(2,1)S(1)} %collective-permute-done.19.refs_1_, bf16[128,1024]{1,0:T(8,128)(2,1)S(1)} %collective-permute-done.14.refs_2_, ...), custom_call_target="tpu_custom_call" | custom-call | tf_op jit(solution)/shard_map/pallas_call | solution.py:29
  108.3 3.7 %shard_map.224 = (bf16[768,1024]{1,0:T(8,128)(2,1)S(1)}, f32[768,1024]{1,0:T(8,128)S(1)}) custom-call(bf16[2,768,1024]{2,1,0:T(8,128)(2,1)S(1)} %get-tuple-element.74.sel_ref, bf16[1024,1024]{1,0:T(8,128)(2,1)S(1)} %shard_map.220.refs_0_, bf16[1024,1024]{1,0:T(8,128)(2,1)S(1)} %shard_map.221.refs_1_, bf16[1024,1024]{1,0:T(8,128)(2,1)S(1)} %shard_map.222.refs_2_, ...), custom_call_target="tpu_custom_call" | custom-call | tf_op jit(solution)/shard_map/pallas_call | solution.py:29
  116.2 16.8 %shard_map.225 = (bf16[128,512]{1,0:T(8,128)(2,1)}, bf16[1536,512]{1,0:T(8,128)(2,1)}, f32[1536,512]{1,0:T(8,128)}) custom-call(s32[1]{0:T(128)} %bitcast.core_ref.me_ref, bf16[1024,1024]{1,0:T(8,128)(2,1)} %bitcast.10.refs_0_, bf16[1024,512]{1,0:T(8,128)(2,1)} %refs_1_.1, bf16[1024,512]{1,0:T(8,128)(2,1)} %refs_2_.1, bf16[768,512]{1,0:T(8,128)(2,1)} %copy-done.12, ...), custom_call_target="tpu_custom_call" | custom-call | tf_op jit(solution)/shard_map/pallas_call | solution.py:463
  144.2 6.6 %collective-permute-done.23 = bf16[384,512]{1,0:T(8,128)(2,1)S(1)} collective-permute-done((bf16[384,512]{1,0:T(8,128)(2,1)}, bf16[384,512]{1,0:T(8,128)(2,1)S(1)}, u32[]{:S(2)}, u32[]{:S(2)}) %collective-permute-start.23) | collective-permute-done | bytes 393248 | tf_op jit(solution)/shard_map/ppermute | solution.py:295
  156.5 3.5 %collective-permute-done.28 = bf16[192,512]{1,0:T(8,128)(2,1)} collective-permute-done((bf16[192,512]{1,0:T(8,128)(2,1)S(1)}, bf16[192,512]{1,0:T(8,128)(2,1)}, u32[]{:S(2)}, u32[]{:S(2)}) %collective-permute-start.28) | collective-permute-done | bytes 196640 | tf_op jit(solution)/shard_map/ppermute | solution.py:295
  162.9 3.4 %collective-permute-start.31 = (bf16[96,512]{1,0:T(8,128)(2,1)S(1)}, bf16[96,512]{1,0:T(8,128)(2,1)S(1)}, u32[]{:S(2)}, u32[]{:S(2)}) collective-permute-start(bf16[96,512]{1,0:T(8,128)(2,1)S(1)} %pad_maximum_fusion.2), channel_id=1, source_target_pairs={{0,6},{1,7},{2,4},{3,5},{4,2},{5,3},{6,0},{7,1},{8,14},{9,15},{10,... | collective-permute-start | bytes 294920 | tf_op jit(solution)/shard_map/ppermute | solution.py:295
  167.5 2.7 %collective-permute-done.31 = bf16[96,512]{1,0:T(8,128)(2,1)S(1)} collective-permute-done((bf16[96,512]{1,0:T(8,128)(2,1)S(1)}, bf16[96,512]{1,0:T(8,128)(2,1)S(1)}, u32[]{:S(2)}, u32[]{:S(2)}) %collective-permute-start.31) | collective-permute-done | bytes 98336 | tf_op jit(solution)/shard_map/ppermute | solution.py:295
  173.2 2.9 %collective-permute-start.33 = (bf16[96,512]{1,0:T(8,128)(2,1)S(1)}, bf16[96,512]{1,0:T(8,128)(2,1)S(1)}, u32[]{:S(2)}, u32[]{:S(2)}) collective-permute-start(bf16[96,512]{1,0:T(8,128)(2,1)S(1)} %fusion.2.refs_0_), channel_id=1, source_target_pairs={{0,4},{1,5},{2,6},{3,7},{4,0},{5,1},{6,2},{7,3},{8,12},{9,13},{10,... | collective-permute-start | bytes 294920 | tf_op jit(solution)/shard_map/ppermute | solution.py:295
  177.3 4.1 %collective-permute-done.33.refs_2_ = bf16[96,512]{1,0:T(8,128)(2,1)S(1)} collective-permute-done((bf16[96,512]{1,0:T(8,128)(2,1)S(1)}, bf16[96,512]{1,0:T(8,128)(2,1)S(1)}, u32[]{:S(2)}, u32[]{:S(2)}) %collective-permute-start.33) | collective-permute-done | bytes 98336 | tf_op jit(solution)/shard_map/ppermute | solution.py:295
  184.2 4.2 %collective-permute-done.35.refs_1_ = bf16[192,512]{1,0:T(8,128)(2,1)S(1)} collective-permute-done((bf16[192,512]{1,0:T(8,128)(2,1)S(1)}, bf16[192,512]{1,0:T(8,128)(2,1)S(1)}, u32[]{:S(2)}, u32[]{:S(2)}) %collective-permute-start.35) | collective-permute-done | bytes 196640 | tf_op jit(solution)/shard_map/ppermute | solution.py:295
  193.0 5.6 %collective-permute-done.37.refs_1_ = bf16[384,512]{1,0:T(8,128)(2,1)S(1)} collective-permute-done((bf16[384,512]{1,0:T(8,128)(2,1)S(1)}, bf16[384,512]{1,0:T(8,128)(2,1)S(1)}, u32[]{:S(2)}, u32[]{:S(2)}) %collective-permute-start.37) | collective-permute-done | bytes 393248 | tf_op jit(solution)/shard_map/ppermute | solution.py:295
  202.6 2.8 %shard_map.231 = (f32[1024,512]{1,0:T(8,128)}, f32[1024,512]{1,0:T(8,128)}, f32[512,512]{1,0:T(8,128)}, f32[512,512]{1,0:T(8,128)}) custom-call(s32[1]{0:T(128)} %bitcast.core_ref.me_ref, bf16[768,512]{1,0:T(8,128)(2,1)S(1)} %shard_map.229.refs_0_, bf16[768,512]{1,0:T(8,128)(2,1)S(1)} %collective-permute-done.39.refs_1_, ...), custom_call_target="tpu_custom_call" | custom-call | tf_op jit(solution)/shard_map/pallas_call | solution.py:510
  (173 shorter events, 82.1 us)
Async XLA Ops:
  3.0 10.2 %collective-permute-start = (bf16[128,1024]{1,0:T(8,128)(2,1)}, bf16[128,1024]{1,0:T(8,128)(2,1)S(1)}, u32[]{:S(2)}, u32[]{:S(2)}) collective-permute-start(bf16[128,1024]{1,0:T(8,128)(2,1)} %dynamic-slice_convert_fusion.1), channel_id=1, source_target_pairs={{0,2},{1,3},{2,0},{3,1},{4,6},{5,7},{6,4},{7,5},{8,10},{9,11},{10,... | collective-permute-start | bytes 786440 | tf_op jit(solution)/shard_map/ppermute | solution.py:295
  8.3 20.8 %all-to-all-start = ((s32[32,1,32]{2,1,0:T(1,128)}), s32[32,1,32]{2,1,0:T(1,128)S(1)}, u32[]{:S(2)}, u32[]{:S(2)}) async-start(s32[32,1,32]{2,1,0:T(1,128)} %bitcast.4), calls=%async_computation | async-start | bytes 32768 | tf_op jit(solution)/shard_map/all_to_all | solution.py:361
  15.6 14.4 %collective-permute-start.1 = (bf16[256,1024]{1,0:T(8,128)(2,1)}, bf16[256,1024]{1,0:T(8,128)(2,1)S(1)}, u32[]{:S(2)}, u32[]{:S(2)}) collective-permute-start(bf16[256,1024]{1,0:T(8,128)(2,1)} %constant_dynamic-update-slice_fusion.refs_0_), channel_id=1, source_target_pairs={{0,16},{8,24},{16,0},{24,8},{1,17},{9,25},{17,1},{25,9},{2,18},{10... | collective-permute-start | bytes 1572872 | tf_op jit(solution)/shard_map/ppermute | solution.py:295
  17.3 13.9 %collective-permute-start.2 = (bf16[256,1024]{1,0:T(8,128)(2,1)}, bf16[256,1024]{1,0:T(8,128)(2,1)S(1)}, u32[]{:S(2)}, u32[]{:S(2)}) collective-permute-start(bf16[256,1024]{1,0:T(8,128)(2,1)} %constant_dynamic-update-slice_fusion.refs_0_), channel_id=1, source_target_pairs={{0,1},{1,0},{2,3},{3,2},{4,5},{5,4},{6,7},{7,6},{8,9},{9,8},{10,11... | collective-permute-start | bytes 1572872 | tf_op jit(solution)/shard_map/ppermute | solution.py:295
  19.7 21.4 %collective-permute-start.3 = (bf16[128,1024]{1,0:T(8,128)(2,1)}, bf16[128,1024]{1,0:T(8,128)(2,1)}, u32[]{:S(2)}, u32[]{:S(2)}) collective-permute-start(bf16[128,1024]{1,0:T(8,128)(2,1)} %dynamic-slice_convert_fusion.1), channel_id=1, source_target_pairs={{0,4},{1,5},{2,6},{3,7},{4,0},{5,1},{6,2},{7,3},{8,12},{9,13},{10,... | collective-permute-start | bytes 786440 | tf_op jit(solution)/shard_map/ppermute | solution.py:295
  22.2 18.9 %collective-permute-start.4 = (bf16[128,1024]{1,0:T(8,128)(2,1)}, bf16[128,1024]{1,0:T(8,128)(2,1)}, u32[]{:S(2)}, u32[]{:S(2)}) collective-permute-start(bf16[128,1024]{1,0:T(8,128)(2,1)} %dynamic-slice_convert_fusion.1), channel_id=1, source_target_pairs={{0,6},{1,7},{2,4},{3,5},{4,2},{5,3},{6,0},{7,1},{8,14},{9,15},{10,... | collective-permute-start | bytes 786440 | tf_op jit(solution)/shard_map/ppermute | solution.py:295
  41.1 75.1 %all-to-all-start.1 = ((bf16[32,32,1024]{2,1,0:T(8,128)(2,1)}), bf16[32,32,1024]{2,1,0:T(8,128)(2,1)}, u32[]{:S(2)}, u32[]{:S(2)}) async-start(bf16[32,32,1024]{2,1,0:T(8,128)(2,1)} %bitcast.21), calls=%async_computation.1 | async-start | bytes 4194304 | tf_op jit(solution)/shard_map/all_to_all | solution.py:416
  52.8 25.3 %collective-permute-start.12 = (bf16[256,1024]{1,0:T(8,128)(2,1)S(1)}, bf16[256,1024]{1,0:T(8,128)(2,1)}, u32[]{:S(2)}, u32[]{:S(2)}) collective-permute-start(bf16[256,1024]{1,0:T(8,128)(2,1)S(1)} %copy-done.11), channel_id=1, source_target_pairs={{0,8},{8,0},{16,24},{24,16},{1,9},{9,1},{17,25},{25,17},{2,10},{10... | collective-permute-start | bytes 1572872 | tf_op jit(solution)/shard_map/ppermute | solution.py:295
  53.2 36.9 %collective-permute-start.5 = (bf16[256,1024]{1,0:T(8,128)(2,1)}, bf16[256,1024]{1,0:T(8,128)(2,1)}, u32[]{:S(2)}, u32[]{:S(2)}) collective-permute-start(bf16[256,1024]{1,0:T(8,128)(2,1)} %constant_dynamic-update-slice_fusion.2.refs_2_), channel_id=1, source_target_pairs={{0,16},{8,24},{16,0},{24,8},{1,17},{9,25},{17,1},{25,9},{2,18},{10... | collective-permute-start | bytes 1572872 | tf_op jit(solution)/shard_map/ppermute | solution.py:295
  54.8 35.4 %collective-permute-start.6 = (bf16[256,1024]{1,0:T(8,128)(2,1)}, bf16[256,1024]{1,0:T(8,128)(2,1)}, u32[]{:S(2)}, u32[]{:S(2)}) collective-permute-start(bf16[256,1024]{1,0:T(8,128)(2,1)} %constant_dynamic-update-slice_fusion.2.refs_2_), channel_id=1, source_target_pairs={{0,1},{1,0},{2,3},{3,2},{4,5},{5,4},{6,7},{7,6},{8,9},{9,8},{10,11... | collective-permute-start | bytes 1572872 | tf_op jit(solution)/shard_map/ppermute | solution.py:295
  58.5 31.6 %collective-permute-start.7 = (bf16[128,1024]{1,0:T(8,128)(2,1)}, bf16[128,1024]{1,0:T(8,128)(2,1)}, u32[]{:S(2)}, u32[]{:S(2)}) collective-permute-start(bf16[128,1024]{1,0:T(8,128)(2,1)} %split.12), channel_id=1, source_target_pairs={{0,16},{8,24},{16,0},{24,8},{1,17},{9,25},{17,1},{25,9},{2,18},{10... | collective-permute-start | bytes 786440 | tf_op jit(solution)/shard_map/ppermute | solution.py:295
  59.8 30.3 %collective-permute-start.8 = (bf16[128,1024]{1,0:T(8,128)(2,1)}, bf16[128,1024]{1,0:T(8,128)(2,1)}, u32[]{:S(2)}, u32[]{:S(2)}) collective-permute-start(bf16[128,1024]{1,0:T(8,128)(2,1)} %split.13), channel_id=1, source_target_pairs={{0,1},{1,0},{2,3},{3,2},{4,5},{5,4},{6,7},{7,6},{8,9},{9,8},{10,11... | collective-permute-start | bytes 786440 | tf_op jit(solution)/shard_map/ppermute | solution.py:295
  93.2 9.1 %collective-permute-start.13 = (bf16[128,1024]{1,0:T(8,128)(2,1)S(1)}, bf16[128,1024]{1,0:T(8,128)(2,1)S(1)}, u32[]{:S(2)}, u32[]{:S(2)}) collective-permute-start(bf16[128,1024]{1,0:T(8,128)(2,1)S(1)} %split.14), channel_id=1, source_target_pairs={{0,16},{8,24},{16,0},{24,8},{1,17},{9,25},{17,1},{25,9},{2,18},{10... | collective-permute-start | bytes 786440 | tf_op jit(solution)/shard_map/ppermute | solution.py:295
  94.0 9.3 %collective-permute-start.14 = (bf16[128,1024]{1,0:T(8,128)(2,1)S(1)}, bf16[128,1024]{1,0:T(8,128)(2,1)S(1)}, u32[]{:S(2)}, u32[]{:S(2)}) collective-permute-start(bf16[128,1024]{1,0:T(8,128)(2,1)S(1)} %split.15), channel_id=1, source_target_pairs={{0,1},{1,0},{2,3},{3,2},{4,5},{5,4},{6,7},{7,6},{8,9},{9,8},{10,11... | collective-permute-start | bytes 786440 | tf_op jit(solution)/shard_map/ppermute | solution.py:295
  114.8 18.1 %collective-permute-start.21 = (bf16[128,1024]{1,0:T(8,128)(2,1)S(1)}, bf16[128,1024]{1,0:T(8,128)(2,1)S(1)}, u32[]{:S(2)}, u32[]{:S(2)}) collective-permute-start(bf16[128,1024]{1,0:T(8,128)(2,1)S(1)} %dynamic-slice_convert_fusion.refs_0_), channel_id=1, source_target_pairs={{0,16},{8,24},{16,0},{24,8},{1,17},{9,25},{17,1},{25,9},{2,18},{10... | collective-permute-start | bytes 786440 | tf_op jit(solution)/shard_map/ppermute | solution.py:295
  139.4 11.4 %collective-permute-start.23 = (bf16[384,512]{1,0:T(8,128)(2,1)}, bf16[384,512]{1,0:T(8,128)(2,1)S(1)}, u32[]{:S(2)}, u32[]{:S(2)}) collective-permute-start(bf16[384,512]{1,0:T(8,128)(2,1)} %get-tuple-element.134), channel_id=1, source_target_pairs={{0,1},{1,0},{2,3},{3,2},{4,5},{5,4},{6,7},{7,6},{8,9},{9,8},{10,11... | collective-permute-start | bytes 1179656 | tf_op jit(solution)/shard_map/ppermute | solution.py:295
  141.7 11.2 %collective-permute-start.24 = (bf16[384,512]{1,0:T(8,128)(2,1)}, bf16[384,512]{1,0:T(8,128)(2,1)}, u32[]{:S(2)}, u32[]{:S(2)}) collective-permute-start(bf16[384,512]{1,0:T(8,128)(2,1)} %get-tuple-element.130), channel_id=1, source_target_pairs={{0,16},{8,24},{16,0},{24,8},{1,17},{9,25},{17,1},{25,9},{2,18},{10... | collective-permute-start | bytes 1179656 | tf_op jit(solution)/shard_map/ppermute | solution.py:295
  162.9 7.3 %collective-permute-start.31 = (bf16[96,512]{1,0:T(8,128)(2,1)S(1)}, bf16[96,512]{1,0:T(8,128)(2,1)S(1)}, u32[]{:S(2)}, u32[]{:S(2)}) collective-permute-start(bf16[96,512]{1,0:T(8,128)(2,1)S(1)} %pad_maximum_fusion.2), channel_id=1, source_target_pairs={{0,6},{1,7},{2,4},{3,5},{4,2},{5,3},{6,0},{7,1},{8,14},{9,15},{10,... | collective-permute-start | bytes 294920 | tf_op jit(solution)/shard_map/ppermute | solution.py:295
  166.2 6.3 %collective-permute-start.30 = (bf16[96,512]{1,0:T(8,128)(2,1)S(1)}, bf16[96,512]{1,0:T(8,128)(2,1)S(1)}, u32[]{:S(2)}, u32[]{:S(2)}) collective-permute-start(bf16[96,512]{1,0:T(8,128)(2,1)S(1)} %pad_maximum_fusion.1), channel_id=1, source_target_pairs={{0,4},{1,5},{2,6},{3,7},{4,0},{5,1},{6,2},{7,3},{8,12},{9,13},{10,... | collective-permute-start | bytes 294920 | tf_op jit(solution)/shard_map/ppermute | solution.py:295
  173.2 8.2 %collective-permute-start.33 = (bf16[96,512]{1,0:T(8,128)(2,1)S(1)}, bf16[96,512]{1,0:T(8,128)(2,1)S(1)}, u32[]{:S(2)}, u32[]{:S(2)}) collective-permute-start(bf16[96,512]{1,0:T(8,128)(2,1)S(1)} %fusion.2.refs_0_), channel_id=1, source_target_pairs={{0,4},{1,5},{2,6},{3,7},{4,0},{5,1},{6,2},{7,3},{8,12},{9,13},{10,... | collective-permute-start | bytes 294920 | tf_op jit(solution)/shard_map/ppermute | solution.py:295
  176.1 6.5 %collective-permute-start.34 = (bf16[96,512]{1,0:T(8,128)(2,1)S(1)}, bf16[96,512]{1,0:T(8,128)(2,1)S(1)}, u32[]{:S(2)}, u32[]{:S(2)}) collective-permute-start(bf16[96,512]{1,0:T(8,128)(2,1)S(1)} %fusion.2.refs_0_), channel_id=1, source_target_pairs={{0,6},{1,7},{2,4},{3,5},{4,2},{5,3},{6,0},{7,1},{8,14},{9,15},{10,... | collective-permute-start | bytes 294920 | tf_op jit(solution)/shard_map/ppermute | solution.py:295
  183.6 7.1 %collective-permute-start.36 = (bf16[192,512]{1,0:T(8,128)(2,1)S(1)}, bf16[192,512]{1,0:T(8,128)(2,1)S(1)}, u32[]{:S(2)}, u32[]{:S(2)}) collective-permute-start(bf16[192,512]{1,0:T(8,128)(2,1)S(1)} %get-tuple-element.109.refs_0_), channel_id=1, source_target_pairs={{0,1},{1,0},{2,3},{3,2},{4,5},{5,4},{6,7},{7,6},{8,9},{9,8},{10,11... | collective-permute-start | bytes 589832 | tf_op jit(solution)/shard_map/ppermute | solution.py:295
  190.7 7.8 %collective-permute-start.37 = (bf16[384,512]{1,0:T(8,128)(2,1)S(1)}, bf16[384,512]{1,0:T(8,128)(2,1)S(1)}, u32[]{:S(2)}, u32[]{:S(2)}) collective-permute-start(bf16[384,512]{1,0:T(8,128)(2,1)S(1)} %shard_map.227.refs_0_), channel_id=1, source_target_pairs={{0,1},{1,0},{2,3},{3,2},{4,5},{5,4},{6,7},{7,6},{8,9},{9,8},{10,11... | collective-permute-start | bytes 1179656 | tf_op jit(solution)/shard_map/ppermute | solution.py:295
  191.3 7.8 %collective-permute-start.38 = (bf16[384,512]{1,0:T(8,128)(2,1)S(1)}, bf16[384,512]{1,0:T(8,128)(2,1)S(1)}, u32[]{:S(2)}, u32[]{:S(2)}) collective-permute-start(bf16[384,512]{1,0:T(8,128)(2,1)S(1)} %shard_map.228.refs_0_), channel_id=1, source_target_pairs={{0,16},{8,24},{16,0},{24,8},{1,17},{9,25},{17,1},{25,9},{2,18},{10... | collective-permute-start | bytes 1179656 | tf_op jit(solution)/shard_map/ppermute | solution.py:295
  (51 other events, 275.4 us)

commit v2 on v1

--- a/solution.py
+++ b/solution.py
@@ -22,7 +22,7 @@
     return lax.broadcasted_iota(I32, shape, dim)
 
 
-def kernel_call(body, out_shape, scratch=(), smem=0, flops=0):
+def kernel_call(body, out_shape, scratch=(), smem=0, grant=GRANT):
     def call(*operands):
         specs = [pl.BlockSpec(memory_space=pltpu.SMEM)] * smem
         specs += [pl.BlockSpec(memory_space=pltpu.VMEM)] * (len(operands) - smem)
@@ -32,7 +32,7 @@
             in_specs=specs,
             out_specs=jax.tree.map(lambda _: pl.BlockSpec(memory_space=pltpu.VMEM), out_shape),
             scratch_shapes=list(scratch),
-            compiler_params=pltpu.CompilerParams(vmem_limit_bytes=GRANT),
+            compiler_params=pltpu.CompilerParams(vmem_limit_bytes=grant),
             cost_estimate=pl.CostEstimate(flops=0, bytes_accessed=0, transcendentals=0),
         )(*operands)
 
@@ -77,6 +77,7 @@
     misses = slot_ref.shape[1]
     slots = sel_miss_ref.shape[2]
     fan, fan_two = names_ref.shape[0] - 1, mask_ref.shape[0]
+    one, zero = jnp.array(1, BF16), jnp.array(0, BF16)
 
     def columns(rows):
         rows = rows.astype(F32)
@@ -96,12 +97,11 @@
         here = named[:, 1:] >= 0
         count_ref[cut, :] = jnp.maximum(jnp.sum(here.astype(F32), axis=1, keepdims=True), 1.0)
         for first, width in ((0, hits), (hits, misses)):
-            lane = iota((seeds, width), 1) + first
-            own = jnp.where(named[:, 0:1] == lane, 1.0, 0.0).astype(BF16)
-            near = jnp.zeros((seeds, width), F32)
+            lane = (iota((seeds, width), 1) + first).astype(jnp.int16)
+            own = jnp.where(named[:, 0:1].astype(jnp.int16) == lane, one, zero)
+            near = jnp.zeros((seeds, width), BF16)
             for k in range(1, fan + 1):
-                near = near + jnp.where(named[:, k : k + 1] == lane, 1.0, 0.0)
-            near = near.astype(BF16)
+                near = near + jnp.where(named[:, k : k + 1].astype(jnp.int16) == lane, one, zero)
             if first == 0:
                 sel_hit_ref[0, cut, :] = own
                 sel_hit_ref[1, cut, :] = near
@@ -173,7 +173,8 @@
 
 
 def step_body(core_ref, *refs, scale, step):
-    sources, (count_ref, mask_ref, out_ref, send_ref, keep_ref, *refs) = refs[:10], refs[10:]
+    sources, (count_ref, mask_ref, out_ref, *refs) = refs[:10], refs[10:]
+    send_refs, keep_refs, refs = refs[:2], refs[2:4], refs[4:]
     held, (self_ref, mean_ref, hid_ref, bp_ref, sems) = refs[:10], refs[10:]
     miss_ref, w1s_ref, w1n_ref, back_ref, w2s_ref, w2n_ref, emb_ref, *turned = held
     sel_ref, own_ref, near_ref = turned
@@ -221,19 +222,25 @@
         bp_ref[cut, :] = (back_ref[cut, :].astype(F32) * slope).astype(BF16)
 
     core = core_ref[0]
-    half = (2 * wide + 2 * hid) // 2
+    quarter = keep_refs[0].shape[0]
 
     def put(at, value):
         value = value * scale
-        place = slice(at % half, at % half + value.shape[0])
-
-        @pl.when(core == at // half)
-        def _():
-            keep_ref[place, :] = value
-
-        @pl.when(core != at // half)
-        def _():
-            send_ref[place, :] = value.astype(BF16)
+        first = 0
+        while first < value.shape[0]:
+            number, place = (at + first) // quarter, (at + first) % quarter
+            depth = min(value.shape[0] - first, quarter - place)
+            part, rows_at = value[first : first + depth], slice(place, place + depth)
+
+            @pl.when(core == number // 2)
+            def _(part=part, rows_at=rows_at, ref=keep_refs[number % 2]):
+                ref[rows_at, :] = part.astype(BF16)
+
+            @pl.when(core != number // 2)
+            def _(part=part, rows_at=rows_at, ref=send_refs[number % 2]):
+                ref[rows_at, :] = part.astype(BF16)
+
+            first += depth
 
     mask = mask_ref[...]
     count_two = jnp.maximum(jnp.sum(mask, axis=1, keepdims=True), 1.0)
@@ -253,6 +260,52 @@
             put(base + at, dot(ref[:, at : at + step], bp_ref[...], 0, 0))
 
 
+def fold_body(me_ref, *refs, terms, counts, together):
+    ins, outs = refs[: sum(terms)], refs[sum(terms) :]
+    for i, count in enumerate(counts):
+        held, ins = ins[: terms[i]], ins[terms[i] :]
+        depth = held[0].shape[0] // count
+        for k in range(count):
+            place = pl.ds(pl.multiple_of((me_ref[i] ^ k) * depth, 16), depth)
+            value = held[0][place, :].astype(F32)
+            for term in held[1:]:
+                value = value + term[place, :].astype(F32)
+            if together:
+                outs[k][i * depth : (i + 1) * depth, :] = value.astype(outs[k].dtype)
+            else:
+                outs[k][...] = value.astype(outs[k].dtype)
+        if not together:
+            outs = outs[count:]
+
+
+def fold(chains, counts, me, together):
+    width = chains[0][0].shape[1]
+    depths = [chain[0].shape[0] // count for chain, count in zip(chains, counts)]
+    if all(depth % 16 == 0 for depth in depths):
+        groups = [(sum(depths), counts[0])] if together else list(zip(depths, counts))
+        shapes = [
+            jax.ShapeDtypeStruct((depth, width), BF16 if k else F32)
+            for depth, count in groups
+            for k in range(count)
+        ]
+        out = iter(kernel_call(
+            functools.partial(
+                fold_body, terms=[len(c) for c in chains], counts=counts, together=together
+            ),
+            shapes,
+            smem=1,
+        )(jnp.stack(me), *[term for chain in chains for term in chain]))
+        return [[next(out) for _ in range(count)] for _, count in groups]
+    found = []
+    for chain, count, depth, at in zip(chains, counts, depths, me):
+        parts = [
+            total([lax.dynamic_slice_in_dim(t, (at ^ k) * depth, depth, 0) for t in chain])
+            for k in range(count)
+        ]
+        found.append([part.astype(BF16) if k else part for k, part in enumerate(parts)])
+    return [[jnp.concatenate(pair, 0) for pair in zip(*found)]] if together else found
+
+
 def finish_body(core_ref, *refs, cuts):
     (p, p_far, q, q_far), outs, held, sems = refs[:4], refs[4:8], refs[8:12], refs[12]
     quarter = p.shape[0]
@@ -294,15 +347,14 @@
         name, count = ("group", self.groups) if axis in "cy" else ("member", self.members)
         return lax.ppermute(array, name, [(i, i ^ (k * stride)) for i in range(count)])
 
-    def part(self, terms, axis, k):
-        depth = terms[0].shape[0] // self.size[axis]
-        place = (self.at[axis] ^ k) * depth
-        return [lax.dynamic_slice_in_dim(term, place, depth, 0) for term in terms]
-
-    def scatter(self, terms, axis):
-        others = range(1, self.size[axis])
-        got = [self.swap(total(self.part(terms, axis, k)).astype(BF16), axis, k) for k in others]
-        return self.part(terms, axis, 0) + got
+    def scatter(self, chains, axes, together=False):
+        out = fold(chains, [self.size[a] for a in axes], [self.at[a] for a in axes], together)
+        if together:
+            axes = axes[:1]
+        return [
+            [mine] + [self.swap(part, axis, k + 1) for k, part in enumerate(parts)]
+            for (mine, *parts), axis in zip(out, axes)
+        ]
 
     def gather(self, part, axis, dtype=BF16, parts=1):
         pieces = [part] + [self.swap(part, axis, k) for k in range(1, self.size[axis])]
@@ -355,7 +407,6 @@
             jax.ShapeDtypeStruct((owners, cap), I32),
             jax.ShapeDtypeStruct((1, misses), I32),
         ),
-        flops=2 * misses * misses * 128,
     )(miss_owner.reshape(1, -1), miss_row.reshape(1, -1))
     store_low = store.astype(BF16)
     asked = lax.all_to_all(
@@ -377,10 +428,13 @@
         found = {(k, 0): box.swap(part, "x", k) for k in range(1, nx)}
         return found | {(0, k): box.swap(part, "y", k) for k in range(1, ny)}
 
-    def corner(sides):
+    def corner(sides, way=0):
         found = {}
         for i in range(1, nx):
             for j in range(1, ny):
+                if way:
+                    found[i, j] = [box.swap(sides[i, 0], "y", j) if way == 1 else box.swap(sides[0, j], "x", i)]
+                    continue
                 upper, lower = jnp.split(sides[i, 0], 2)[0], jnp.split(sides[0, j], 2)[1]
                 found[i, j] = [box.swap(upper, "y", j), box.swap(lower, "x", i)]
         return found
@@ -398,20 +452,20 @@
         return kernel_call(
             functools.partial(cached_body, bases=bases),
             jax.ShapeDtypeStruct((hits, wide), BF16),
-            flops=2 * hits * wide * sum(piece.shape[0] for piece in pieces),
         )(code, *pieces)
 
+    far = [box.swap(mine, "z", k) for k in range(nz // 2, nz - 1)]
     near = lax.optimization_barrier(near)
     near_own = jnp.concatenate(near, 0)
     half = near_own.shape[0]
     near_side = side(near_own)
-    far = [box.swap(near[0], "z", k) for k in range(nz // 2, nz)]
+    far.append(box.swap(near[0], "z", nz - 1))
     asked, store_low, near_side = lax.optimization_barrier((asked, store_low, near_side))
     served = kernel_call(
         serve_body,
         jax.ShapeDtypeStruct((owners * cap, wide), BF16),
-        flops=2 * owners * cap * store.shape[0] * wide,
     )(asked, store_low)
+    near_corner = corner(near_side, 1)
     served, far, hot, names = lax.optimization_barrier((served, far, hot, names))
     miss_rows = lax.all_to_all(
         served.reshape(owners, cap, wide), BOTH, split_axis=0, concat_axis=0, tiled=True
@@ -427,28 +481,23 @@
             jax.ShapeDtypeStruct((seeds, fan_two), F32),
             jax.ShapeDtypeStruct((hits, 1), I32),
         ),
-        flops=8 * rows * misses * owners * cap,
     )(targets, names, slot, seed_mask.T, code, d_emb, w2_self, w2_nbr)
 
     far_own = jnp.concatenate(far, 0)
     far_side = side(far_own)
-    near_corner = corner(near_side)
     first = cached((0, {(0, 0): [near_own]}), (half, {(0, 0): [far_own]}))
     second = cached((0, {at: [piece] for at, piece in near_side.items()}))
-    far_side, near_corner, first, second = lax.optimization_barrier(
-        (far_side, near_corner, first, second)
-    )
-    far_corner = corner(far_side)
-    third = cached((half, {at: [piece] for at, piece in far_side.items()}), (0, near_corner))
-    far_corner, third = lax.optimization_barrier((far_corner, third))
-    fourth = cached((half, far_corner))
+    far_side, first, second = lax.optimization_barrier((far_side, first, second))
+    far_corner = corner(far_side, 2)
+    third = cached((half, {at: [piece] for at, piece in far_side.items()}))
+    near_corner, far_corner, third = lax.optimization_barrier((near_corner, far_corner, third))
+    fourth = cached((0, near_corner), (half, far_corner))
     own_part, near_part = kernel_call(
         share_body,
         (
             jax.ShapeDtypeStruct((rows, wide), BF16),
             jax.ShapeDtypeStruct((rows, wide), F32),
         ),
-        flops=4 * hits * wide * rows,
     )(sel_hit, first, second, third, fourth)
 
     hot, own_part, near_part = lax.optimization_barrier((hot, own_part, near_part))
@@ -460,15 +509,14 @@
         miss_rows, w1_self, w1_nbr, back, w2_self, w2_nbr, d_emb, sel_miss, own_part, near_part
     )
     turn = 256
-    emb, send, keep = pl.pallas_call(
+    emb, *sums = pl.pallas_call(
         functools.partial(step_body, scale=grad_scale, step=turn),
         out_shape=(
             jax.ShapeDtypeStruct((seeds, hid), BF16),
-            jax.ShapeDtypeStruct((total_rows // 2, hid), BF16),
-            jax.ShapeDtypeStruct((total_rows // 2, hid), F32),
+            *[jax.ShapeDtypeStruct((total_rows // 4, hid), kind) for kind in (BF16,) * 4],
         ),
         in_specs=[pl.BlockSpec(memory_space=pltpu.SMEM)] + [hbm] * 10 + [vmem] * 2,
-        out_specs=(vmem,) * 3,
+        out_specs=(vmem,) * 5,
         scratch_shapes=[pltpu.VMEM(array.shape, array.dtype) for array in streamed]
         + [
             pltpu.VMEM((rows, wide), BF16),
@@ -482,25 +530,17 @@
             flops=0, bytes_accessed=0, transcendentals=0
         ),
     )(box.at["c"].reshape(1), *streamed, count, flags)
-    send, far_hot = lax.optimization_barrier((send, far_hot))
-
-    sums = [keep, box.swap(send, "c", 1)]
-    p = [term[: total_rows // 4] for term in sums]
-    q = [term[total_rows // 4 :] for term in sums]
-    p, q = box.scatter(p, "x"), box.scatter(q, "y")
+    sums, far_hot = lax.optimization_barrier((sums, far_hot))
+
+    p, q = ([sums[2 + i], box.swap(sums[i], "c", 1)] for i in range(2))
+    p, q = box.scatter((p, q), ("x", "y"))
     near_hot = [box.swap(block, "c", 1) for block in far_hot]
     p, q, near_hot = lax.optimization_barrier((p, q, near_hot))
     pairs = [join(pair, box.at["c"], BF16)[0] for pair in zip(far_hot, near_hot)]
     (new_cache,) = join(pairs, box.at["y"], F32)
-    p, q = box.scatter(p, "y"), box.scatter(q, "x")
-    others = range(1, nz)
-    outgoing = [
-        jnp.concatenate([total(box.part(p, "z", k)), total(box.part(q, "z", k))], 0).astype(BF16)
-        for k in others
-    ]
-    summed = jnp.concatenate([total(box.part(p, "z", 0)), total(box.part(q, "z", 0))], 0)
-    incoming = [box.swap(outgoing[k - 1], "z", k) for k in others]
-    summed = total([summed] + incoming).astype(BF16)
+    p, q = box.scatter((p, q), ("y", "x"))
+    (summed,) = box.scatter((p, q), ("z", "z"), together=True)
+    summed = total(summed).astype(BF16)
     p, q = box.gather(summed, "z", parts=2)
     (p,), (q,) = lax.optimization_barrier((box.gather(p, "y"), box.gather(q, "x")))
     (p,), (q,) = lax.optimization_barrier((box.gather(p, "x"), box.gather(q, "y")))

time: 207 us -> 195 us (0.942)
  waiting for transfers between devices: 58.8 us -> 66.1 us
  other arithmetic: 11.4 us -> 5.03 us
  local copies, waits for them, and re-layouts: 27.4 us -> 21.3 us
  Pallas kernels: 57 us -> 54 us
  starting transfers between devices: 48.8 us -> 45.9 us
    ppermute x41 -> x38, waiting for transfers between devices: 58.8 us -> 66.1 us  [swap(): lax.ppermute(array, name, [(i, i ^ k * stride) for i in range(count)])]
    convert_element_type x5 -> x1, other arithmetic: 4.28 us -> 0.05 us  [on_device(): summed = total(summed).astype(BF16)]
    slice x2 -> x0, local copies, waits for them, and re-layouts: 3.66 us -> none  [on_device(): q = [term[total_rows // 4:] for term in sums]]
    all_to_all x1, starting transfers between devices: 7.64 us -> 4.04 us  [on_device(): lax.all_to_all(served.reshape(owners, cap, wide), BOTH, split_axis=0, con...]
    unnamed x66 -> x60, local copies, waits for them, and re-layouts: 15 us -> 18.5 us
    split x4 -> x0, local copies, waits for them, and re-layouts: 3.36 us -> none  [corner(): upper, lower = (jnp.split(sides[i, 0], 2)[0], jnp.split(sides[0, j], 2)[1])]
    ppermute x41 -> x38, starting transfers between devices: 36.3 us -> 39.1 us  [swap(): lax.ppermute(array, name, [(i, i ^ k * stride) for i in range(count)])]
    pallas_call x16 -> x19, Pallas kernels: 37.5 us -> 34.9 us  [call(): pl.pallas_call(body, out_shape=out_shape, in_specs=specs, out_specs=jax.t...]
  transfers between devices with their start and end apart: 43 -> 40, of which waited for: 25 -> 28; matrix products, arithmetic and copies ran while one was open for 11% -> 5% of each run, Pallas kernels for 26% -> 25%
where the time goes in v2:
time: 195 us; the launch traced here: 194 us
  waiting for transfers between devices  66.1 us (34%)
  Pallas kernels  54 us (28%)
  starting transfers between devices  45.9 us (24%)
  local copies, waits for them, and re-layouts  21.3 us (11%)
  other arithmetic  5.03 us (3%)
  between operations  1.98 us (1%)
    ppermute x38, waiting for transfers between devices, swap(): lax.ppermute(array, name, [(i, i ^ k * stride) for i in range(count)])  66.1 us
    ppermute x38, starting transfers between devices, swap(): lax.ppermute(array, name, [(i, i ^ k * stride) for i in range(count)])  39.1 us
    pallas_call x19, Pallas kernels, call(): pl.pallas_call(body, out_shape=out_shape, in_specs=specs, out_specs=jax.t...  34.9 us
    unnamed x60, local copies, waits for them, and re-layouts  18.5 us
    pallas_call x1, Pallas kernels, on_device(): pl.pallas_call(functools.partial(step_body, scale=grad_scale, step=turn),...  16.2 us
    all_to_all x1, starting transfers between devices, on_device(): lax.all_to_all(served.reshape(owners, cap, wide), BOTH, split_axis=0, con...  4.04 us
  transfers between devices with their start and end apart: 40, of which 28 were waited for; matrix products, arithmetic and copies ran while one was open for 5% of the time, Pallas kernels for 25%

profile of v2, /device:TPU:0, one launch (start us, length us, event | category | flops | bytes accessed | tf_op | source)
XLA Modules:
  0.0 194.4 jit_solution(5649065069631489178)
XLA Ops:
  2.3 3.1 %collective-permute-start = (bf16[128,1024]{1,0:T(8,128)(2,1)S(1)}, bf16[128,1024]{1,0:T(8,128)(2,1)S(1)}, u32[]{:S(2)}, u32[]{:S(2)}) collective-permute-start(bf16[128,1024]{1,0:T(8,128)(2,1)S(1)} %dynamic-slice_convert_fusion.1), channel_id=1, source_target_pairs={{0,2},{1,3},{2,0},{3,1},{4,6},{5,7},{6,4},{7,5},{8,10},{9,11},{10,... | collective-permute-start | bytes 786440 | tf_op jit(solution)/shard_map/ppermute | solution.py:348
  5.4 2.6 %collective-permute-start.3 = (bf16[128,1024]{1,0:T(8,128)(2,1)S(1)}, bf16[128,1024]{1,0:T(8,128)(2,1)}, u32[]{:S(2)}, u32[]{:S(2)}) collective-permute-start(bf16[128,1024]{1,0:T(8,128)(2,1)S(1)} %dynamic-slice_convert_fusion.1), channel_id=1, source_target_pairs={{0,4},{1,5},{2,6},{3,7},{4,0},{5,1},{6,2},{7,3},{8,12},{9,13},{10,... | collective-permute-start | bytes 786440 | tf_op jit(solution)/shard_map/ppermute | solution.py:348
  10.3 2.8 %all-to-all-start = ((s32[32,1,32]{2,1,0:T(1,128)}), s32[32,1,32]{2,1,0:T(1,128)S(1)}, u32[]{:S(2)}, u32[]{:S(2)}) async-start(s32[32,1,32]{2,1,0:T(1,128)} %bitcast.4), calls=%async_computation | async-start | bytes 32768 | tf_op jit(solution)/shard_map/all_to_all | solution.py:412
  13.1 4.1 %collective-permute-done = bf16[128,1024]{1,0:T(8,128)(2,1)S(1)} collective-permute-done((bf16[128,1024]{1,0:T(8,128)(2,1)S(1)}, bf16[128,1024]{1,0:T(8,128)(2,1)S(1)}, u32[]{:S(2)}, u32[]{:S(2)}) %collective-permute-start) | collective-permute-done | bytes 262176 | tf_op jit(solution)/shard_map/ppermute | solution.py:348
  21.4 2.6 %collective-permute-start.4 = (bf16[128,1024]{1,0:T(8,128)(2,1)S(1)}, bf16[128,1024]{1,0:T(8,128)(2,1)}, u32[]{:S(2)}, u32[]{:S(2)}) collective-permute-start(bf16[128,1024]{1,0:T(8,128)(2,1)S(1)} %dynamic-slice_convert_fusion.1), channel_id=1, source_target_pairs={{0,6},{1,7},{2,4},{3,5},{4,2},{5,3},{6,0},{7,1},{8,14},{9,15},{10,... | collective-permute-start | bytes 786440 | tf_op jit(solution)/shard_map/ppermute | solution.py:348
  31.8 2.6 %shard_map.218 = bf16[1024,1024]{1,0:T(8,128)(2,1)S(1)} custom-call(s32[32,32]{1,0:T(8,128)S(1)} %bitcast.22, bf16[1024,1024]{1,0:T(8,128)(2,1)S(1)} %convert_element_type.21.store_ref), custom_call_target="tpu_custom_call" | custom-call | tf_op jit(solution)/shard_map/pallas_call | solution.py:29
  35.8 4.0 %all-to-all-start.1 = ((bf16[32,32,1024]{2,1,0:T(8,128)(2,1)}), bf16[32,32,1024]{2,1,0:T(8,128)(2,1)}, u32[]{:S(2)}, u32[]{:S(2)}) async-start(bf16[32,32,1024]{2,1,0:T(8,128)(2,1)} %bitcast.21), calls=%async_computation.1 | async-start | bytes 4194304 | tf_op jit(solution)/shard_map/all_to_all | solution.py:470
  48.2 7.4 %shard_map.219 = (bf16[2,768,1024]{2,1,0:T(8,128)(2,1)S(1)}, bf16[2,768,1024]{2,1,0:T(8,128)(2,1)S(1)}, f32[768,1]{1,0:T(8,128)S(1)}, bf16[768,512]{1,0:T(8,128)...) custom-call(s32[6,128]{1,0:T(8,128)S(1)} %pad_add_fusion.1.targets_ref, s32[11,1024]{1,0:T(8,128)S(1)} %copy-done.20, ...), custom_call_target="tpu_custom_call" | custom-call | tf_op jit(solution)/shard_map/pallas_call | solution.py:29
  62.3 4.2 %shard_map.220.refs_0_ = bf16[1024,1024]{1,0:T(8,128)(2,1)S(1)} custom-call(s32[1024,1]{1,0:T(8,128)S(1)} %get-tuple-element.90.code_ref, bf16[256,1024]{1,0:T(8,128)(2,1)S(1)} %copy-done.10, bf16[256,1024]{1,0:T(8,128)(2,1)S(1)} %copy-done.16, bf16[256,1024]{1,0:T(8,128)(2,1)} %constant_dynamic-update-slice_fusion.2.refs_2_, bf16[256,1024]{1,0:T(8,128)(2,1)S(1)} %copy-done.18), custom_call_target="tpu_custom_call" | custom-call | tf_op jit(solution)/shard_map/pallas_call | solution.py:29
  66.5 4.6 %shard_map.221.refs_1_ = bf16[1024,1024]{1,0:T(8,128)(2,1)S(1)} custom-call(s32[1024,1]{1,0:T(8,128)S(1)} %get-tuple-element.90.code_ref, bf16[256,1024]{1,0:T(8,128)(2,1)} %collective-permute-done.1.refs_0_, bf16[256,1024]{1,0:T(8,128)(2,1)} %collective-permute-done.9.refs_1_, bf16[256,1024]{1,0:T(8,128)(2,1)} %collective-permute-done.2.refs_2_, ...), custom_call_target="tpu_custom_call" | custom-call | tf_op jit(solution)/shard_map/pallas_call | solution.py:29
  71.1 4.3 %collective-permute-done.5.refs_0_ = bf16[256,1024]{1,0:T(8,128)(2,1)} collective-permute-done((bf16[256,1024]{1,0:T(8,128)(2,1)}, bf16[256,1024]{1,0:T(8,128)(2,1)}, u32[]{:S(2)}, u32[]{:S(2)}) %collective-permute-start.5) | collective-permute-done | bytes 524320 | tf_op jit(solution)/shard_map/ppermute | solution.py:348
  78.3 4.3 %shard_map.222.refs_2_ = bf16[1024,1024]{1,0:T(8,128)(2,1)S(1)} custom-call(s32[1024,1]{1,0:T(8,128)S(1)} %get-tuple-element.90.code_ref, bf16[256,1024]{1,0:T(8,128)(2,1)} %collective-permute-done.5.refs_0_, bf16[256,1024]{1,0:T(8,128)(2,1)S(1)} %collective-permute-done.13.refs_1_, bf16[256,1024]{1,0:T(8,128)(2,1)} %collective-permute-done.6.refs_2_, ...), custom_call_target="tpu_custom_call" | custom-call | tf_op jit(solution)/shard_map/pallas_call | solution.py:29
  82.5 8.4 %collective-permute-done.11.refs_0_ = bf16[256,1024]{1,0:T(8,128)(2,1)S(1)} collective-permute-done((bf16[256,1024]{1,0:T(8,128)(2,1)}, bf16[256,1024]{1,0:T(8,128)(2,1)S(1)}, u32[]{:S(2)}, u32[]{:S(2)}) %collective-permute-start.11) | collective-permute-done | bytes 524320 | tf_op jit(solution)/shard_map/ppermute | solution.py:348
  95.6 3.3 %shard_map.223.refs_3_ = bf16[1024,1024]{1,0:T(8,128)(2,1)S(1)} custom-call(s32[1024,1]{1,0:T(8,128)S(1)} %get-tuple-element.90.code_ref, bf16[256,1024]{1,0:T(8,128)(2,1)S(1)} %collective-permute-done.11.refs_0_, bf16[256,1024]{1,0:T(8,128)(2,1)S(1)} %collective-permute-done.15.refs_1_, bf16[256,1024]{1,0:T(8,128)(2,1)S(1)} %collective-permute-done.12.refs_2_, ...), custom_call_target="tpu_custom_call" | custom-call | tf_op jit(solution)/shard_map/pallas_call | solution.py:29
  98.9 3.6 %shard_map.224 = (bf16[768,1024]{1,0:T(8,128)(2,1)S(1)}, f32[768,1024]{1,0:T(8,128)S(1)}) custom-call(bf16[2,768,1024]{2,1,0:T(8,128)(2,1)S(1)} %get-tuple-element.87.sel_ref, bf16[1024,1024]{1,0:T(8,128)(2,1)S(1)} %shard_map.220.refs_0_, bf16[1024,1024]{1,0:T(8,128)(2,1)S(1)} %shard_map.221.refs_1_, bf16[1024,1024]{1,0:T(8,128)(2,1)S(1)} %shard_map.222.refs_2_, ...), custom_call_target="tpu_custom_call" | custom-call | tf_op jit(solution)/shard_map/pallas_call | solution.py:29
  106.8 16.2 %shard_map.225 = (bf16[128,512]{1,0:T(8,128)(2,1)}, bf16[768,512]{1,0:T(8,128)(2,1)}, bf16[768,512]{1,0:T(8,128)(2,1)}, bf16[768,512]{1,0:T(8,128)(2,1)}, bf16[768,512]{1,0:T(8,128)(2,1)}) custom-call(s32[1]{0:T(128)} %bitcast.core_ref.me_ref, bf16[1024,1024]{1,0:T(8,128)(2,1)} %bitcast.10.refs_0_, bf16[1024,512]{1,0:T(8,128)(2,1)} %refs_1_.1, ...), custom_call_target="tpu_custom_call" | custom-call | tf_op jit(solution)/shard_map/pallas_call | solution.py:512
  134.9 6.9 %collective-permute-done.20.refs_1_ = bf16[384,512]{1,0:T(8,128)(2,1)S(1)} collective-permute-done((bf16[384,512]{1,0:T(8,128)(2,1)S(1)}, bf16[384,512]{1,0:T(8,128)(2,1)S(1)}, u32[]{:S(2)}, u32[]{:S(2)}) %collective-permute-start.20) | collective-permute-done | bytes 393248 | tf_op jit(solution)/shard_map/ppermute | solution.py:348
  145.0 4.7 %collective-permute-done.24.refs_1_ = bf16[192,512]{1,0:T(8,128)(2,1)S(1)} collective-permute-done((bf16[192,512]{1,0:T(8,128)(2,1)S(1)}, bf16[192,512]{1,0:T(8,128)(2,1)S(1)}, u32[]{:S(2)}, u32[]{:S(2)}) %collective-permute-start.24) | collective-permute-done | bytes 196640 | tf_op jit(solution)/shard_map/ppermute | solution.py:348
  150.9 3.2 %collective-permute-start.28 = (bf16[96,512]{1,0:T(8,128)(2,1)S(1)}, bf16[96,512]{1,0:T(8,128)(2,1)S(1)}, u32[]{:S(2)}, u32[]{:S(2)}) collective-permute-start(bf16[96,512]{1,0:T(8,128)(2,1)S(1)} %get-tuple-element.133), channel_id=1, source_target_pairs={{0,6},{1,7},{2,4},{3,5},{4,2},{5,3},{6,0},{7,1},{8,14},{9,15},{10,... | collective-permute-start | bytes 294920 | tf_op jit(solution)/shard_map/ppermute | solution.py:348
  155.3 3.0 %collective-permute-done.28 = bf16[96,512]{1,0:T(8,128)(2,1)S(1)} collective-permute-done((bf16[96,512]{1,0:T(8,128)(2,1)S(1)}, bf16[96,512]{1,0:T(8,128)(2,1)S(1)}, u32[]{:S(2)}, u32[]{:S(2)}) %collective-permute-start.28) | collective-permute-done | bytes 98336 | tf_op jit(solution)/shard_map/ppermute | solution.py:348
  165.3 5.1 %collective-permute-done.30.refs_2_ = bf16[96,512]{1,0:T(8,128)(2,1)S(1)} collective-permute-done((bf16[96,512]{1,0:T(8,128)(2,1)S(1)}, bf16[96,512]{1,0:T(8,128)(2,1)S(1)}, u32[]{:S(2)}, u32[]{:S(2)}) %collective-permute-start.30) | collective-permute-done | bytes 98336 | tf_op jit(solution)/shard_map/ppermute | solution.py:348
  173.1 3.1 %collective-permute-done.32.refs_1_ = bf16[192,512]{1,0:T(8,128)(2,1)S(1)} collective-permute-done((bf16[192,512]{1,0:T(8,128)(2,1)S(1)}, bf16[192,512]{1,0:T(8,128)(2,1)S(1)}, u32[]{:S(2)}, u32[]{:S(2)}) %collective-permute-start.32) | collective-permute-done | bytes 196640 | tf_op jit(solution)/shard_map/ppermute | solution.py:348
  180.6 5.2 %collective-permute-done.34.refs_1_ = bf16[384,512]{1,0:T(8,128)(2,1)S(1)} collective-permute-done((bf16[384,512]{1,0:T(8,128)(2,1)S(1)}, bf16[384,512]{1,0:T(8,128)(2,1)S(1)}, u32[]{:S(2)}, u32[]{:S(2)}) %collective-permute-start.34) | collective-permute-done | bytes 393248 | tf_op jit(solution)/shard_map/ppermute | solution.py:348
  191.3 2.8 %shard_map.234 = (f32[1024,512]{1,0:T(8,128)}, f32[1024,512]{1,0:T(8,128)}, f32[512,512]{1,0:T(8,128)}, f32[512,512]{1,0:T(8,128)}) custom-call(s32[1]{0:T(128)} %bitcast.core_ref.me_ref, bf16[768,512]{1,0:T(8,128)(2,1)S(1)} %shard_map.232.refs_0_, bf16[768,512]{1,0:T(8,128)(2,1)S(1)} %collective-permute-done.36.refs_1_, ...), custom_call_target="tpu_custom_call" | custom-call | tf_op jit(solution)/shard_map/pallas_call | solution.py:550
  (151 shorter events, 80.1 us)
Async XLA Ops:
  2.3 14.9 %collective-permute-start = (bf16[128,1024]{1,0:T(8,128)(2,1)S(1)}, bf16[128,1024]{1,0:T(8,128)(2,1)S(1)}, u32[]{:S(2)}, u32[]{:S(2)}) collective-permute-start(bf16[128,1024]{1,0:T(8,128)(2,1)S(1)} %dynamic-slice_convert_fusion.1), channel_id=1, source_target_pairs={{0,2},{1,3},{2,0},{3,1},{4,6},{5,7},{6,4},{7,5},{8,10},{9,11},{10,... | collective-permute-start | bytes 786440 | tf_op jit(solution)/shard_map/ppermute | solution.py:348
  5.4 30.4 %collective-permute-start.3 = (bf16[128,1024]{1,0:T(8,128)(2,1)S(1)}, bf16[128,1024]{1,0:T(8,128)(2,1)}, u32[]{:S(2)}, u32[]{:S(2)}) collective-permute-start(bf16[128,1024]{1,0:T(8,128)(2,1)S(1)} %dynamic-slice_convert_fusion.1), channel_id=1, source_target_pairs={{0,4},{1,5},{2,6},{3,7},{4,0},{5,1},{6,2},{7,3},{8,12},{9,13},{10,... | collective-permute-start | bytes 786440 | tf_op jit(solution)/shard_map/ppermute | solution.py:348
  10.3 19.3 %all-to-all-start = ((s32[32,1,32]{2,1,0:T(1,128)}), s32[32,1,32]{2,1,0:T(1,128)S(1)}, u32[]{:S(2)}, u32[]{:S(2)}) async-start(s32[32,1,32]{2,1,0:T(1,128)} %bitcast.4), calls=%async_computation | async-start | bytes 32768 | tf_op jit(solution)/shard_map/all_to_all | solution.py:412
  17.3 13.4 %collective-permute-start.1 = (bf16[256,1024]{1,0:T(8,128)(2,1)S(1)}, bf16[256,1024]{1,0:T(8,128)(2,1)}, u32[]{:S(2)}, u32[]{:S(2)}) collective-permute-start(bf16[256,1024]{1,0:T(8,128)(2,1)S(1)} %constant_dynamic-update-slice_fusion.refs_0_), channel_id=1, source_target_pairs={{0,16},{8,24},{16,0},{24,8},{1,17},{9,25},{17,1},{25,9},{2,18},{10... | collective-permute-start | bytes 1572872 | tf_op jit(solution)/shard_map/ppermute | solution.py:348
  19.0 12.7 %collective-permute-start.2 = (bf16[256,1024]{1,0:T(8,128)(2,1)S(1)}, bf16[256,1024]{1,0:T(8,128)(2,1)}, u32[]{:S(2)}, u32[]{:S(2)}) collective-permute-start(bf16[256,1024]{1,0:T(8,128)(2,1)S(1)} %constant_dynamic-update-slice_fusion.refs_0_), channel_id=1, source_target_pairs={{0,1},{1,0},{2,3},{3,2},{4,5},{5,4},{6,7},{7,6},{8,9},{9,8},{10,11... | collective-permute-start | bytes 1572872 | tf_op jit(solution)/shard_map/ppermute | solution.py:348
  21.4 14.3 %collective-permute-start.4 = (bf16[128,1024]{1,0:T(8,128)(2,1)S(1)}, bf16[128,1024]{1,0:T(8,128)(2,1)}, u32[]{:S(2)}, u32[]{:S(2)}) collective-permute-start(bf16[128,1024]{1,0:T(8,128)(2,1)S(1)} %dynamic-slice_convert_fusion.1), channel_id=1, source_target_pairs={{0,6},{1,7},{2,4},{3,5},{4,2},{5,3},{6,0},{7,1},{8,14},{9,15},{10,... | collective-permute-start | bytes 786440 | tf_op jit(solution)/shard_map/ppermute | solution.py:348
  35.8 70.9 %all-to-all-start.1 = ((bf16[32,32,1024]{2,1,0:T(8,128)(2,1)}), bf16[32,32,1024]{2,1,0:T(8,128)(2,1)}, u32[]{:S(2)}, u32[]{:S(2)}) async-start(bf16[32,32,1024]{2,1,0:T(8,128)(2,1)} %bitcast.21), calls=%async_computation.1 | async-start | bytes 4194304 | tf_op jit(solution)/shard_map/all_to_all | solution.py:470
  43.3 14.6 %collective-permute-start.8 = (bf16[256,1024]{1,0:T(8,128)(2,1)}, bf16[256,1024]{1,0:T(8,128)(2,1)S(1)}, u32[]{:S(2)}, u32[]{:S(2)}) collective-permute-start(bf16[256,1024]{1,0:T(8,128)(2,1)} %constant_dynamic-update-slice_fusion.2.refs_2_), channel_id=1, source_target_pairs={{0,8},{8,0},{16,24},{24,16},{1,9},{9,1},{17,25},{25,17},{2,10},{10... | collective-permute-start | bytes 1572872 | tf_op jit(solution)/shard_map/ppermute | solution.py:348
  43.8 22.6 %collective-permute-start.9 = (bf16[256,1024]{1,0:T(8,128)(2,1)}, bf16[256,1024]{1,0:T(8,128)(2,1)}, u32[]{:S(2)}, u32[]{:S(2)}) collective-permute-start(bf16[256,1024]{1,0:T(8,128)(2,1)} %collective-permute-done.1.refs_0_), channel_id=1, source_target_pairs={{0,8},{8,0},{16,24},{24,16},{1,9},{9,1},{17,25},{25,17},{2,10},{10... | collective-permute-start | bytes 1572872 | tf_op jit(solution)/shard_map/ppermute | solution.py:348
  43.8 22.6 %collective-permute-start.10 = (bf16[256,1024]{1,0:T(8,128)(2,1)}, bf16[256,1024]{1,0:T(8,128)(2,1)}, u32[]{:S(2)}, u32[]{:S(2)}) collective-permute-start(bf16[256,1024]{1,0:T(8,128)(2,1)} %collective-permute-done.2.refs_2_), channel_id=1, source_target_pairs={{0,8},{8,0},{16,24},{24,16},{1,9},{9,1},{17,25},{25,17},{2,10},{10... | collective-permute-start | bytes 1572872 | tf_op jit(solution)/shard_map/ppermute | solution.py:348
  44.3 31.0 %collective-permute-start.5 = (bf16[256,1024]{1,0:T(8,128)(2,1)}, bf16[256,1024]{1,0:T(8,128)(2,1)}, u32[]{:S(2)}, u32[]{:S(2)}) collective-permute-start(bf16[256,1024]{1,0:T(8,128)(2,1)} %constant_dynamic-update-slice_fusion.2.refs_2_), channel_id=1, source_target_pairs={{0,16},{8,24},{16,0},{24,8},{1,17},{9,25},{17,1},{25,9},{2,18},{10... | collective-permute-start | bytes 1572872 | tf_op jit(solution)/shard_map/ppermute | solution.py:348
  46.7 28.7 %collective-permute-start.6 = (bf16[256,1024]{1,0:T(8,128)(2,1)}, bf16[256,1024]{1,0:T(8,128)(2,1)}, u32[]{:S(2)}, u32[]{:S(2)}) collective-permute-start(bf16[256,1024]{1,0:T(8,128)(2,1)} %constant_dynamic-update-slice_fusion.2.refs_2_), channel_id=1, source_target_pairs={{0,1},{1,0},{2,3},{3,2},{4,5},{5,4},{6,7},{7,6},{8,9},{9,8},{10,11... | collective-permute-start | bytes 1572872 | tf_op jit(solution)/shard_map/ppermute | solution.py:348
  75.9 15.1 %collective-permute-start.11 = (bf16[256,1024]{1,0:T(8,128)(2,1)}, bf16[256,1024]{1,0:T(8,128)(2,1)S(1)}, u32[]{:S(2)}, u32[]{:S(2)}) collective-permute-start(bf16[256,1024]{1,0:T(8,128)(2,1)} %collective-permute-done.2.refs_2_), channel_id=1, source_target_pairs={{0,16},{8,24},{16,0},{24,8},{1,17},{9,25},{17,1},{25,9},{2,18},{10... | collective-permute-start | bytes 1572872 | tf_op jit(solution)/shard_map/ppermute | solution.py:348
  77.1 15.9 %collective-permute-start.12 = (bf16[256,1024]{1,0:T(8,128)(2,1)}, bf16[256,1024]{1,0:T(8,128)(2,1)S(1)}, u32[]{:S(2)}, u32[]{:S(2)}) collective-permute-start(bf16[256,1024]{1,0:T(8,128)(2,1)} %collective-permute-done.5.refs_0_), channel_id=1, source_target_pairs={{0,1},{1,0},{2,3},{3,2},{4,5},{5,4},{6,7},{7,6},{8,9},{9,8},{10,11... | collective-permute-start | bytes 1572872 | tf_op jit(solution)/shard_map/ppermute | solution.py:348
  105.4 17.6 %collective-permute-start.17 = (bf16[128,1024]{1,0:T(8,128)(2,1)S(1)}, bf16[128,1024]{1,0:T(8,128)(2,1)S(1)}, u32[]{:S(2)}, u32[]{:S(2)}) collective-permute-start(bf16[128,1024]{1,0:T(8,128)(2,1)S(1)} %dynamic-slice_convert_fusion.refs_0_), channel_id=1, source_target_pairs={{0,16},{8,24},{16,0},{24,8},{1,17},{9,25},{17,1},{25,9},{2,18},{10... | collective-permute-start | bytes 786440 | tf_op jit(solution)/shard_map/ppermute | solution.py:348
  129.9 11.9 %collective-permute-start.20 = (bf16[384,512]{1,0:T(8,128)(2,1)S(1)}, bf16[384,512]{1,0:T(8,128)(2,1)S(1)}, u32[]{:S(2)}, u32[]{:S(2)}) collective-permute-start(bf16[384,512]{1,0:T(8,128)(2,1)S(1)} %get-tuple-element.117), channel_id=1, source_target_pairs={{0,1},{1,0},{2,3},{3,2},{4,5},{5,4},{6,7},{7,6},{8,9},{9,8},{10,11... | collective-permute-start | bytes 1179656 | tf_op jit(solution)/shard_map/ppermute | solution.py:348
  132.3 10.9 %collective-permute-start.21 = (bf16[384,512]{1,0:T(8,128)(2,1)S(1)}, bf16[384,512]{1,0:T(8,128)(2,1)S(1)}, u32[]{:S(2)}, u32[]{:S(2)}) collective-permute-start(bf16[384,512]{1,0:T(8,128)(2,1)S(1)} %get-tuple-element.119), channel_id=1, source_target_pairs={{0,16},{8,24},{16,0},{24,8},{1,17},{9,25},{17,1},{25,9},{2,18},{10... | collective-permute-start | bytes 1179656 | tf_op jit(solution)/shard_map/ppermute | solution.py:348
  150.9 7.5 %collective-permute-start.28 = (bf16[96,512]{1,0:T(8,128)(2,1)S(1)}, bf16[96,512]{1,0:T(8,128)(2,1)S(1)}, u32[]{:S(2)}, u32[]{:S(2)}) collective-permute-start(bf16[96,512]{1,0:T(8,128)(2,1)S(1)} %get-tuple-element.133), channel_id=1, source_target_pairs={{0,6},{1,7},{2,4},{3,5},{4,2},{5,3},{6,0},{7,1},{8,14},{9,15},{10,... | collective-permute-start | bytes 294920 | tf_op jit(solution)/shard_map/ppermute | solution.py:348
  154.1 6.4 %collective-permute-start.27 = (bf16[96,512]{1,0:T(8,128)(2,1)S(1)}, bf16[96,512]{1,0:T(8,128)(2,1)S(1)}, u32[]{:S(2)}, u32[]{:S(2)}) collective-permute-start(bf16[96,512]{1,0:T(8,128)(2,1)S(1)} %get-tuple-element.132), channel_id=1, source_target_pairs={{0,4},{1,5},{2,6},{3,7},{4,0},{5,1},{6,2},{7,3},{8,12},{9,13},{10,... | collective-permute-start | bytes 294920 | tf_op jit(solution)/shard_map/ppermute | solution.py:348
  161.1 9.3 %collective-permute-start.30 = (bf16[96,512]{1,0:T(8,128)(2,1)S(1)}, bf16[96,512]{1,0:T(8,128)(2,1)S(1)}, u32[]{:S(2)}, u32[]{:S(2)}) collective-permute-start(bf16[96,512]{1,0:T(8,128)(2,1)S(1)} %add_convert_fusion.refs_0_), channel_id=1, source_target_pairs={{0,4},{1,5},{2,6},{3,7},{4,0},{5,1},{6,2},{7,3},{8,12},{9,13},{10,... | collective-permute-start | bytes 294920 | tf_op jit(solution)/shard_map/ppermute | solution.py:348
  163.2 7.2 %collective-permute-start.31 = (bf16[96,512]{1,0:T(8,128)(2,1)S(1)}, bf16[96,512]{1,0:T(8,128)(2,1)S(1)}, u32[]{:S(2)}, u32[]{:S(2)}) collective-permute-start(bf16[96,512]{1,0:T(8,128)(2,1)S(1)} %add_convert_fusion.refs_0_), channel_id=1, source_target_pairs={{0,6},{1,7},{2,4},{3,5},{4,2},{5,3},{6,0},{7,1},{8,14},{9,15},{10,... | collective-permute-start | bytes 294920 | tf_op jit(solution)/shard_map/ppermute | solution.py:348
  171.2 6.7 %collective-permute-start.33 = (bf16[192,512]{1,0:T(8,128)(2,1)S(1)}, bf16[192,512]{1,0:T(8,128)(2,1)S(1)}, u32[]{:S(2)}, u32[]{:S(2)}) collective-permute-start(bf16[192,512]{1,0:T(8,128)(2,1)S(1)} %get-tuple-element.135.refs_0_), channel_id=1, source_target_pairs={{0,1},{1,0},{2,3},{3,2},{4,5},{5,4},{6,7},{7,6},{8,9},{9,8},{10,11... | collective-permute-start | bytes 589832 | tf_op jit(solution)/shard_map/ppermute | solution.py:348
  177.9 7.8 %collective-permute-start.34 = (bf16[384,512]{1,0:T(8,128)(2,1)S(1)}, bf16[384,512]{1,0:T(8,128)(2,1)S(1)}, u32[]{:S(2)}, u32[]{:S(2)}) collective-permute-start(bf16[384,512]{1,0:T(8,128)(2,1)S(1)} %shard_map.230.refs_0_), channel_id=1, source_target_pairs={{0,1},{1,0},{2,3},{3,2},{4,5},{5,4},{6,7},{7,6},{8,9},{9,8},{10,11... | collective-permute-start | bytes 1179656 | tf_op jit(solution)/shard_map/ppermute | solution.py:348
  180.0 7.8 %collective-permute-start.35 = (bf16[384,512]{1,0:T(8,128)(2,1)S(1)}, bf16[384,512]{1,0:T(8,128)(2,1)S(1)}, u32[]{:S(2)}, u32[]{:S(2)}) collective-permute-start(bf16[384,512]{1,0:T(8,128)(2,1)S(1)} %shard_map.231.refs_0_), channel_id=1, source_target_pairs={{0,16},{8,24},{16,0},{24,8},{1,17},{9,25},{17,1},{25,9},{2,18},{10... | collective-permute-start | bytes 1179656 | tf_op jit(solution)/shard_map/ppermute | solution.py:348
  (45 other events, 218.2 us)

commit v3 on v2

--- a/solution.py
+++ b/solution.py
@@ -121,15 +121,23 @@
 def cached_body(code_ref, *refs, bases):
     pieces, held_ref = refs[:-1], refs[-1]
     step = 256
+    groups, depth = [], step
+    for i, piece in enumerate(pieces):
+        if depth + piece.shape[0] > step:
+            groups, depth = groups + [[]], 0
+        groups[-1].append(i)
+        depth += piece.shape[0]
 
     @pl.loop(0, code_ref.shape[0] // step)
     def _(turn):
         cut = pl.ds(pl.multiple_of(turn * step, step), step)
         total = None
-        for piece, base in zip(pieces, bases):
-            lane = iota((step, piece.shape[0]), 1) + base
+        for group in groups:
+            lanes = [iota((step, pieces[i].shape[0]), 1) + bases[i] for i in group]
+            lane = lanes[0] if len(group) == 1 else jnp.concatenate(lanes, 1)
+            rows = [pieces[i][...] for i in group]
             pick = (code_ref[cut, :] == lane).astype(F32).astype(BF16)
-            part = dot(pick, piece[...])
+            part = dot(pick, rows[0] if len(group) == 1 else jnp.concatenate(rows, 0))
             total = part if total is None else total + part
         held_ref[cut, :] = total.astype(BF16)
 
@@ -399,7 +407,11 @@
 
     share = cache.shape[0] // box.groups
     group = lax.axis_index("group")
-    mine = lax.dynamic_slice_in_dim(cache, group * share, share, 0).astype(BF16)
+
+    def cast_share(number):
+        return lax.dynamic_slice_in_dim(cache, number * share, share, 0).astype(BF16)
+
+    mine = cast_share(group)
 
     ids, slot = kernel_call(
         request_body,
@@ -412,7 +424,7 @@
     asked = lax.all_to_all(
         ids.reshape(owners, 1, cap), BOTH, split_axis=0, concat_axis=0, tiled=True
     ).reshape(owners, cap)
-    near = [mine] + [box.swap(mine, "z", k) for k in range(1, nz // 2)]
+    near = [box.swap(mine, "z", k) for k in range(1, nz // 2)]
 
     targets = jnp.concatenate([seed_self[None, :], seed_nbr.T], 0)
     names = jnp.concatenate([tgt_self[None, :] + 1, jnp.where(tgt_mask > 0, tgt_nbr + 1, 0).T], 0)
@@ -444,7 +456,7 @@
         for first, batch in batches:
             for (i, j), held in batch.items():
                 start = first
-                for piece in held:
+                for piece in held if isinstance(held, list) else [held]:
                     for k in range(2):
                         pieces.append(piece if k == 0 else box.swap(piece, "c", 1))
                         bases.append(((k * ny + j) * nx + i) * nz * share + start)
@@ -455,12 +467,17 @@
         )(code, *pieces)
 
     far = [box.swap(mine, "z", k) for k in range(nz // 2, nz - 1)]
-    near = lax.optimization_barrier(near)
-    near_own = jnp.concatenate(near, 0)
-    half = near_own.shape[0]
+    home = {(0, k): cast_share(group ^ (2 * k)) for k in range(1, ny)}
+    home[0, 0] = mine
+    beside = {(i, k): box.swap(home[0, k], "x", i) for i in range(1, nx) for k in range(ny)}
+    near, last = lax.optimization_barrier((near, mine))
+    near_own = near[0] if len(near) == 1 else jnp.concatenate(near, 0)
+    half = share + near_own.shape[0]
     near_side = side(near_own)
-    far.append(box.swap(near[0], "z", nz - 1))
-    asked, store_low, near_side = lax.optimization_barrier((asked, store_low, near_side))
+    far.append(box.swap(last, "z", nz - 1))
+    asked, store_low, near_side, beside = lax.optimization_barrier(
+        (asked, store_low, near_side, beside)
+    )
     served = kernel_call(
         serve_body,
         jax.ShapeDtypeStruct((owners * cap, wide), BF16),
@@ -485,13 +502,15 @@
 
     far_own = jnp.concatenate(far, 0)
     far_side = side(far_own)
-    first = cached((0, {(0, 0): [near_own]}), (half, {(0, 0): [far_own]}))
-    second = cached((0, {at: [piece] for at, piece in near_side.items()}))
-    far_side, first, second = lax.optimization_barrier((far_side, first, second))
-    far_corner = corner(far_side, 2)
-    third = cached((half, {at: [piece] for at, piece in far_side.items()}))
-    near_corner, far_corner, third = lax.optimization_barrier((near_corner, far_corner, third))
-    fourth = cached((0, near_corner), (half, far_corner))
+    first = cached((0, home), (share, {(0, 0): near_own}), (half, {(0, 0): far_own}))
+    second = cached((0, beside), (share, near_side))
+    far_side, near_corner, first, second = lax.optimization_barrier(
+        (far_side, near_corner, first, second)
+    )
+    far_corner = corner(far_side)
+    third = cached((half, far_side))
+    far_corner, third = lax.optimization_barrier((far_corner, third))
+    fourth = cached((share, near_corner), (half, far_corner))
     own_part, near_part = kernel_call(
         share_body,
         (

time: 195 us -> 192 us (0.985)
  waiting for transfers between devices: 66.1 us -> 55.3 us
  starting transfers between devices: 45.9 us -> 50.4 us
  local copies, waits for them, and re-layouts: 21.3 us -> 23.6 us
    ppermute x38 -> x46, waiting for transfers between devices: 66.1 us -> 55.2 us  [swap(): lax.ppermute(array, name, [(i, i ^ k * stride) for i in range(count)])]
    ppermute x38 -> x46, starting transfers between devices: 39.1 us -> 41.7 us  [swap(): lax.ppermute(array, name, [(i, i ^ k * stride) for i in range(count)])]
    all_to_all x1, starting transfers between devices: 4.04 us -> 6.1 us  [on_device(): lax.all_to_all(served.reshape(owners, cap, wide), BOTH, split_axis=0, con...]
    unnamed x60 -> x67, local copies, waits for them, and re-layouts: 18.5 us -> 20.3 us
  transfers between devices with their start and end apart: 40 -> 48, of which waited for: 28 -> 26; matrix products, arithmetic and copies ran while one was open for 5% -> 5% of each run, Pallas kernels for 25% -> 25%
where the time goes in v3:
time: 192 us; the launch traced here: 191 us
  waiting for transfers between devices  55.3 us (29%)
  Pallas kernels  53.4 us (28%)
  starting transfers between devices  50.4 us (26%)
  local copies, waits for them, and re-layouts  23.6 us (12%)
  other arithmetic  6.41 us (3%)
  between operations  2.01 us (1%)
    ppermute x46, waiting for transfers between devices, swap(): lax.ppermute(array, name, [(i, i ^ k * stride) for i in range(count)])  55.2 us
    ppermute x46, starting transfers between devices, swap(): lax.ppermute(array, name, [(i, i ^ k * stride) for i in range(count)])  41.7 us
    pallas_call x19, Pallas kernels, call(): pl.pallas_call(body, out_shape=out_shape, in_specs=specs, out_specs=jax.t...  34.4 us
    unnamed x67, local copies, waits for them, and re-layouts  20.3 us
    pallas_call x1, Pallas kernels, on_device(): pl.pallas_call(functools.partial(step_body, scale=grad_scale, step=turn),...  16.2 us
    all_to_all x1, starting transfers between devices, on_device(): lax.all_to_all(served.reshape(owners, cap, wide), BOTH, split_axis=0, con...  6.1 us
  transfers between devices with their start and end apart: 48, of which 26 were waited for; matrix products, arithmetic and copies ran while one was open for 5% of the time, Pallas kernels for 25%

profile of v3, /device:TPU:0, one launch (start us, length us, event | category | flops | bytes accessed | tf_op | source)
XLA Modules:
  0.0 191.1 jit_solution(13126816153289283116)
XLA Ops:
  1.9 3.1 %collective-permute-start = (bf16[128,1024]{1,0:T(8,128)(2,1)S(1)}, bf16[128,1024]{1,0:T(8,128)(2,1)S(1)}, u32[]{:S(2)}, u32[]{:S(2)}) collective-permute-start(bf16[128,1024]{1,0:T(8,128)(2,1)S(1)} %get-tuple-element.83.refs_2_), channel_id=1, source_target_pairs={{0,2},{1,3},{2,0},{3,1},{4,6},{5,7},{6,4},{7,5},{8,10},{9,11},{10,... | collective-permute-start | bytes 786440 | tf_op jit(solution)/shard_map/ppermute | solution.py:356
  6.5 2.6 %collective-permute-start.5 = (bf16[128,1024]{1,0:T(8,128)(2,1)S(1)}, bf16[128,1024]{1,0:T(8,128)(2,1)}, u32[]{:S(2)}, u32[]{:S(2)}) collective-permute-start(bf16[128,1024]{1,0:T(8,128)(2,1)S(1)} %get-tuple-element.83.refs_2_), channel_id=1, source_target_pairs={{0,4},{1,5},{2,6},{3,7},{4,0},{5,1},{6,2},{7,3},{8,12},{9,13},{10,... | collective-permute-start | bytes 786440 | tf_op jit(solution)/shard_map/ppermute | solution.py:356
  11.4 2.5 %all-to-all-start = ((s32[32,1,32]{2,1,0:T(1,128)}), s32[32,1,32]{2,1,0:T(1,128)S(1)}, u32[]{:S(2)}, u32[]{:S(2)}) async-start(s32[32,1,32]{2,1,0:T(1,128)} %bitcast.4), calls=%async_computation | async-start | bytes 32768 | tf_op jit(solution)/shard_map/all_to_all | solution.py:424
  28.1 2.6 %shard_map.218 = bf16[1024,1024]{1,0:T(8,128)(2,1)S(1)} custom-call(s32[32,32]{1,0:T(8,128)S(1)} %bitcast.22, bf16[1024,1024]{1,0:T(8,128)(2,1)S(1)} %convert_element_type.24.store_ref), custom_call_target="tpu_custom_call" | custom-call | tf_op jit(solution)/shard_map/pallas_call | solution.py:29
  32.2 6.1 %all-to-all-start.1 = ((bf16[32,32,1024]{2,1,0:T(8,128)(2,1)}), bf16[32,32,1024]{2,1,0:T(8,128)(2,1)}, u32[]{:S(2)}, u32[]{:S(2)}) async-start(bf16[32,32,1024]{2,1,0:T(8,128)(2,1)} %bitcast.21), calls=%async_computation.1 | async-start | bytes 4194304 | tf_op jit(solution)/shard_map/all_to_all | solution.py:487
  51.5 7.4 %shard_map.219 = (bf16[2,768,1024]{2,1,0:T(8,128)(2,1)S(1)}, bf16[2,768,1024]{2,1,0:T(8,128)(2,1)S(1)}, f32[768,1]{1,0:T(8,128)S(1)}, bf16[768,512]{1,0:T(8,128)...) custom-call(s32[6,128]{1,0:T(8,128)S(1)} %pad_add_fusion.1.targets_ref, s32[11,1024]{1,0:T(8,128)S(1)} %copy-done.27, ...), custom_call_target="tpu_custom_call" | custom-call | tf_op jit(solution)/shard_map/pallas_call | solution.py:29
  66.1 4.3 %shard_map.221.refs_1_ = bf16[1024,1024]{1,0:T(8,128)(2,1)S(1)} custom-call(s32[1024,1]{1,0:T(8,128)S(1)} %get-tuple-element.94.code_ref, bf16[128,1024]{1,0:T(8,128)(2,1)} %collective-permute-done.3.refs_0_, bf16[128,1024]{1,0:T(8,128)(2,1)S(1)} %copy-done.20, bf16[128,1024]{1,0:T(8,128)(2,1)} %collective-permute-done.4.refs_2_, ...), custom_call_target="tpu_custom_call" | custom-call | tf_op jit(solution)/shard_map/pallas_call | solution.py:29
  70.5 4.8 %shard_map.220.refs_0_ = bf16[1024,1024]{1,0:T(8,128)(2,1)S(1)} custom-call(s32[1024,1]{1,0:T(8,128)S(1)} %get-tuple-element.94.code_ref, bf16[128,1024]{1,0:T(8,128)(2,1)S(1)} %get-tuple-element.152.refs_0_, bf16[128,1024]{1,0:T(8,128)(2,1)S(1)} %copy-done.16, bf16[128,1024]{1,0:T(8,128)(2,1)S(1)} %get-tuple-element.83.refs_2_, ...), custom_call_target="tpu_custom_call" | custom-call | tf_op jit(solution)/shard_map/pallas_call | solution.py:29
  75.2 4.5 %collective-permute-done.9.refs_0_ = bf16[128,1024]{1,0:T(8,128)(2,1)} collective-permute-done((bf16[128,1024]{1,0:T(8,128)(2,1)}, bf16[128,1024]{1,0:T(8,128)(2,1)}, u32[]{:S(2)}, u32[]{:S(2)}) %collective-permute-start.9) | collective-permute-done | bytes 262176 | tf_op jit(solution)/shard_map/ppermute | solution.py:356
  82.4 3.1 %shard_map.222.refs_2_ = bf16[1024,1024]{1,0:T(8,128)(2,1)S(1)} custom-call(s32[1024,1]{1,0:T(8,128)S(1)} %get-tuple-element.94.code_ref, bf16[256,1024]{1,0:T(8,128)(2,1)S(1)} %collective-permute-done.7.refs_0_, bf16[256,1024]{1,0:T(8,128)(2,1)S(1)} %collective-permute-done.20.refs_1_, bf16[256,1024]{1,0:T(8,128)(2,1)S(1)} %collective-permute-done.8.refs_2_, ...), custom_call_target="tpu_custom_call" | custom-call | tf_op jit(solution)/shard_map/pallas_call | solution.py:29
  85.4 3.9 %collective-permute-done.18.refs_2_ = bf16[128,1024]{1,0:T(8,128)(2,1)S(1)} collective-permute-done((bf16[128,1024]{1,0:T(8,128)(2,1)S(1)}, bf16[128,1024]{1,0:T(8,128)(2,1)S(1)}, u32[]{:S(2)}, u32[]{:S(2)}) %collective-permute-start.18) | collective-permute-done | bytes 262176 | tf_op jit(solution)/shard_map/ppermute | solution.py:356
  92.0 3.7 %shard_map.223.refs_3_ = bf16[1024,1024]{1,0:T(8,128)(2,1)S(1)} custom-call(s32[1024,1]{1,0:T(8,128)S(1)} %get-tuple-element.94.code_ref, bf16[128,1024]{1,0:T(8,128)(2,1)} %collective-permute-done.9.refs_0_, bf16[128,1024]{1,0:T(8,128)(2,1)S(1)} %collective-permute-done.22.refs_1_, bf16[128,1024]{1,0:T(8,128)(2,1)S(1)} %collective-permute-done.18.refs_2_, ...), custom_call_target="tpu_custom_call" | custom-call | tf_op jit(solution)/shard_map/pallas_call | solution.py:29
  95.7 3.7 %shard_map.224 = (bf16[768,1024]{1,0:T(8,128)(2,1)S(1)}, f32[768,1024]{1,0:T(8,128)S(1)}) custom-call(bf16[2,768,1024]{2,1,0:T(8,128)(2,1)S(1)} %get-tuple-element.90.sel_ref, bf16[1024,1024]{1,0:T(8,128)(2,1)S(1)} %shard_map.220.refs_0_, bf16[1024,1024]{1,0:T(8,128)(2,1)S(1)} %shard_map.221.refs_1_, bf16[1024,1024]{1,0:T(8,128)(2,1)S(1)} %shard_map.222.refs_2_, ...), custom_call_target="tpu_custom_call" | custom-call | tf_op jit(solution)/shard_map/pallas_call | solution.py:29
  103.9 16.2 %shard_map.225 = (bf16[128,512]{1,0:T(8,128)(2,1)}, bf16[768,512]{1,0:T(8,128)(2,1)}, bf16[768,512]{1,0:T(8,128)(2,1)}, bf16[768,512]{1,0:T(8,128)(2,1)}, bf16[768,512]{1,0:T(8,128)(2,1)}) custom-call(s32[1]{0:T(128)} %bitcast.core_ref.me_ref, bf16[1024,1024]{1,0:T(8,128)(2,1)} %bitcast.10.refs_0_, bf16[1024,512]{1,0:T(8,128)(2,1)} %refs_1_.1, ...), custom_call_target="tpu_custom_call" | custom-call | tf_op jit(solution)/shard_map/pallas_call | solution.py:531
  131.5 7.0 %collective-permute-done.28.refs_1_ = bf16[384,512]{1,0:T(8,128)(2,1)S(1)} collective-permute-done((bf16[384,512]{1,0:T(8,128)(2,1)S(1)}, bf16[384,512]{1,0:T(8,128)(2,1)S(1)}, u32[]{:S(2)}, u32[]{:S(2)}) %collective-permute-start.28) | collective-permute-done | bytes 393248 | tf_op jit(solution)/shard_map/ppermute | solution.py:356
  141.7 4.9 %collective-permute-done.32.refs_1_ = bf16[192,512]{1,0:T(8,128)(2,1)S(1)} collective-permute-done((bf16[192,512]{1,0:T(8,128)(2,1)S(1)}, bf16[192,512]{1,0:T(8,128)(2,1)S(1)}, u32[]{:S(2)}, u32[]{:S(2)}) %collective-permute-start.32) | collective-permute-done | bytes 196640 | tf_op jit(solution)/shard_map/ppermute | solution.py:356
  147.5 3.2 %collective-permute-start.36 = (bf16[96,512]{1,0:T(8,128)(2,1)S(1)}, bf16[96,512]{1,0:T(8,128)(2,1)S(1)}, u32[]{:S(2)}, u32[]{:S(2)}) collective-permute-start(bf16[96,512]{1,0:T(8,128)(2,1)S(1)} %get-tuple-element.139), channel_id=1, source_target_pairs={{0,6},{1,7},{2,4},{3,5},{4,2},{5,3},{6,0},{7,1},{8,14},{9,15},{10,... | collective-permute-start | bytes 294920 | tf_op jit(solution)/shard_map/ppermute | solution.py:356
  152.0 2.8 %collective-permute-done.36 = bf16[96,512]{1,0:T(8,128)(2,1)S(1)} collective-permute-done((bf16[96,512]{1,0:T(8,128)(2,1)S(1)}, bf16[96,512]{1,0:T(8,128)(2,1)S(1)}, u32[]{:S(2)}, u32[]{:S(2)}) %collective-permute-start.36) | collective-permute-done | bytes 98336 | tf_op jit(solution)/shard_map/ppermute | solution.py:356
  158.0 2.6 %collective-permute-start.38 = (bf16[96,512]{1,0:T(8,128)(2,1)S(1)}, bf16[96,512]{1,0:T(8,128)(2,1)S(1)}, u32[]{:S(2)}, u32[]{:S(2)}) collective-permute-start(bf16[96,512]{1,0:T(8,128)(2,1)S(1)} %add_convert_fusion.refs_0_), channel_id=1, source_target_pairs={{0,4},{1,5},{2,6},{3,7},{4,0},{5,1},{6,2},{7,3},{8,12},{9,13},{10,... | collective-permute-start | bytes 294920 | tf_op jit(solution)/shard_map/ppermute | solution.py:356
  162.2 5.2 %collective-permute-done.38.refs_2_ = bf16[96,512]{1,0:T(8,128)(2,1)S(1)} collective-permute-done((bf16[96,512]{1,0:T(8,128)(2,1)S(1)}, bf16[96,512]{1,0:T(8,128)(2,1)S(1)}, u32[]{:S(2)}, u32[]{:S(2)}) %collective-permute-start.38) | collective-permute-done | bytes 98336 | tf_op jit(solution)/shard_map/ppermute | solution.py:356
  170.3 2.8 %collective-permute-done.40.refs_1_ = bf16[192,512]{1,0:T(8,128)(2,1)S(1)} collective-permute-done((bf16[192,512]{1,0:T(8,128)(2,1)S(1)}, bf16[192,512]{1,0:T(8,128)(2,1)S(1)}, u32[]{:S(2)}, u32[]{:S(2)}) %collective-permute-start.40) | collective-permute-done | bytes 196640 | tf_op jit(solution)/shard_map/ppermute | solution.py:356
  173.2 2.7 %collective-permute-done.41.refs_1_ = bf16[192,512]{1,0:T(8,128)(2,1)S(1)} collective-permute-done((bf16[192,512]{1,0:T(8,128)(2,1)S(1)}, bf16[192,512]{1,0:T(8,128)(2,1)S(1)}, u32[]{:S(2)}, u32[]{:S(2)}) %collective-permute-start.41) | collective-permute-done | bytes 196640 | tf_op jit(solution)/shard_map/ppermute | solution.py:356
  177.7 6.2 %collective-permute-done.42.refs_1_ = bf16[384,512]{1,0:T(8,128)(2,1)S(1)} collective-permute-done((bf16[384,512]{1,0:T(8,128)(2,1)S(1)}, bf16[384,512]{1,0:T(8,128)(2,1)S(1)}, u32[]{:S(2)}, u32[]{:S(2)}) %collective-permute-start.42) | collective-permute-done | bytes 393248 | tf_op jit(solution)/shard_map/ppermute | solution.py:356
  188.1 2.8 %shard_map.234 = (f32[1024,512]{1,0:T(8,128)}, f32[1024,512]{1,0:T(8,128)}, f32[512,512]{1,0:T(8,128)}, f32[512,512]{1,0:T(8,128)}) custom-call(s32[1]{0:T(128)} %bitcast.core_ref.me_ref, bf16[768,512]{1,0:T(8,128)(2,1)S(1)} %shard_map.232.refs_0_, bf16[768,512]{1,0:T(8,128)(2,1)S(1)} %collective-permute-done.44.refs_1_, ...), custom_call_target="tpu_custom_call" | custom-call | tf_op jit(solution)/shard_map/pallas_call | solution.py:569
  (175 shorter events, 80.4 us)
Async XLA Ops:
  1.9 14.6 %collective-permute-start = (bf16[128,1024]{1,0:T(8,128)(2,1)S(1)}, bf16[128,1024]{1,0:T(8,128)(2,1)S(1)}, u32[]{:S(2)}, u32[]{:S(2)}) collective-permute-start(bf16[128,1024]{1,0:T(8,128)(2,1)S(1)} %get-tuple-element.83.refs_2_), channel_id=1, source_target_pairs={{0,2},{1,3},{2,0},{3,1},{4,6},{5,7},{6,4},{7,5},{8,10},{9,11},{10,... | collective-permute-start | bytes 786440 | tf_op jit(solution)/shard_map/ppermute | solution.py:356
  5.0 14.8 %collective-permute-start.3 = (bf16[128,1024]{1,0:T(8,128)(2,1)S(1)}, bf16[128,1024]{1,0:T(8,128)(2,1)}, u32[]{:S(2)}, u32[]{:S(2)}) collective-permute-start(bf16[128,1024]{1,0:T(8,128)(2,1)S(1)} %get-tuple-element.83.refs_2_), channel_id=1, source_target_pairs={{0,1},{1,0},{2,3},{3,2},{4,5},{5,4},{6,7},{7,6},{8,9},{9,8},{10,11... | collective-permute-start | bytes 786440 | tf_op jit(solution)/shard_map/ppermute | solution.py:356
  6.5 25.6 %collective-permute-start.5 = (bf16[128,1024]{1,0:T(8,128)(2,1)S(1)}, bf16[128,1024]{1,0:T(8,128)(2,1)}, u32[]{:S(2)}, u32[]{:S(2)}) collective-permute-start(bf16[128,1024]{1,0:T(8,128)(2,1)S(1)} %get-tuple-element.83.refs_2_), channel_id=1, source_target_pairs={{0,4},{1,5},{2,6},{3,7},{4,0},{5,1},{6,2},{7,3},{8,12},{9,13},{10,... | collective-permute-start | bytes 786440 | tf_op jit(solution)/shard_map/ppermute | solution.py:356
  11.4 16.4 %all-to-all-start = ((s32[32,1,32]{2,1,0:T(1,128)}), s32[32,1,32]{2,1,0:T(1,128)S(1)}, u32[]{:S(2)}, u32[]{:S(2)}) async-start(s32[32,1,32]{2,1,0:T(1,128)} %bitcast.4), calls=%async_computation | async-start | bytes 32768 | tf_op jit(solution)/shard_map/all_to_all | solution.py:424
  14.0 13.9 %collective-permute-start.4 = (bf16[128,1024]{1,0:T(8,128)(2,1)S(1)}, bf16[128,1024]{1,0:T(8,128)(2,1)}, u32[]{:S(2)}, u32[]{:S(2)}) collective-permute-start(bf16[128,1024]{1,0:T(8,128)(2,1)S(1)} %get-tuple-element.152.refs_0_), channel_id=1, source_target_pairs={{0,1},{1,0},{2,3},{3,2},{4,5},{5,4},{6,7},{7,6},{8,9},{9,8},{10,11... | collective-permute-start | bytes 786440 | tf_op jit(solution)/shard_map/ppermute | solution.py:356
  16.6 11.3 %collective-permute-start.1 = (bf16[128,1024]{1,0:T(8,128)(2,1)S(1)}, bf16[128,1024]{1,0:T(8,128)(2,1)}, u32[]{:S(2)}, u32[]{:S(2)}) collective-permute-start(bf16[128,1024]{1,0:T(8,128)(2,1)S(1)} %collective-permute-done.refs_4_), channel_id=1, source_target_pairs={{0,16},{8,24},{16,0},{24,8},{1,17},{9,25},{17,1},{25,9},{2,18},{10... | collective-permute-start | bytes 786440 | tf_op jit(solution)/shard_map/ppermute | solution.py:356
  18.1 10.0 %collective-permute-start.2 = (bf16[128,1024]{1,0:T(8,128)(2,1)S(1)}, bf16[128,1024]{1,0:T(8,128)(2,1)S(1)}, u32[]{:S(2)}, u32[]{:S(2)}) collective-permute-start(bf16[128,1024]{1,0:T(8,128)(2,1)S(1)} %collective-permute-done.refs_4_), channel_id=1, source_target_pairs={{0,1},{1,0},{2,3},{3,2},{4,5},{5,4},{6,7},{7,6},{8,9},{9,8},{10,11... | collective-permute-start | bytes 786440 | tf_op jit(solution)/shard_map/ppermute | solution.py:356
  19.8 12.3 %collective-permute-start.6 = (bf16[128,1024]{1,0:T(8,128)(2,1)S(1)}, bf16[128,1024]{1,0:T(8,128)(2,1)}, u32[]{:S(2)}, u32[]{:S(2)}) collective-permute-start(bf16[128,1024]{1,0:T(8,128)(2,1)S(1)} %get-tuple-element.83.refs_2_), channel_id=1, source_target_pairs={{0,6},{1,7},{2,4},{3,5},{4,2},{5,3},{6,0},{7,1},{8,14},{9,15},{10,... | collective-permute-start | bytes 786440 | tf_op jit(solution)/shard_map/ppermute | solution.py:356
  32.2 71.7 %all-to-all-start.1 = ((bf16[32,32,1024]{2,1,0:T(8,128)(2,1)}), bf16[32,32,1024]{2,1,0:T(8,128)(2,1)}, u32[]{:S(2)}, u32[]{:S(2)}) async-start(bf16[32,32,1024]{2,1,0:T(8,128)(2,1)} %bitcast.21), calls=%async_computation.1 | async-start | bytes 4194304 | tf_op jit(solution)/shard_map/all_to_all | solution.py:487
  39.4 7.8 %collective-permute-start.16 = (bf16[128,1024]{1,0:T(8,128)(2,1)}, bf16[128,1024]{1,0:T(8,128)(2,1)S(1)}, u32[]{:S(2)}, u32[]{:S(2)}) collective-permute-start(bf16[128,1024]{1,0:T(8,128)(2,1)} %collective-permute-done.1.refs_4_), channel_id=1, source_target_pairs={{0,8},{8,0},{16,24},{24,16},{1,9},{9,1},{17,25},{25,17},{2,10},{10... | collective-permute-start | bytes 786440 | tf_op jit(solution)/shard_map/ppermute | solution.py:356
  42.6 27.8 %collective-permute-start.13 = (bf16[256,1024]{1,0:T(8,128)(2,1)S(1)}, bf16[256,1024]{1,0:T(8,128)(2,1)}, u32[]{:S(2)}, u32[]{:S(2)}) collective-permute-start(bf16[256,1024]{1,0:T(8,128)(2,1)S(1)} %constant_dynamic-update-slice_fusion.refs_6_), channel_id=1, source_target_pairs={{0,8},{8,0},{16,24},{24,16},{1,9},{9,1},{17,25},{25,17},{2,10},{10... | collective-permute-start | bytes 1572872 | tf_op jit(solution)/shard_map/ppermute | solution.py:356
  43.4 36.3 %collective-permute-start.7 = (bf16[256,1024]{1,0:T(8,128)(2,1)S(1)}, bf16[256,1024]{1,0:T(8,128)(2,1)S(1)}, u32[]{:S(2)}, u32[]{:S(2)}) collective-permute-start(bf16[256,1024]{1,0:T(8,128)(2,1)S(1)} %constant_dynamic-update-slice_fusion.refs_6_), channel_id=1, source_target_pairs={{0,16},{8,24},{16,0},{24,8},{1,17},{9,25},{17,1},{25,9},{2,18},{10... | collective-permute-start | bytes 1572872 | tf_op jit(solution)/shard_map/ppermute | solution.py:356
  45.7 34.0 %collective-permute-start.8 = (bf16[256,1024]{1,0:T(8,128)(2,1)S(1)}, bf16[256,1024]{1,0:T(8,128)(2,1)S(1)}, u32[]{:S(2)}, u32[]{:S(2)}) collective-permute-start(bf16[256,1024]{1,0:T(8,128)(2,1)S(1)} %constant_dynamic-update-slice_fusion.refs_6_), channel_id=1, source_target_pairs={{0,1},{1,0},{2,3},{3,2},{4,5},{5,4},{6,7},{7,6},{8,9},{9,8},{10,11... | collective-permute-start | bytes 1572872 | tf_op jit(solution)/shard_map/ppermute | solution.py:356
  47.9 22.5 %collective-permute-start.12 = (bf16[128,1024]{1,0:T(8,128)(2,1)}, bf16[128,1024]{1,0:T(8,128)(2,1)}, u32[]{:S(2)}, u32[]{:S(2)}) collective-permute-start(bf16[128,1024]{1,0:T(8,128)(2,1)} %copy-done.11), channel_id=1, source_target_pairs={{0,8},{8,0},{16,24},{24,16},{1,9},{9,1},{17,25},{25,17},{2,10},{10... | collective-permute-start | bytes 786440 | tf_op jit(solution)/shard_map/ppermute | solution.py:356
  48.6 31.1 %collective-permute-start.9 = (bf16[128,1024]{1,0:T(8,128)(2,1)}, bf16[128,1024]{1,0:T(8,128)(2,1)}, u32[]{:S(2)}, u32[]{:S(2)}) collective-permute-start(bf16[128,1024]{1,0:T(8,128)(2,1)} %copy-done.13), channel_id=1, source_target_pairs={{0,16},{8,24},{16,0},{24,8},{1,17},{9,25},{17,1},{25,9},{2,18},{10... | collective-permute-start | bytes 786440 | tf_op jit(solution)/shard_map/ppermute | solution.py:356
  80.3 9.1 %collective-permute-start.18 = (bf16[128,1024]{1,0:T(8,128)(2,1)S(1)}, bf16[128,1024]{1,0:T(8,128)(2,1)S(1)}, u32[]{:S(2)}, u32[]{:S(2)}) collective-permute-start(bf16[128,1024]{1,0:T(8,128)(2,1)S(1)} %split.6), channel_id=1, source_target_pairs={{0,16},{8,24},{16,0},{24,8},{1,17},{9,25},{17,1},{25,9},{2,18},{10... | collective-permute-start | bytes 786440 | tf_op jit(solution)/shard_map/ppermute | solution.py:356
  80.7 9.4 %collective-permute-start.19 = (bf16[128,1024]{1,0:T(8,128)(2,1)S(1)}, bf16[128,1024]{1,0:T(8,128)(2,1)S(1)}, u32[]{:S(2)}, u32[]{:S(2)}) collective-permute-start(bf16[128,1024]{1,0:T(8,128)(2,1)S(1)} %split.7), channel_id=1, source_target_pairs={{0,1},{1,0},{2,3},{3,2},{4,5},{5,4},{6,7},{7,6},{8,9},{9,8},{10,11... | collective-permute-start | bytes 786440 | tf_op jit(solution)/shard_map/ppermute | solution.py:356
  80.7 9.9 %collective-permute-start.22 = (bf16[128,1024]{1,0:T(8,128)(2,1)}, bf16[128,1024]{1,0:T(8,128)(2,1)S(1)}, u32[]{:S(2)}, u32[]{:S(2)}) collective-permute-start(bf16[128,1024]{1,0:T(8,128)(2,1)} %collective-permute-done.9.refs_0_), channel_id=1, source_target_pairs={{0,8},{8,0},{16,24},{24,16},{1,9},{9,1},{17,25},{25,17},{2,10},{10... | collective-permute-start | bytes 786440 | tf_op jit(solution)/shard_map/ppermute | solution.py:356
  102.2 17.9 %collective-permute-start.25 = (bf16[128,1024]{1,0:T(8,128)(2,1)S(1)}, bf16[128,1024]{1,0:T(8,128)(2,1)S(1)}, u32[]{:S(2)}, u32[]{:S(2)}) collective-permute-start(bf16[128,1024]{1,0:T(8,128)(2,1)S(1)} %dynamic-slice_convert_fusion.refs_0_), channel_id=1, source_target_pairs={{0,16},{8,24},{16,0},{24,8},{1,17},{9,25},{17,1},{25,9},{2,18},{10... | collective-permute-start | bytes 786440 | tf_op jit(solution)/shard_map/ppermute | solution.py:356
  126.9 11.6 %collective-permute-start.28 = (bf16[384,512]{1,0:T(8,128)(2,1)S(1)}, bf16[384,512]{1,0:T(8,128)(2,1)S(1)}, u32[]{:S(2)}, u32[]{:S(2)}) collective-permute-start(bf16[384,512]{1,0:T(8,128)(2,1)S(1)} %get-tuple-element.123), channel_id=1, source_target_pairs={{0,1},{1,0},{2,3},{3,2},{4,5},{5,4},{6,7},{7,6},{8,9},{9,8},{10,11... | collective-permute-start | bytes 1179656 | tf_op jit(solution)/shard_map/ppermute | solution.py:356
  129.1 10.9 %collective-permute-start.29 = (bf16[384,512]{1,0:T(8,128)(2,1)S(1)}, bf16[384,512]{1,0:T(8,128)(2,1)S(1)}, u32[]{:S(2)}, u32[]{:S(2)}) collective-permute-start(bf16[384,512]{1,0:T(8,128)(2,1)S(1)} %get-tuple-element.125), channel_id=1, source_target_pairs={{0,16},{8,24},{16,0},{24,8},{1,17},{9,25},{17,1},{25,9},{2,18},{10... | collective-permute-start | bytes 1179656 | tf_op jit(solution)/shard_map/ppermute | solution.py:356
  158.0 9.4 %collective-permute-start.38 = (bf16[96,512]{1,0:T(8,128)(2,1)S(1)}, bf16[96,512]{1,0:T(8,128)(2,1)S(1)}, u32[]{:S(2)}, u32[]{:S(2)}) collective-permute-start(bf16[96,512]{1,0:T(8,128)(2,1)S(1)} %add_convert_fusion.refs_0_), channel_id=1, source_target_pairs={{0,4},{1,5},{2,6},{3,7},{4,0},{5,1},{6,2},{7,3},{8,12},{9,13},{10,... | collective-permute-start | bytes 294920 | tf_op jit(solution)/shard_map/ppermute | solution.py:356
  176.0 7.8 %collective-permute-start.42 = (bf16[384,512]{1,0:T(8,128)(2,1)S(1)}, bf16[384,512]{1,0:T(8,128)(2,1)S(1)}, u32[]{:S(2)}, u32[]{:S(2)}) collective-permute-start(bf16[384,512]{1,0:T(8,128)(2,1)S(1)} %shard_map.230.refs_0_), channel_id=1, source_target_pairs={{0,1},{1,0},{2,3},{3,2},{4,5},{5,4},{6,7},{7,6},{8,9},{9,8},{10,11... | collective-permute-start | bytes 1179656 | tf_op jit(solution)/shard_map/ppermute | solution.py:356
  176.8 7.8 %collective-permute-start.43 = (bf16[384,512]{1,0:T(8,128)(2,1)S(1)}, bf16[384,512]{1,0:T(8,128)(2,1)S(1)}, u32[]{:S(2)}, u32[]{:S(2)}) collective-permute-start(bf16[384,512]{1,0:T(8,128)(2,1)S(1)} %shard_map.231.refs_0_), channel_id=1, source_target_pairs={{0,16},{8,24},{16,0},{24,8},{1,17},{9,25},{17,1},{25,9},{2,18},{10... | collective-permute-start | bytes 1179656 | tf_op jit(solution)/shard_map/ppermute | solution.py:356
  (57 other events, 269.9 us)

commit v4 on v3

--- a/solution.py
+++ b/solution.py
@@ -120,10 +120,10 @@
 
 def cached_body(code_ref, *refs, bases):
     pieces, held_ref = refs[:-1], refs[-1]
-    step = 256
+    step = 512
     groups, depth = [], step
     for i, piece in enumerate(pieces):
-        if depth + piece.shape[0] > step:
+        if depth + piece.shape[0] > 512:
             groups, depth = groups + [[]], 0
         groups[-1].append(i)
         depth += piece.shape[0]
@@ -527,7 +527,7 @@
     streamed = (
         miss_rows, w1_self, w1_nbr, back, w2_self, w2_nbr, d_emb, sel_miss, own_part, near_part
     )
-    turn = 256
+    turn = 384
     emb, *sums = pl.pallas_call(
         functools.partial(step_body, scale=grad_scale, step=turn),
         out_shape=(
@@ -551,7 +551,7 @@
     )(box.at["c"].reshape(1), *streamed, count, flags)
     sums, far_hot = lax.optimization_barrier((sums, far_hot))
 
-    p, q = ([sums[2 + i], box.swap(sums[i], "c", 1)] for i in range(2))
+    p, q = ([sums[2 + i].astype(F32), box.swap(sums[i], "c", 1)] for i in range(2))
     p, q = box.scatter((p, q), ("x", "y"))
     near_hot = [box.swap(block, "c", 1) for block in far_hot]
     p, q, near_hot = lax.optimization_barrier((p, q, near_hot))

time: 192 us -> 189 us (0.984)
  Pallas kernels: 53.4 us -> 50.9 us
  local copies, waits for them, and re-layouts: 23.6 us -> 21.4 us
    unnamed x67 -> x65, local copies, waits for them, and re-layouts: 20.3 us -> 18 us
    pallas_call x19, Pallas kernels: 34.4 us -> 32.3 us  [call(): pl.pallas_call(body, out_shape=out_shape, in_specs=specs, out_specs=jax.t...]
  transfers between devices with their start and end apart: 48 -> 48, of which waited for: 26 -> 26; matrix products, arithmetic and copies ran while one was open for 5% -> 6% of each run, Pallas kernels for 25% -> 24%
where the time goes in v4:
time: 189 us; the launch traced here: 188 us
  waiting for transfers between devices  55.2 us (29%)
  Pallas kernels  50.9 us (27%)
  starting transfers between devices  50.4 us (27%)
  local copies, waits for them, and re-layouts  21.4 us (11%)
  other arithmetic  7.95 us (4%)
  between operations  2.04 us (1%)
    ppermute x46, waiting for transfers between devices, swap(): lax.ppermute(array, name, [(i, i ^ k * stride) for i in range(count)])  55.2 us
    ppermute x46, starting transfers between devices, swap(): lax.ppermute(array, name, [(i, i ^ k * stride) for i in range(count)])  41.8 us
    pallas_call x19, Pallas kernels, call(): pl.pallas_call(body, out_shape=out_shape, in_specs=specs, out_specs=jax.t...  32.3 us
    unnamed x65, local copies, waits for them, and re-layouts  18 us
    pallas_call x1, Pallas kernels, on_device(): pl.pallas_call(functools.partial(step_body, scale=grad_scale, step=turn),...  15.7 us
    all_to_all x1, starting transfers between devices, on_device(): lax.all_to_all(served.reshape(owners, cap, wide), BOTH, split_axis=0, con...  6.1 us
  transfers between devices with their start and end apart: 48, of which 26 were waited for; matrix products, arithmetic and copies ran while one was open for 6% of the time, Pallas kernels for 24%

profile of v4, /device:TPU:0, one launch (start us, length us, event | category | flops | bytes accessed | tf_op | source)
XLA Modules:
  0.0 187.9 jit_solution(12976289667176255887)
XLA Ops:
  1.9 3.1 %collective-permute-start = (bf16[128,1024]{1,0:T(8,128)(2,1)S(1)}, bf16[128,1024]{1,0:T(8,128)(2,1)S(1)}, u32[]{:S(2)}, u32[]{:S(2)}) collective-permute-start(bf16[128,1024]{1,0:T(8,128)(2,1)S(1)} %get-tuple-element.83.refs_2_), channel_id=1, source_target_pairs={{0,2},{1,3},{2,0},{3,1},{4,6},{5,7},{6,4},{7,5},{8,10},{9,11},{10,... | collective-permute-start | bytes 786440 | tf_op jit(solution)/shard_map/ppermute | solution.py:356
  6.5 2.6 %collective-permute-start.5 = (bf16[128,1024]{1,0:T(8,128)(2,1)S(1)}, bf16[128,1024]{1,0:T(8,128)(2,1)}, u32[]{:S(2)}, u32[]{:S(2)}) collective-permute-start(bf16[128,1024]{1,0:T(8,128)(2,1)S(1)} %get-tuple-element.83.refs_2_), channel_id=1, source_target_pairs={{0,4},{1,5},{2,6},{3,7},{4,0},{5,1},{6,2},{7,3},{8,12},{9,13},{10,... | collective-permute-start | bytes 786440 | tf_op jit(solution)/shard_map/ppermute | solution.py:356
  11.4 2.5 %all-to-all-start = ((s32[32,1,32]{2,1,0:T(1,128)}), s32[32,1,32]{2,1,0:T(1,128)S(1)}, u32[]{:S(2)}, u32[]{:S(2)}) async-start(s32[32,1,32]{2,1,0:T(1,128)} %bitcast.4), calls=%async_computation | async-start | bytes 32768 | tf_op jit(solution)/shard_map/all_to_all | solution.py:424
  28.1 2.6 %shard_map.218 = bf16[1024,1024]{1,0:T(8,128)(2,1)S(1)} custom-call(s32[32,32]{1,0:T(8,128)S(1)} %bitcast.22, bf16[1024,1024]{1,0:T(8,128)(2,1)S(1)} %convert_element_type.30.store_ref), custom_call_target="tpu_custom_call" | custom-call | tf_op jit(solution)/shard_map/pallas_call | solution.py:29
  32.2 6.1 %all-to-all-start.1 = ((bf16[32,32,1024]{2,1,0:T(8,128)(2,1)}), bf16[32,32,1024]{2,1,0:T(8,128)(2,1)}, u32[]{:S(2)}, u32[]{:S(2)}) async-start(bf16[32,32,1024]{2,1,0:T(8,128)(2,1)} %bitcast.21), calls=%async_computation.1 | async-start | bytes 4194304 | tf_op jit(solution)/shard_map/all_to_all | solution.py:487
  51.5 7.4 %shard_map.219 = (bf16[2,768,1024]{2,1,0:T(8,128)(2,1)S(1)}, bf16[2,768,1024]{2,1,0:T(8,128)(2,1)S(1)}, f32[768,1]{1,0:T(8,128)S(1)}, bf16[768,512]{1,0:T(8,128)...) custom-call(s32[6,128]{1,0:T(8,128)S(1)} %pad_add_fusion.1.targets_ref, s32[11,1024]{1,0:T(8,128)S(1)} %copy-done.25, ...), custom_call_target="tpu_custom_call" | custom-call | tf_op jit(solution)/shard_map/pallas_call | solution.py:29
  66.0 3.8 %shard_map.221.refs_1_ = bf16[1024,1024]{1,0:T(8,128)(2,1)S(1)} custom-call(s32[1024,1]{1,0:T(8,128)S(1)} %get-tuple-element.94.code_ref, bf16[128,1024]{1,0:T(8,128)(2,1)} %collective-permute-done.3.refs_0_, bf16[128,1024]{1,0:T(8,128)(2,1)S(1)} %copy-done.18, bf16[128,1024]{1,0:T(8,128)(2,1)} %collective-permute-done.4.refs_2_, ...), custom_call_target="tpu_custom_call" | custom-call | tf_op jit(solution)/shard_map/pallas_call | solution.py:29
  69.9 4.2 %shard_map.220.refs_0_ = bf16[1024,1024]{1,0:T(8,128)(2,1)S(1)} custom-call(s32[1024,1]{1,0:T(8,128)S(1)} %get-tuple-element.94.code_ref, bf16[128,1024]{1,0:T(8,128)(2,1)S(1)} %get-tuple-element.152.refs_0_, bf16[128,1024]{1,0:T(8,128)(2,1)S(1)} %copy-done.14, bf16[128,1024]{1,0:T(8,128)(2,1)S(1)} %get-tuple-element.83.refs_2_, ...), custom_call_target="tpu_custom_call" | custom-call | tf_op jit(solution)/shard_map/pallas_call | solution.py:29
  74.1 5.6 %collective-permute-done.9.refs_0_ = bf16[128,1024]{1,0:T(8,128)(2,1)} collective-permute-done((bf16[128,1024]{1,0:T(8,128)(2,1)}, bf16[128,1024]{1,0:T(8,128)(2,1)}, u32[]{:S(2)}, u32[]{:S(2)}) %collective-permute-start.9) | collective-permute-done | bytes 262176 | tf_op jit(solution)/shard_map/ppermute | solution.py:356
  82.4 2.6 %shard_map.222.refs_2_ = bf16[1024,1024]{1,0:T(8,128)(2,1)S(1)} custom-call(s32[1024,1]{1,0:T(8,128)S(1)} %get-tuple-element.94.code_ref, bf16[256,1024]{1,0:T(8,128)(2,1)S(1)} %collective-permute-done.7.refs_0_, bf16[256,1024]{1,0:T(8,128)(2,1)S(1)} %collective-permute-done.20.refs_1_, bf16[256,1024]{1,0:T(8,128)(2,1)S(1)} %collective-permute-done.8.refs_2_, ...), custom_call_target="tpu_custom_call" | custom-call | tf_op jit(solution)/shard_map/pallas_call | solution.py:29
  84.9 4.4 %collective-permute-done.18.refs_2_ = bf16[128,1024]{1,0:T(8,128)(2,1)S(1)} collective-permute-done((bf16[128,1024]{1,0:T(8,128)(2,1)S(1)}, bf16[128,1024]{1,0:T(8,128)(2,1)S(1)}, u32[]{:S(2)}, u32[]{:S(2)}) %collective-permute-start.18) | collective-permute-done | bytes 262176 | tf_op jit(solution)/shard_map/ppermute | solution.py:356
  92.0 3.3 %shard_map.223.refs_3_ = bf16[1024,1024]{1,0:T(8,128)(2,1)S(1)} custom-call(s32[1024,1]{1,0:T(8,128)S(1)} %get-tuple-element.94.code_ref, bf16[128,1024]{1,0:T(8,128)(2,1)} %collective-permute-done.9.refs_0_, bf16[128,1024]{1,0:T(8,128)(2,1)S(1)} %collective-permute-done.22.refs_1_, bf16[128,1024]{1,0:T(8,128)(2,1)S(1)} %collective-permute-done.18.refs_2_, ...), custom_call_target="tpu_custom_call" | custom-call | tf_op jit(solution)/shard_map/pallas_call | solution.py:29
  95.3 3.7 %shard_map.224 = (bf16[768,1024]{1,0:T(8,128)(2,1)S(1)}, f32[768,1024]{1,0:T(8,128)S(1)}) custom-call(bf16[2,768,1024]{2,1,0:T(8,128)(2,1)S(1)} %get-tuple-element.90.sel_ref, bf16[1024,1024]{1,0:T(8,128)(2,1)S(1)} %shard_map.220.refs_0_, bf16[1024,1024]{1,0:T(8,128)(2,1)S(1)} %shard_map.221.refs_1_, bf16[1024,1024]{1,0:T(8,128)(2,1)S(1)} %shard_map.222.refs_2_, ...), custom_call_target="tpu_custom_call" | custom-call | tf_op jit(solution)/shard_map/pallas_call | solution.py:29
  103.4 15.7 %shard_map.225 = (bf16[128,512]{1,0:T(8,128)(2,1)}, bf16[768,512]{1,0:T(8,128)(2,1)}, bf16[768,512]{1,0:T(8,128)(2,1)}, bf16[768,512]{1,0:T(8,128)(2,1)}, bf16[768,512]{1,0:T(8,128)(2,1)}) custom-call(s32[1]{0:T(128)} %bitcast.core_ref.me_ref, bf16[1024,1024]{1,0:T(8,128)(2,1)} %bitcast.10.refs_0_, bf16[1024,512]{1,0:T(8,128)(2,1)} %refs_1_.1, ...), custom_call_target="tpu_custom_call" | custom-call | tf_op jit(solution)/shard_map/pallas_call | solution.py:531
  128.3 7.0 %collective-permute-done.28.refs_1_ = bf16[384,512]{1,0:T(8,128)(2,1)S(1)} collective-permute-done((bf16[384,512]{1,0:T(8,128)(2,1)S(1)}, bf16[384,512]{1,0:T(8,128)(2,1)S(1)}, u32[]{:S(2)}, u32[]{:S(2)}) %collective-permute-start.28) | collective-permute-done | bytes 393248 | tf_op jit(solution)/shard_map/ppermute | solution.py:356
  138.5 4.8 %collective-permute-done.32.refs_1_ = bf16[192,512]{1,0:T(8,128)(2,1)S(1)} collective-permute-done((bf16[192,512]{1,0:T(8,128)(2,1)S(1)}, bf16[192,512]{1,0:T(8,128)(2,1)S(1)}, u32[]{:S(2)}, u32[]{:S(2)}) %collective-permute-start.32) | collective-permute-done | bytes 196640 | tf_op jit(solution)/shard_map/ppermute | solution.py:356
  144.3 3.2 %collective-permute-start.36 = (bf16[96,512]{1,0:T(8,128)(2,1)S(1)}, bf16[96,512]{1,0:T(8,128)(2,1)S(1)}, u32[]{:S(2)}, u32[]{:S(2)}) collective-permute-start(bf16[96,512]{1,0:T(8,128)(2,1)S(1)} %get-tuple-element.139), channel_id=1, source_target_pairs={{0,6},{1,7},{2,4},{3,5},{4,2},{5,3},{6,0},{7,1},{8,14},{9,15},{10,... | collective-permute-start | bytes 294920 | tf_op jit(solution)/shard_map/ppermute | solution.py:356
  148.8 2.8 %collective-permute-done.36 = bf16[96,512]{1,0:T(8,128)(2,1)S(1)} collective-permute-done((bf16[96,512]{1,0:T(8,128)(2,1)S(1)}, bf16[96,512]{1,0:T(8,128)(2,1)S(1)}, u32[]{:S(2)}, u32[]{:S(2)}) %collective-permute-start.36) | collective-permute-done | bytes 98336 | tf_op jit(solution)/shard_map/ppermute | solution.py:356
  154.8 2.6 %collective-permute-start.38 = (bf16[96,512]{1,0:T(8,128)(2,1)S(1)}, bf16[96,512]{1,0:T(8,128)(2,1)S(1)}, u32[]{:S(2)}, u32[]{:S(2)}) collective-permute-start(bf16[96,512]{1,0:T(8,128)(2,1)S(1)} %add_convert_fusion.refs_0_), channel_id=1, source_target_pairs={{0,4},{1,5},{2,6},{3,7},{4,0},{5,1},{6,2},{7,3},{8,12},{9,13},{10,... | collective-permute-start | bytes 294920 | tf_op jit(solution)/shard_map/ppermute | solution.py:356
  159.0 5.2 %collective-permute-done.38.refs_2_ = bf16[96,512]{1,0:T(8,128)(2,1)S(1)} collective-permute-done((bf16[96,512]{1,0:T(8,128)(2,1)S(1)}, bf16[96,512]{1,0:T(8,128)(2,1)S(1)}, u32[]{:S(2)}, u32[]{:S(2)}) %collective-permute-start.38) | collective-permute-done | bytes 98336 | tf_op jit(solution)/shard_map/ppermute | solution.py:356
  167.1 2.9 %collective-permute-done.40.refs_1_ = bf16[192,512]{1,0:T(8,128)(2,1)S(1)} collective-permute-done((bf16[192,512]{1,0:T(8,128)(2,1)S(1)}, bf16[192,512]{1,0:T(8,128)(2,1)S(1)}, u32[]{:S(2)}, u32[]{:S(2)}) %collective-permute-start.40) | collective-permute-done | bytes 196640 | tf_op jit(solution)/shard_map/ppermute | solution.py:356
  170.0 2.7 %collective-permute-done.41.refs_1_ = bf16[192,512]{1,0:T(8,128)(2,1)S(1)} collective-permute-done((bf16[192,512]{1,0:T(8,128)(2,1)S(1)}, bf16[192,512]{1,0:T(8,128)(2,1)S(1)}, u32[]{:S(2)}, u32[]{:S(2)}) %collective-permute-start.41) | collective-permute-done | bytes 196640 | tf_op jit(solution)/shard_map/ppermute | solution.py:356
  174.5 6.1 %collective-permute-done.42.refs_1_ = bf16[384,512]{1,0:T(8,128)(2,1)S(1)} collective-permute-done((bf16[384,512]{1,0:T(8,128)(2,1)S(1)}, bf16[384,512]{1,0:T(8,128)(2,1)S(1)}, u32[]{:S(2)}, u32[]{:S(2)}) %collective-permute-start.42) | collective-permute-done | bytes 393248 | tf_op jit(solution)/shard_map/ppermute | solution.py:356
  184.9 2.8 %shard_map.234 = (f32[1024,512]{1,0:T(8,128)}, f32[1024,512]{1,0:T(8,128)}, f32[512,512]{1,0:T(8,128)}, f32[512,512]{1,0:T(8,128)}) custom-call(s32[1]{0:T(128)} %bitcast.core_ref.me_ref, bf16[768,512]{1,0:T(8,128)(2,1)S(1)} %shard_map.232.refs_0_, bf16[768,512]{1,0:T(8,128)(2,1)S(1)} %collective-permute-done.44.refs_1_, ...), custom_call_target="tpu_custom_call" | custom-call | tf_op jit(solution)/shard_map/pallas_call | solution.py:569
  (175 shorter events, 78.1 us)
Async XLA Ops:
  1.9 14.6 %collective-permute-start = (bf16[128,1024]{1,0:T(8,128)(2,1)S(1)}, bf16[128,1024]{1,0:T(8,128)(2,1)S(1)}, u32[]{:S(2)}, u32[]{:S(2)}) collective-permute-start(bf16[128,1024]{1,0:T(8,128)(2,1)S(1)} %get-tuple-element.83.refs_2_), channel_id=1, source_target_pairs={{0,2},{1,3},{2,0},{3,1},{4,6},{5,7},{6,4},{7,5},{8,10},{9,11},{10,... | collective-permute-start | bytes 786440 | tf_op jit(solution)/shard_map/ppermute | solution.py:356
  5.0 14.8 %collective-permute-start.3 = (bf16[128,1024]{1,0:T(8,128)(2,1)S(1)}, bf16[128,1024]{1,0:T(8,128)(2,1)}, u32[]{:S(2)}, u32[]{:S(2)}) collective-permute-start(bf16[128,1024]{1,0:T(8,128)(2,1)S(1)} %get-tuple-element.83.refs_2_), channel_id=1, source_target_pairs={{0,1},{1,0},{2,3},{3,2},{4,5},{5,4},{6,7},{7,6},{8,9},{9,8},{10,11... | collective-permute-start | bytes 786440 | tf_op jit(solution)/shard_map/ppermute | solution.py:356
  6.5 25.6 %collective-permute-start.5 = (bf16[128,1024]{1,0:T(8,128)(2,1)S(1)}, bf16[128,1024]{1,0:T(8,128)(2,1)}, u32[]{:S(2)}, u32[]{:S(2)}) collective-permute-start(bf16[128,1024]{1,0:T(8,128)(2,1)S(1)} %get-tuple-element.83.refs_2_), channel_id=1, source_target_pairs={{0,4},{1,5},{2,6},{3,7},{4,0},{5,1},{6,2},{7,3},{8,12},{9,13},{10,... | collective-permute-start | bytes 786440 | tf_op jit(solution)/shard_map/ppermute | solution.py:356
  11.4 16.4 %all-to-all-start = ((s32[32,1,32]{2,1,0:T(1,128)}), s32[32,1,32]{2,1,0:T(1,128)S(1)}, u32[]{:S(2)}, u32[]{:S(2)}) async-start(s32[32,1,32]{2,1,0:T(1,128)} %bitcast.4), calls=%async_computation | async-start | bytes 32768 | tf_op jit(solution)/shard_map/all_to_all | solution.py:424
  14.0 13.9 %collective-permute-start.4 = (bf16[128,1024]{1,0:T(8,128)(2,1)S(1)}, bf16[128,1024]{1,0:T(8,128)(2,1)}, u32[]{:S(2)}, u32[]{:S(2)}) collective-permute-start(bf16[128,1024]{1,0:T(8,128)(2,1)S(1)} %get-tuple-element.152.refs_0_), channel_id=1, source_target_pairs={{0,1},{1,0},{2,3},{3,2},{4,5},{5,4},{6,7},{7,6},{8,9},{9,8},{10,11... | collective-permute-start | bytes 786440 | tf_op jit(solution)/shard_map/ppermute | solution.py:356
  16.6 11.3 %collective-permute-start.1 = (bf16[128,1024]{1,0:T(8,128)(2,1)S(1)}, bf16[128,1024]{1,0:T(8,128)(2,1)}, u32[]{:S(2)}, u32[]{:S(2)}) collective-permute-start(bf16[128,1024]{1,0:T(8,128)(2,1)S(1)} %collective-permute-done.refs_4_), channel_id=1, source_target_pairs={{0,16},{8,24},{16,0},{24,8},{1,17},{9,25},{17,1},{25,9},{2,18},{10... | collective-permute-start | bytes 786440 | tf_op jit(solution)/shard_map/ppermute | solution.py:356
  18.1 10.0 %collective-permute-start.2 = (bf16[128,1024]{1,0:T(8,128)(2,1)S(1)}, bf16[128,1024]{1,0:T(8,128)(2,1)S(1)}, u32[]{:S(2)}, u32[]{:S(2)}) collective-permute-start(bf16[128,1024]{1,0:T(8,128)(2,1)S(1)} %collective-permute-done.refs_4_), channel_id=1, source_target_pairs={{0,1},{1,0},{2,3},{3,2},{4,5},{5,4},{6,7},{7,6},{8,9},{9,8},{10,11... | collective-permute-start | bytes 786440 | tf_op jit(solution)/shard_map/ppermute | solution.py:356
  19.8 12.3 %collective-permute-start.6 = (bf16[128,1024]{1,0:T(8,128)(2,1)S(1)}, bf16[128,1024]{1,0:T(8,128)(2,1)}, u32[]{:S(2)}, u32[]{:S(2)}) collective-permute-start(bf16[128,1024]{1,0:T(8,128)(2,1)S(1)} %get-tuple-element.83.refs_2_), channel_id=1, source_target_pairs={{0,6},{1,7},{2,4},{3,5},{4,2},{5,3},{6,0},{7,1},{8,14},{9,15},{10,... | collective-permute-start | bytes 786440 | tf_op jit(solution)/shard_map/ppermute | solution.py:356
  32.2 71.3 %all-to-all-start.1 = ((bf16[32,32,1024]{2,1,0:T(8,128)(2,1)}), bf16[32,32,1024]{2,1,0:T(8,128)(2,1)}, u32[]{:S(2)}, u32[]{:S(2)}) async-start(bf16[32,32,1024]{2,1,0:T(8,128)(2,1)} %bitcast.21), calls=%async_computation.1 | async-start | bytes 4194304 | tf_op jit(solution)/shard_map/all_to_all | solution.py:487
  39.4 7.8 %collective-permute-start.16 = (bf16[128,1024]{1,0:T(8,128)(2,1)}, bf16[128,1024]{1,0:T(8,128)(2,1)S(1)}, u32[]{:S(2)}, u32[]{:S(2)}) collective-permute-start(bf16[128,1024]{1,0:T(8,128)(2,1)} %collective-permute-done.1.refs_4_), channel_id=1, source_target_pairs={{0,8},{8,0},{16,24},{24,16},{1,9},{9,1},{17,25},{25,17},{2,10},{10... | collective-permute-start | bytes 786440 | tf_op jit(solution)/shard_map/ppermute | solution.py:356
  42.6 27.2 %collective-permute-start.13 = (bf16[256,1024]{1,0:T(8,128)(2,1)S(1)}, bf16[256,1024]{1,0:T(8,128)(2,1)}, u32[]{:S(2)}, u32[]{:S(2)}) collective-permute-start(bf16[256,1024]{1,0:T(8,128)(2,1)S(1)} %constant_dynamic-update-slice_fusion.refs_6_), channel_id=1, source_target_pairs={{0,8},{8,0},{16,24},{24,16},{1,9},{9,1},{17,25},{25,17},{2,10},{10... | collective-permute-start | bytes 1572872 | tf_op jit(solution)/shard_map/ppermute | solution.py:356
  43.4 36.3 %collective-permute-start.7 = (bf16[256,1024]{1,0:T(8,128)(2,1)S(1)}, bf16[256,1024]{1,0:T(8,128)(2,1)S(1)}, u32[]{:S(2)}, u32[]{:S(2)}) collective-permute-start(bf16[256,1024]{1,0:T(8,128)(2,1)S(1)} %constant_dynamic-update-slice_fusion.refs_6_), channel_id=1, source_target_pairs={{0,16},{8,24},{16,0},{24,8},{1,17},{9,25},{17,1},{25,9},{2,18},{10... | collective-permute-start | bytes 1572872 | tf_op jit(solution)/shard_map/ppermute | solution.py:356
  45.7 34.0 %collective-permute-start.8 = (bf16[256,1024]{1,0:T(8,128)(2,1)S(1)}, bf16[256,1024]{1,0:T(8,128)(2,1)S(1)}, u32[]{:S(2)}, u32[]{:S(2)}) collective-permute-start(bf16[256,1024]{1,0:T(8,128)(2,1)S(1)} %constant_dynamic-update-slice_fusion.refs_6_), channel_id=1, source_target_pairs={{0,1},{1,0},{2,3},{3,2},{4,5},{5,4},{6,7},{7,6},{8,9},{9,8},{10,11... | collective-permute-start | bytes 1572872 | tf_op jit(solution)/shard_map/ppermute | solution.py:356
  47.9 21.9 %collective-permute-start.12 = (bf16[128,1024]{1,0:T(8,128)(2,1)}, bf16[128,1024]{1,0:T(8,128)(2,1)}, u32[]{:S(2)}, u32[]{:S(2)}) collective-permute-start(bf16[128,1024]{1,0:T(8,128)(2,1)} %copy-done.9), channel_id=1, source_target_pairs={{0,8},{8,0},{16,24},{24,16},{1,9},{9,1},{17,25},{25,17},{2,10},{10... | collective-permute-start | bytes 786440 | tf_op jit(solution)/shard_map/ppermute | solution.py:356
  48.6 31.1 %collective-permute-start.9 = (bf16[128,1024]{1,0:T(8,128)(2,1)}, bf16[128,1024]{1,0:T(8,128)(2,1)}, u32[]{:S(2)}, u32[]{:S(2)}) collective-permute-start(bf16[128,1024]{1,0:T(8,128)(2,1)} %copy-done.11), channel_id=1, source_target_pairs={{0,16},{8,24},{16,0},{24,8},{1,17},{9,25},{17,1},{25,9},{2,18},{10... | collective-permute-start | bytes 786440 | tf_op jit(solution)/shard_map/ppermute | solution.py:356
  80.3 9.1 %collective-permute-start.18 = (bf16[128,1024]{1,0:T(8,128)(2,1)S(1)}, bf16[128,1024]{1,0:T(8,128)(2,1)S(1)}, u32[]{:S(2)}, u32[]{:S(2)}) collective-permute-start(bf16[128,1024]{1,0:T(8,128)(2,1)S(1)} %split.6), channel_id=1, source_target_pairs={{0,16},{8,24},{16,0},{24,8},{1,17},{9,25},{17,1},{25,9},{2,18},{10... | collective-permute-start | bytes 786440 | tf_op jit(solution)/shard_map/ppermute | solution.py:356
  80.7 9.4 %collective-permute-start.19 = (bf16[128,1024]{1,0:T(8,128)(2,1)S(1)}, bf16[128,1024]{1,0:T(8,128)(2,1)S(1)}, u32[]{:S(2)}, u32[]{:S(2)}) collective-permute-start(bf16[128,1024]{1,0:T(8,128)(2,1)S(1)} %split.7), channel_id=1, source_target_pairs={{0,1},{1,0},{2,3},{3,2},{4,5},{5,4},{6,7},{7,6},{8,9},{9,8},{10,11... | collective-permute-start | bytes 786440 | tf_op jit(solution)/shard_map/ppermute | solution.py:356
  80.7 9.9 %collective-permute-start.22 = (bf16[128,1024]{1,0:T(8,128)(2,1)}, bf16[128,1024]{1,0:T(8,128)(2,1)S(1)}, u32[]{:S(2)}, u32[]{:S(2)}) collective-permute-start(bf16[128,1024]{1,0:T(8,128)(2,1)} %collective-permute-done.9.refs_0_), channel_id=1, source_target_pairs={{0,8},{8,0},{16,24},{24,16},{1,9},{9,1},{17,25},{25,17},{2,10},{10... | collective-permute-start | bytes 786440 | tf_op jit(solution)/shard_map/ppermute | solution.py:356
  101.8 17.4 %collective-permute-start.25 = (bf16[128,1024]{1,0:T(8,128)(2,1)S(1)}, bf16[128,1024]{1,0:T(8,128)(2,1)S(1)}, u32[]{:S(2)}, u32[]{:S(2)}) collective-permute-start(bf16[128,1024]{1,0:T(8,128)(2,1)S(1)} %dynamic-slice_convert_fusion.refs_0_), channel_id=1, source_target_pairs={{0,16},{8,24},{16,0},{24,8},{1,17},{9,25},{17,1},{25,9},{2,18},{10... | collective-permute-start | bytes 786440 | tf_op jit(solution)/shard_map/ppermute | solution.py:356
  123.7 11.6 %collective-permute-start.28 = (bf16[384,512]{1,0:T(8,128)(2,1)S(1)}, bf16[384,512]{1,0:T(8,128)(2,1)S(1)}, u32[]{:S(2)}, u32[]{:S(2)}) collective-permute-start(bf16[384,512]{1,0:T(8,128)(2,1)S(1)} %get-tuple-element.123), channel_id=1, source_target_pairs={{0,1},{1,0},{2,3},{3,2},{4,5},{5,4},{6,7},{7,6},{8,9},{9,8},{10,11... | collective-permute-start | bytes 1179656 | tf_op jit(solution)/shard_map/ppermute | solution.py:356
  125.9 10.9 %collective-permute-start.29 = (bf16[384,512]{1,0:T(8,128)(2,1)S(1)}, bf16[384,512]{1,0:T(8,128)(2,1)S(1)}, u32[]{:S(2)}, u32[]{:S(2)}) collective-permute-start(bf16[384,512]{1,0:T(8,128)(2,1)S(1)} %get-tuple-element.125), channel_id=1, source_target_pairs={{0,16},{8,24},{16,0},{24,8},{1,17},{9,25},{17,1},{25,9},{2,18},{10... | collective-permute-start | bytes 1179656 | tf_op jit(solution)/shard_map/ppermute | solution.py:356
  154.8 9.4 %collective-permute-start.38 = (bf16[96,512]{1,0:T(8,128)(2,1)S(1)}, bf16[96,512]{1,0:T(8,128)(2,1)S(1)}, u32[]{:S(2)}, u32[]{:S(2)}) collective-permute-start(bf16[96,512]{1,0:T(8,128)(2,1)S(1)} %add_convert_fusion.refs_0_), channel_id=1, source_target_pairs={{0,4},{1,5},{2,6},{3,7},{4,0},{5,1},{6,2},{7,3},{8,12},{9,13},{10,... | collective-permute-start | bytes 294920 | tf_op jit(solution)/shard_map/ppermute | solution.py:356
  172.8 7.8 %collective-permute-start.42 = (bf16[384,512]{1,0:T(8,128)(2,1)S(1)}, bf16[384,512]{1,0:T(8,128)(2,1)S(1)}, u32[]{:S(2)}, u32[]{:S(2)}) collective-permute-start(bf16[384,512]{1,0:T(8,128)(2,1)S(1)} %shard_map.230.refs_0_), channel_id=1, source_target_pairs={{0,1},{1,0},{2,3},{3,2},{4,5},{5,4},{6,7},{7,6},{8,9},{9,8},{10,11... | collective-permute-start | bytes 1179656 | tf_op jit(solution)/shard_map/ppermute | solution.py:356
  173.6 7.8 %collective-permute-start.43 = (bf16[384,512]{1,0:T(8,128)(2,1)S(1)}, bf16[384,512]{1,0:T(8,128)(2,1)S(1)}, u32[]{:S(2)}, u32[]{:S(2)}) collective-permute-start(bf16[384,512]{1,0:T(8,128)(2,1)S(1)} %shard_map.231.refs_0_), channel_id=1, source_target_pairs={{0,16},{8,24},{16,0},{24,8},{1,17},{9,25},{17,1},{25,9},{2,18},{10... | collective-permute-start | bytes 1179656 | tf_op jit(solution)/shard_map/ppermute | solution.py:356
  (56 other events, 266.8 us)

commit v5 on v4

--- a/solution.py
+++ b/solution.py
@@ -562,7 +562,7 @@
     summed = total(summed).astype(BF16)
     p, q = box.gather(summed, "z", parts=2)
     (p,), (q,) = lax.optimization_barrier((box.gather(p, "y"), box.gather(q, "x")))
-    (p,), (q,) = lax.optimization_barrier((box.gather(p, "x"), box.gather(q, "y")))
+    (p,), (q,) = box.gather(p, "x"), box.gather(q, "y")
     p, q = (p, box.swap(p, "c", 1)), (q, box.swap(q, "c", 1))
     cuts = [(0, wide), (wide, 2 * wide), (2 * wide, 2 * wide + hid), (2 * wide + hid, total_rows)]
     shapes = [jax.ShapeDtypeStruct((last - at, hid), F32) for at, last in cuts]

time: 189 us -> 188 us (level)
  transfers between devices with their start and end apart: 48 -> 48, of which waited for: 26 -> 25; matrix products, arithmetic and copies ran while one was open for 6% -> 6% of each run, Pallas kernels for 24% -> 25%
where the time goes in v5:
time: 188 us; the launch traced here: 187 us
  waiting for transfers between devices  54.9 us (29%)
  Pallas kernels  50.9 us (27%)
  starting transfers between devices  50 us (27%)
  local copies, waits for them, and re-layouts  21.4 us (11%)
  other arithmetic  7.95 us (4%)
  between operations  2.05 us (1%)
    ppermute x46, waiting for transfers between devices, swap(): lax.ppermute(array, name, [(i, i ^ k * stride) for i in range(count)])  54.9 us
    ppermute x46, starting transfers between devices, swap(): lax.ppermute(array, name, [(i, i ^ k * stride) for i in range(count)])  41.4 us
    pallas_call x19, Pallas kernels, call(): pl.pallas_call(body, out_shape=out_shape, in_specs=specs, out_specs=jax.t...  32.3 us
    unnamed x65, local copies, waits for them, and re-layouts  18 us
    pallas_call x1, Pallas kernels, on_device(): pl.pallas_call(functools.partial(step_body, scale=grad_scale, step=turn),...  15.7 us
    all_to_all x1, starting transfers between devices, on_device(): lax.all_to_all(served.reshape(owners, cap, wide), BOTH, split_axis=0, con...  6.1 us
  transfers between devices with their start and end apart: 48, of which 25 were waited for; matrix products, arithmetic and copies ran while one was open for 6% of the time, Pallas kernels for 25%

profile of v5, /device:TPU:0, one launch (start us, length us, event | category | flops | bytes accessed | tf_op | source)
XLA Modules:
  0.0 187.2 jit_solution(14573469767666449853)
XLA Ops:
  1.9 3.1 %collective-permute-start = (bf16[128,1024]{1,0:T(8,128)(2,1)S(1)}, bf16[128,1024]{1,0:T(8,128)(2,1)S(1)}, u32[]{:S(2)}, u32[]{:S(2)}) collective-permute-start(bf16[128,1024]{1,0:T(8,128)(2,1)S(1)} %get-tuple-element.81.refs_2_), channel_id=1, source_target_pairs={{0,2},{1,3},{2,0},{3,1},{4,6},{5,7},{6,4},{7,5},{8,10},{9,11},{10,... | collective-permute-start | bytes 786440 | tf_op jit(solution)/shard_map/ppermute | solution.py:356
  6.5 2.6 %collective-permute-start.5 = (bf16[128,1024]{1,0:T(8,128)(2,1)S(1)}, bf16[128,1024]{1,0:T(8,128)(2,1)}, u32[]{:S(2)}, u32[]{:S(2)}) collective-permute-start(bf16[128,1024]{1,0:T(8,128)(2,1)S(1)} %get-tuple-element.81.refs_2_), channel_id=1, source_target_pairs={{0,4},{1,5},{2,6},{3,7},{4,0},{5,1},{6,2},{7,3},{8,12},{9,13},{10,... | collective-permute-start | bytes 786440 | tf_op jit(solution)/shard_map/ppermute | solution.py:356
  11.4 2.5 %all-to-all-start = ((s32[32,1,32]{2,1,0:T(1,128)}), s32[32,1,32]{2,1,0:T(1,128)S(1)}, u32[]{:S(2)}, u32[]{:S(2)}) async-start(s32[32,1,32]{2,1,0:T(1,128)} %bitcast.4), calls=%async_computation | async-start | bytes 32768 | tf_op jit(solution)/shard_map/all_to_all | solution.py:424
  28.1 2.6 %shard_map.218 = bf16[1024,1024]{1,0:T(8,128)(2,1)S(1)} custom-call(s32[32,32]{1,0:T(8,128)S(1)} %bitcast.22, bf16[1024,1024]{1,0:T(8,128)(2,1)S(1)} %convert_element_type.30.store_ref), custom_call_target="tpu_custom_call" | custom-call | tf_op jit(solution)/shard_map/pallas_call | solution.py:29
  32.2 6.1 %all-to-all-start.1 = ((bf16[32,32,1024]{2,1,0:T(8,128)(2,1)}), bf16[32,32,1024]{2,1,0:T(8,128)(2,1)}, u32[]{:S(2)}, u32[]{:S(2)}) async-start(bf16[32,32,1024]{2,1,0:T(8,128)(2,1)} %bitcast.21), calls=%async_computation.1 | async-start | bytes 4194304 | tf_op jit(solution)/shard_map/all_to_all | solution.py:487
  51.5 7.4 %shard_map.219 = (bf16[2,768,1024]{2,1,0:T(8,128)(2,1)S(1)}, bf16[2,768,1024]{2,1,0:T(8,128)(2,1)S(1)}, f32[768,1]{1,0:T(8,128)S(1)}, bf16[768,512]{1,0:T(8,128)...) custom-call(s32[6,128]{1,0:T(8,128)S(1)} %pad_add_fusion.1.targets_ref, s32[11,1024]{1,0:T(8,128)S(1)} %copy-done.25, ...), custom_call_target="tpu_custom_call" | custom-call | tf_op jit(solution)/shard_map/pallas_call | solution.py:29
  66.0 3.8 %shard_map.221.refs_1_ = bf16[1024,1024]{1,0:T(8,128)(2,1)S(1)} custom-call(s32[1024,1]{1,0:T(8,128)S(1)} %get-tuple-element.92.code_ref, bf16[128,1024]{1,0:T(8,128)(2,1)} %collective-permute-done.3.refs_0_, bf16[128,1024]{1,0:T(8,128)(2,1)S(1)} %copy-done.18, bf16[128,1024]{1,0:T(8,128)(2,1)} %collective-permute-done.4.refs_2_, ...), custom_call_target="tpu_custom_call" | custom-call | tf_op jit(solution)/shard_map/pallas_call | solution.py:29
  69.9 4.2 %shard_map.220.refs_0_ = bf16[1024,1024]{1,0:T(8,128)(2,1)S(1)} custom-call(s32[1024,1]{1,0:T(8,128)S(1)} %get-tuple-element.92.code_ref, bf16[128,1024]{1,0:T(8,128)(2,1)S(1)} %get-tuple-element.148.refs_0_, bf16[128,1024]{1,0:T(8,128)(2,1)S(1)} %copy-done.14, bf16[128,1024]{1,0:T(8,128)(2,1)S(1)} %get-tuple-element.81.refs_2_, ...), custom_call_target="tpu_custom_call" | custom-call | tf_op jit(solution)/shard_map/pallas_call | solution.py:29
  74.1 5.6 %collective-permute-done.9.refs_0_ = bf16[128,1024]{1,0:T(8,128)(2,1)} collective-permute-done((bf16[128,1024]{1,0:T(8,128)(2,1)}, bf16[128,1024]{1,0:T(8,128)(2,1)}, u32[]{:S(2)}, u32[]{:S(2)}) %collective-permute-start.9) | collective-permute-done | bytes 262176 | tf_op jit(solution)/shard_map/ppermute | solution.py:356
  82.4 2.6 %shard_map.222.refs_2_ = bf16[1024,1024]{1,0:T(8,128)(2,1)S(1)} custom-call(s32[1024,1]{1,0:T(8,128)S(1)} %get-tuple-element.92.code_ref, bf16[256,1024]{1,0:T(8,128)(2,1)S(1)} %collective-permute-done.7.refs_0_, bf16[256,1024]{1,0:T(8,128)(2,1)S(1)} %collective-permute-done.20.refs_1_, bf16[256,1024]{1,0:T(8,128)(2,1)S(1)} %collective-permute-done.8.refs_2_, ...), custom_call_target="tpu_custom_call" | custom-call | tf_op jit(solution)/shard_map/pallas_call | solution.py:29
  84.9 4.4 %collective-permute-done.18.refs_2_ = bf16[128,1024]{1,0:T(8,128)(2,1)S(1)} collective-permute-done((bf16[128,1024]{1,0:T(8,128)(2,1)S(1)}, bf16[128,1024]{1,0:T(8,128)(2,1)S(1)}, u32[]{:S(2)}, u32[]{:S(2)}) %collective-permute-start.18) | collective-permute-done | bytes 262176 | tf_op jit(solution)/shard_map/ppermute | solution.py:356
  92.0 3.3 %shard_map.223.refs_3_ = bf16[1024,1024]{1,0:T(8,128)(2,1)S(1)} custom-call(s32[1024,1]{1,0:T(8,128)S(1)} %get-tuple-element.92.code_ref, bf16[128,1024]{1,0:T(8,128)(2,1)} %collective-permute-done.9.refs_0_, bf16[128,1024]{1,0:T(8,128)(2,1)S(1)} %collective-permute-done.22.refs_1_, bf16[128,1024]{1,0:T(8,128)(2,1)S(1)} %collective-permute-done.18.refs_2_, ...), custom_call_target="tpu_custom_call" | custom-call | tf_op jit(solution)/shard_map/pallas_call | solution.py:29
  95.3 3.7 %shard_map.224 = (bf16[768,1024]{1,0:T(8,128)(2,1)S(1)}, f32[768,1024]{1,0:T(8,128)S(1)}) custom-call(bf16[2,768,1024]{2,1,0:T(8,128)(2,1)S(1)} %get-tuple-element.88.sel_ref, bf16[1024,1024]{1,0:T(8,128)(2,1)S(1)} %shard_map.220.refs_0_, bf16[1024,1024]{1,0:T(8,128)(2,1)S(1)} %shard_map.221.refs_1_, bf16[1024,1024]{1,0:T(8,128)(2,1)S(1)} %shard_map.222.refs_2_, ...), custom_call_target="tpu_custom_call" | custom-call | tf_op jit(solution)/shard_map/pallas_call | solution.py:29
  103.4 15.7 %shard_map.225 = (bf16[128,512]{1,0:T(8,128)(2,1)}, bf16[768,512]{1,0:T(8,128)(2,1)}, bf16[768,512]{1,0:T(8,128)(2,1)}, bf16[768,512]{1,0:T(8,128)(2,1)}, bf16[768,512]{1,0:T(8,128)(2,1)}) custom-call(s32[1]{0:T(128)} %bitcast.core_ref.me_ref, bf16[1024,1024]{1,0:T(8,128)(2,1)} %bitcast.10.refs_0_, bf16[1024,512]{1,0:T(8,128)(2,1)} %refs_1_.1, ...), custom_call_target="tpu_custom_call" | custom-call | tf_op jit(solution)/shard_map/pallas_call | solution.py:531
  128.3 7.0 %collective-permute-done.28.refs_1_ = bf16[384,512]{1,0:T(8,128)(2,1)S(1)} collective-permute-done((bf16[384,512]{1,0:T(8,128)(2,1)S(1)}, bf16[384,512]{1,0:T(8,128)(2,1)S(1)}, u32[]{:S(2)}, u32[]{:S(2)}) %collective-permute-start.28) | collective-permute-done | bytes 393248 | tf_op jit(solution)/shard_map/ppermute | solution.py:356
  138.5 4.8 %collective-permute-done.32.refs_1_ = bf16[192,512]{1,0:T(8,128)(2,1)S(1)} collective-permute-done((bf16[192,512]{1,0:T(8,128)(2,1)S(1)}, bf16[192,512]{1,0:T(8,128)(2,1)S(1)}, u32[]{:S(2)}, u32[]{:S(2)}) %collective-permute-start.32) | collective-permute-done | bytes 196640 | tf_op jit(solution)/shard_map/ppermute | solution.py:356
  144.3 3.2 %collective-permute-start.36 = (bf16[96,512]{1,0:T(8,128)(2,1)S(1)}, bf16[96,512]{1,0:T(8,128)(2,1)S(1)}, u32[]{:S(2)}, u32[]{:S(2)}) collective-permute-start(bf16[96,512]{1,0:T(8,128)(2,1)S(1)} %get-tuple-element.137), channel_id=1, source_target_pairs={{0,6},{1,7},{2,4},{3,5},{4,2},{5,3},{6,0},{7,1},{8,14},{9,15},{10,... | collective-permute-start | bytes 294920 | tf_op jit(solution)/shard_map/ppermute | solution.py:356
  148.8 2.8 %collective-permute-done.36 = bf16[96,512]{1,0:T(8,128)(2,1)S(1)} collective-permute-done((bf16[96,512]{1,0:T(8,128)(2,1)S(1)}, bf16[96,512]{1,0:T(8,128)(2,1)S(1)}, u32[]{:S(2)}, u32[]{:S(2)}) %collective-permute-start.36) | collective-permute-done | bytes 98336 | tf_op jit(solution)/shard_map/ppermute | solution.py:356
  154.8 2.6 %collective-permute-start.38 = (bf16[96,512]{1,0:T(8,128)(2,1)S(1)}, bf16[96,512]{1,0:T(8,128)(2,1)S(1)}, u32[]{:S(2)}, u32[]{:S(2)}) collective-permute-start(bf16[96,512]{1,0:T(8,128)(2,1)S(1)} %add_convert_fusion.refs_0_), channel_id=1, source_target_pairs={{0,4},{1,5},{2,6},{3,7},{4,0},{5,1},{6,2},{7,3},{8,12},{9,13},{10,... | collective-permute-start | bytes 294920 | tf_op jit(solution)/shard_map/ppermute | solution.py:356
  159.0 5.2 %collective-permute-done.38.refs_2_ = bf16[96,512]{1,0:T(8,128)(2,1)S(1)} collective-permute-done((bf16[96,512]{1,0:T(8,128)(2,1)S(1)}, bf16[96,512]{1,0:T(8,128)(2,1)S(1)}, u32[]{:S(2)}, u32[]{:S(2)}) %collective-permute-start.38) | collective-permute-done | bytes 98336 | tf_op jit(solution)/shard_map/ppermute | solution.py:356
  167.1 2.9 %collective-permute-done.40.refs_1_ = bf16[192,512]{1,0:T(8,128)(2,1)S(1)} collective-permute-done((bf16[192,512]{1,0:T(8,128)(2,1)S(1)}, bf16[192,512]{1,0:T(8,128)(2,1)S(1)}, u32[]{:S(2)}, u32[]{:S(2)}) %collective-permute-start.40) | collective-permute-done | bytes 196640 | tf_op jit(solution)/shard_map/ppermute | solution.py:356
  170.0 2.7 %collective-permute-done.41.refs_1_ = bf16[192,512]{1,0:T(8,128)(2,1)S(1)} collective-permute-done((bf16[192,512]{1,0:T(8,128)(2,1)S(1)}, bf16[192,512]{1,0:T(8,128)(2,1)S(1)}, u32[]{:S(2)}, u32[]{:S(2)}) %collective-permute-start.41) | collective-permute-done | bytes 196640 | tf_op jit(solution)/shard_map/ppermute | solution.py:356
  174.5 6.1 %collective-permute-done.42.refs_1_ = bf16[384,512]{1,0:T(8,128)(2,1)S(1)} collective-permute-done((bf16[384,512]{1,0:T(8,128)(2,1)S(1)}, bf16[384,512]{1,0:T(8,128)(2,1)S(1)}, u32[]{:S(2)}, u32[]{:S(2)}) %collective-permute-start.42) | collective-permute-done | bytes 393248 | tf_op jit(solution)/shard_map/ppermute | solution.py:356
  184.1 2.8 %shard_map.234 = (f32[1024,512]{1,0:T(8,128)}, f32[1024,512]{1,0:T(8,128)}, f32[512,512]{1,0:T(8,128)}, f32[512,512]{1,0:T(8,128)}) custom-call(s32[1]{0:T(128)} %bitcast.core_ref.me_ref, bf16[768,512]{1,0:T(8,128)(2,1)S(1)} %shard_map.232.refs_0_, bf16[768,512]{1,0:T(8,128)(2,1)S(1)} %collective-permute-done.43.refs_1_, ...), custom_call_target="tpu_custom_call" | custom-call | tf_op jit(solution)/shard_map/pallas_call | solution.py:569
  (175 shorter events, 77.3 us)
Async XLA Ops:
  1.9 14.6 %collective-permute-start = (bf16[128,1024]{1,0:T(8,128)(2,1)S(1)}, bf16[128,1024]{1,0:T(8,128)(2,1)S(1)}, u32[]{:S(2)}, u32[]{:S(2)}) collective-permute-start(bf16[128,1024]{1,0:T(8,128)(2,1)S(1)} %get-tuple-element.81.refs_2_), channel_id=1, source_target_pairs={{0,2},{1,3},{2,0},{3,1},{4,6},{5,7},{6,4},{7,5},{8,10},{9,11},{10,... | collective-permute-start | bytes 786440 | tf_op jit(solution)/shard_map/ppermute | solution.py:356
  5.0 14.8 %collective-permute-start.3 = (bf16[128,1024]{1,0:T(8,128)(2,1)S(1)}, bf16[128,1024]{1,0:T(8,128)(2,1)}, u32[]{:S(2)}, u32[]{:S(2)}) collective-permute-start(bf16[128,1024]{1,0:T(8,128)(2,1)S(1)} %get-tuple-element.81.refs_2_), channel_id=1, source_target_pairs={{0,1},{1,0},{2,3},{3,2},{4,5},{5,4},{6,7},{7,6},{8,9},{9,8},{10,11... | collective-permute-start | bytes 786440 | tf_op jit(solution)/shard_map/ppermute | solution.py:356
  6.5 25.6 %collective-permute-start.5 = (bf16[128,1024]{1,0:T(8,128)(2,1)S(1)}, bf16[128,1024]{1,0:T(8,128)(2,1)}, u32[]{:S(2)}, u32[]{:S(2)}) collective-permute-start(bf16[128,1024]{1,0:T(8,128)(2,1)S(1)} %get-tuple-element.81.refs_2_), channel_id=1, source_target_pairs={{0,4},{1,5},{2,6},{3,7},{4,0},{5,1},{6,2},{7,3},{8,12},{9,13},{10,... | collective-permute-start | bytes 786440 | tf_op jit(solution)/shard_map/ppermute | solution.py:356
  11.4 16.4 %all-to-all-start = ((s32[32,1,32]{2,1,0:T(1,128)}), s32[32,1,32]{2,1,0:T(1,128)S(1)}, u32[]{:S(2)}, u32[]{:S(2)}) async-start(s32[32,1,32]{2,1,0:T(1,128)} %bitcast.4), calls=%async_computation | async-start | bytes 32768 | tf_op jit(solution)/shard_map/all_to_all | solution.py:424
  14.0 13.9 %collective-permute-start.4 = (bf16[128,1024]{1,0:T(8,128)(2,1)S(1)}, bf16[128,1024]{1,0:T(8,128)(2,1)}, u32[]{:S(2)}, u32[]{:S(2)}) collective-permute-start(bf16[128,1024]{1,0:T(8,128)(2,1)S(1)} %get-tuple-element.148.refs_0_), channel_id=1, source_target_pairs={{0,1},{1,0},{2,3},{3,2},{4,5},{5,4},{6,7},{7,6},{8,9},{9,8},{10,11... | collective-permute-start | bytes 786440 | tf_op jit(solution)/shard_map/ppermute | solution.py:356
  16.6 11.3 %collective-permute-start.1 = (bf16[128,1024]{1,0:T(8,128)(2,1)S(1)}, bf16[128,1024]{1,0:T(8,128)(2,1)}, u32[]{:S(2)}, u32[]{:S(2)}) collective-permute-start(bf16[128,1024]{1,0:T(8,128)(2,1)S(1)} %collective-permute-done.refs_4_), channel_id=1, source_target_pairs={{0,16},{8,24},{16,0},{24,8},{1,17},{9,25},{17,1},{25,9},{2,18},{10... | collective-permute-start | bytes 786440 | tf_op jit(solution)/shard_map/ppermute | solution.py:356
  18.1 10.0 %collective-permute-start.2 = (bf16[128,1024]{1,0:T(8,128)(2,1)S(1)}, bf16[128,1024]{1,0:T(8,128)(2,1)S(1)}, u32[]{:S(2)}, u32[]{:S(2)}) collective-permute-start(bf16[128,1024]{1,0:T(8,128)(2,1)S(1)} %collective-permute-done.refs_4_), channel_id=1, source_target_pairs={{0,1},{1,0},{2,3},{3,2},{4,5},{5,4},{6,7},{7,6},{8,9},{9,8},{10,11... | collective-permute-start | bytes 786440 | tf_op jit(solution)/shard_map/ppermute | solution.py:356
  19.8 12.3 %collective-permute-start.6 = (bf16[128,1024]{1,0:T(8,128)(2,1)S(1)}, bf16[128,1024]{1,0:T(8,128)(2,1)}, u32[]{:S(2)}, u32[]{:S(2)}) collective-permute-start(bf16[128,1024]{1,0:T(8,128)(2,1)S(1)} %get-tuple-element.81.refs_2_), channel_id=1, source_target_pairs={{0,6},{1,7},{2,4},{3,5},{4,2},{5,3},{6,0},{7,1},{8,14},{9,15},{10,... | collective-permute-start | bytes 786440 | tf_op jit(solution)/shard_map/ppermute | solution.py:356
  32.2 71.3 %all-to-all-start.1 = ((bf16[32,32,1024]{2,1,0:T(8,128)(2,1)}), bf16[32,32,1024]{2,1,0:T(8,128)(2,1)}, u32[]{:S(2)}, u32[]{:S(2)}) async-start(bf16[32,32,1024]{2,1,0:T(8,128)(2,1)} %bitcast.21), calls=%async_computation.1 | async-start | bytes 4194304 | tf_op jit(solution)/shard_map/all_to_all | solution.py:487
  39.4 7.8 %collective-permute-start.16 = (bf16[128,1024]{1,0:T(8,128)(2,1)}, bf16[128,1024]{1,0:T(8,128)(2,1)S(1)}, u32[]{:S(2)}, u32[]{:S(2)}) collective-permute-start(bf16[128,1024]{1,0:T(8,128)(2,1)} %collective-permute-done.1.refs_4_), channel_id=1, source_target_pairs={{0,8},{8,0},{16,24},{24,16},{1,9},{9,1},{17,25},{25,17},{2,10},{10... | collective-permute-start | bytes 786440 | tf_op jit(solution)/shard_map/ppermute | solution.py:356
  42.6 27.2 %collective-permute-start.13 = (bf16[256,1024]{1,0:T(8,128)(2,1)S(1)}, bf16[256,1024]{1,0:T(8,128)(2,1)}, u32[]{:S(2)}, u32[]{:S(2)}) collective-permute-start(bf16[256,1024]{1,0:T(8,128)(2,1)S(1)} %constant_dynamic-update-slice_fusion.refs_6_), channel_id=1, source_target_pairs={{0,8},{8,0},{16,24},{24,16},{1,9},{9,1},{17,25},{25,17},{2,10},{10... | collective-permute-start | bytes 1572872 | tf_op jit(solution)/shard_map/ppermute | solution.py:356
  43.4 36.3 %collective-permute-start.7 = (bf16[256,1024]{1,0:T(8,128)(2,1)S(1)}, bf16[256,1024]{1,0:T(8,128)(2,1)S(1)}, u32[]{:S(2)}, u32[]{:S(2)}) collective-permute-start(bf16[256,1024]{1,0:T(8,128)(2,1)S(1)} %constant_dynamic-update-slice_fusion.refs_6_), channel_id=1, source_target_pairs={{0,16},{8,24},{16,0},{24,8},{1,17},{9,25},{17,1},{25,9},{2,18},{10... | collective-permute-start | bytes 1572872 | tf_op jit(solution)/shard_map/ppermute | solution.py:356
  45.7 34.0 %collective-permute-start.8 = (bf16[256,1024]{1,0:T(8,128)(2,1)S(1)}, bf16[256,1024]{1,0:T(8,128)(2,1)S(1)}, u32[]{:S(2)}, u32[]{:S(2)}) collective-permute-start(bf16[256,1024]{1,0:T(8,128)(2,1)S(1)} %constant_dynamic-update-slice_fusion.refs_6_), channel_id=1, source_target_pairs={{0,1},{1,0},{2,3},{3,2},{4,5},{5,4},{6,7},{7,6},{8,9},{9,8},{10,11... | collective-permute-start | bytes 1572872 | tf_op jit(solution)/shard_map/ppermute | solution.py:356
  47.9 21.9 %collective-permute-start.12 = (bf16[128,1024]{1,0:T(8,128)(2,1)}, bf16[128,1024]{1,0:T(8,128)(2,1)}, u32[]{:S(2)}, u32[]{:S(2)}) collective-permute-start(bf16[128,1024]{1,0:T(8,128)(2,1)} %copy-done.9), channel_id=1, source_target_pairs={{0,8},{8,0},{16,24},{24,16},{1,9},{9,1},{17,25},{25,17},{2,10},{10... | collective-permute-start | bytes 786440 | tf_op jit(solution)/shard_map/ppermute | solution.py:356
  48.6 31.1 %collective-permute-start.9 = (bf16[128,1024]{1,0:T(8,128)(2,1)}, bf16[128,1024]{1,0:T(8,128)(2,1)}, u32[]{:S(2)}, u32[]{:S(2)}) collective-permute-start(bf16[128,1024]{1,0:T(8,128)(2,1)} %copy-done.11), channel_id=1, source_target_pairs={{0,16},{8,24},{16,0},{24,8},{1,17},{9,25},{17,1},{25,9},{2,18},{10... | collective-permute-start | bytes 786440 | tf_op jit(solution)/shard_map/ppermute | solution.py:356
  80.3 9.1 %collective-permute-start.18 = (bf16[128,1024]{1,0:T(8,128)(2,1)S(1)}, bf16[128,1024]{1,0:T(8,128)(2,1)S(1)}, u32[]{:S(2)}, u32[]{:S(2)}) collective-permute-start(bf16[128,1024]{1,0:T(8,128)(2,1)S(1)} %split.6), channel_id=1, source_target_pairs={{0,16},{8,24},{16,0},{24,8},{1,17},{9,25},{17,1},{25,9},{2,18},{10... | collective-permute-start | bytes 786440 | tf_op jit(solution)/shard_map/ppermute | solution.py:356
  80.7 9.4 %collective-permute-start.19 = (bf16[128,1024]{1,0:T(8,128)(2,1)S(1)}, bf16[128,1024]{1,0:T(8,128)(2,1)S(1)}, u32[]{:S(2)}, u32[]{:S(2)}) collective-permute-start(bf16[128,1024]{1,0:T(8,128)(2,1)S(1)} %split.7), channel_id=1, source_target_pairs={{0,1},{1,0},{2,3},{3,2},{4,5},{5,4},{6,7},{7,6},{8,9},{9,8},{10,11... | collective-permute-start | bytes 786440 | tf_op jit(solution)/shard_map/ppermute | solution.py:356
  80.7 9.9 %collective-permute-start.22 = (bf16[128,1024]{1,0:T(8,128)(2,1)}, bf16[128,1024]{1,0:T(8,128)(2,1)S(1)}, u32[]{:S(2)}, u32[]{:S(2)}) collective-permute-start(bf16[128,1024]{1,0:T(8,128)(2,1)} %collective-permute-done.9.refs_0_), channel_id=1, source_target_pairs={{0,8},{8,0},{16,24},{24,16},{1,9},{9,1},{17,25},{25,17},{2,10},{10... | collective-permute-start | bytes 786440 | tf_op jit(solution)/shard_map/ppermute | solution.py:356
  101.8 17.4 %collective-permute-start.25 = (bf16[128,1024]{1,0:T(8,128)(2,1)S(1)}, bf16[128,1024]{1,0:T(8,128)(2,1)S(1)}, u32[]{:S(2)}, u32[]{:S(2)}) collective-permute-start(bf16[128,1024]{1,0:T(8,128)(2,1)S(1)} %dynamic-slice_convert_fusion.refs_0_), channel_id=1, source_target_pairs={{0,16},{8,24},{16,0},{24,8},{1,17},{9,25},{17,1},{25,9},{2,18},{10... | collective-permute-start | bytes 786440 | tf_op jit(solution)/shard_map/ppermute | solution.py:356
  123.7 11.6 %collective-permute-start.28 = (bf16[384,512]{1,0:T(8,128)(2,1)S(1)}, bf16[384,512]{1,0:T(8,128)(2,1)S(1)}, u32[]{:S(2)}, u32[]{:S(2)}) collective-permute-start(bf16[384,512]{1,0:T(8,128)(2,1)S(1)} %get-tuple-element.121), channel_id=1, source_target_pairs={{0,1},{1,0},{2,3},{3,2},{4,5},{5,4},{6,7},{7,6},{8,9},{9,8},{10,11... | collective-permute-start | bytes 1179656 | tf_op jit(solution)/shard_map/ppermute | solution.py:356
  125.9 10.9 %collective-permute-start.29 = (bf16[384,512]{1,0:T(8,128)(2,1)S(1)}, bf16[384,512]{1,0:T(8,128)(2,1)S(1)}, u32[]{:S(2)}, u32[]{:S(2)}) collective-permute-start(bf16[384,512]{1,0:T(8,128)(2,1)S(1)} %get-tuple-element.123), channel_id=1, source_target_pairs={{0,16},{8,24},{16,0},{24,8},{1,17},{9,25},{17,1},{25,9},{2,18},{10... | collective-permute-start | bytes 1179656 | tf_op jit(solution)/shard_map/ppermute | solution.py:356
  154.8 9.4 %collective-permute-start.38 = (bf16[96,512]{1,0:T(8,128)(2,1)S(1)}, bf16[96,512]{1,0:T(8,128)(2,1)S(1)}, u32[]{:S(2)}, u32[]{:S(2)}) collective-permute-start(bf16[96,512]{1,0:T(8,128)(2,1)S(1)} %add_convert_fusion.refs_0_), channel_id=1, source_target_pairs={{0,4},{1,5},{2,6},{3,7},{4,0},{5,1},{6,2},{7,3},{8,12},{9,13},{10,... | collective-permute-start | bytes 294920 | tf_op jit(solution)/shard_map/ppermute | solution.py:356
  172.8 7.8 %collective-permute-start.42 = (bf16[384,512]{1,0:T(8,128)(2,1)S(1)}, bf16[384,512]{1,0:T(8,128)(2,1)S(1)}, u32[]{:S(2)}, u32[]{:S(2)}) collective-permute-start(bf16[384,512]{1,0:T(8,128)(2,1)S(1)} %shard_map.230.refs_0_), channel_id=1, source_target_pairs={{0,1},{1,0},{2,3},{3,2},{4,5},{5,4},{6,7},{7,6},{8,9},{9,8},{10,11... | collective-permute-start | bytes 1179656 | tf_op jit(solution)/shard_map/ppermute | solution.py:356
  173.6 7.8 %collective-permute-start.44 = (bf16[384,512]{1,0:T(8,128)(2,1)S(1)}, bf16[384,512]{1,0:T(8,128)(2,1)S(1)}, u32[]{:S(2)}, u32[]{:S(2)}) collective-permute-start(bf16[384,512]{1,0:T(8,128)(2,1)S(1)} %shard_map.231.refs_0_), channel_id=1, source_target_pairs={{0,16},{8,24},{16,0},{24,8},{1,17},{9,25},{17,1},{25,9},{2,18},{10... | collective-permute-start | bytes 1179656 | tf_op jit(solution)/shard_map/ppermute | solution.py:356
  (56 other events, 266.2 us)
